TPU v7x, 32 devices: a whole 2x2x4 slice. The times are simulated.
32 devices in a mesh: dp: 8 (over z, core), tensor: 4 (over y, x).
Axes of the slice: x: 2, y: 2, z: 4, core: 2. Of those that a mesh axis runs over, the one named last changes fastest.
Arguments:
- hidden_in: bfloat16 [8192, 2048], P(('dp', 'tensor')), may hold values from -6 to 6
- grad_out: bfloat16 [8192, 2048], P(('dp', 'tensor')), may hold values from -6 to 6
- mix_gain: float32 [2048], replicated, may hold values from 0.5 to 1.5
- w_query: float32 [2048, 2048], P('dp', 'tensor'), may hold values from -0.125 to 0.125
- w_key: float32 [2048, 2048], P('dp', 'tensor'), may hold values from -0.125 to 0.125
- w_value: float32 [2048, 4096], P('dp', 'tensor'), may hold values from -0.125 to 0.125
- conv_query: float32 [4, 2048], P(None, ('tensor', 'dp')), may hold values from -0.5 to 0.5
- conv_key: float32 [4, 2048], P(None, ('tensor', 'dp')), may hold values from -0.5 to 0.5
- conv_value: float32 [4, 4096], P(None, ('tensor', 'dp')), may hold values from -0.5 to 0.5
- w_decay: float32 [2048, 16], P('dp', 'tensor'), may hold values from -0.125 to 0.125
- w_beta: float32 [2048, 16], P('dp', 'tensor'), may hold values from -0.125 to 0.125
- log_rate: float32 [16], replicated
- decay_bias: float32 [16], replicated, may hold values from -1.5 to 0.5
- w_outgate: float32 [2048, 4096], P('dp', 'tensor'), may hold values from -0.125 to 0.125
- head_gain: float32 [256], replicated, may hold values from 0.5 to 1.5
- w_output: float32 [4096, 2048], P('tensor', 'dp'), may hold values from -0.125 to 0.125
- ffn_gain: float32 [2048], replicated, may hold values from 0.5 to 1.5
- w_gate: float32 [2048, 5632], P('dp', 'tensor'), may hold values from -0.125 to 0.125
- w_up: float32 [2048, 5632], P('dp', 'tensor'), may hold values from -0.125 to 0.125
- w_down: float32 [5632, 2048], P('tensor', 'dp'), may hold values from -0.109375 to 0.109375
Outputs:
- hidden_out: bfloat16 [8192, 2048], P(('dp', 'tensor'))
- grad_in: bfloat16 [8192, 2048], P(('dp', 'tensor'))
- grad_mix_gain: float32 [2048], replicated
- grad_w_query: float32 [2048, 2048], P('dp', 'tensor')
- grad_w_key: float32 [2048, 2048], P('dp', 'tensor')
- grad_w_value: float32 [2048, 4096], P('dp', 'tensor')
- grad_conv_query: float32 [4, 2048], P(None, ('tensor', 'dp'))
- grad_conv_key: float32 [4, 2048], P(None, ('tensor', 'dp'))
- grad_conv_value: float32 [4, 4096], P(None, ('tensor', 'dp'))
- grad_w_decay: float32 [2048, 16], P('dp', 'tensor')
- grad_w_beta: float32 [2048, 16], P('dp', 'tensor')
- grad_log_rate: float32 [16], replicated
- grad_decay_bias: float32 [16], replicated
- grad_w_outgate: float32 [2048, 4096], P('dp', 'tensor')
- grad_head_gain: float32 [256], replicated
- grad_w_output: float32 [4096, 2048], P('tensor', 'dp')
- grad_ffn_gain: float32 [2048], replicated
- grad_w_gate: float32 [2048, 5632], P('dp', 'tensor')
- grad_w_up: float32 [2048, 5632], P('dp', 'tensor')
- grad_w_down: float32 [5632, 2048], P('tensor', 'dp')
All inputs are finite; a program needn't handle non-finite values.
Results may differ from a plain program's by a relative error of at most 0.02.
Values may be sent and summed in bfloat16 or wider, within the bound.
No kernel may reach another device: no remote copies, remote signals or barrier semaphores. Data moves between devices by JAX's collectives and lax.ppermute only.
A program may use at most 320 MiB of HBM per device.

v0:
```python
import jax
import jax.numpy as jnp
from jax import lax
from jax.sharding import PartitionSpec as P

GROUP = 64


highest_precision = lax.Precision.HIGHEST


def rms_norm(values, gain_vec):
    return values * lax.rsqrt(jnp.mean(values * values, -1, keepdims=True) + 1e-05) * gain_vec


def unit_norm(values):
    return values * lax.rsqrt(jnp.sum(values * values, -1, keepdims=True) + 1e-06)


def swiglu(gate_pre, up_pre):
    return jax.nn.silu(gate_pre) * up_pre


def conv_silu(projected, kernel):
    tap_count = kernel.shape[0]
    row_count = projected.shape[0]
    padded = jnp.pad(projected, ((tap_count - 1, 0), (0, 0)))
    running = padded[0:row_count] * kernel[0]
    for offset in range(1, tap_count):
        running = running + padded[offset : offset + row_count] * kernel[offset]
    return jax.nn.silu(running)


def unit_lower_inverse(lower_part, tri_size):
    negated = -lower_part
    inverse = jnp.eye(tri_size, dtype=jnp.float32) + negated
    power = negated
    reach = 2
    while reach < tri_size:
        power = jnp.einsum("hab,hbc->hac", power, power, precision=highest_precision)
        inverse = inverse + jnp.einsum("hab,hbc->hac", inverse, power, precision=highest_precision)
        reach = reach * 2
    return inverse


def group_step(carried_state, block_in):
    query_rows, key_matrix_rows, value_rows, log_gates, write_rate = block_in
    tri_size = query_rows.shape[1]
    cumulative_decay_sum = jnp.cumsum(log_gates, axis=-1)
    differ = cumulative_decay_sum[:, :, None] - cumulative_decay_sum[:, None, :]
    positions = jnp.arange(tri_size)
    inclusive = positions[:, None] >= positions[None, :]
    strictly = positions[:, None] > positions[None, :]
    relative = jnp.where(inclusive, jnp.exp(jnp.minimum(differ, 0.0)), 0.0)
    key_key = jnp.einsum(
        "hck,hdk->hcd", key_matrix_rows, key_matrix_rows, precision=highest_precision
    )
    lower_part = jnp.where(strictly, write_rate[:, :, None] * relative * key_key, 0.0)
    start_decay = jnp.exp(cumulative_decay_sum)
    state_contribution = jnp.einsum(
        "zrg,zgl->zrl", key_matrix_rows, carried_state, precision=highest_precision
    )
    right_side = write_rate[..., None] * (value_rows - start_decay[..., None] * state_contribution)
    inverse = unit_lower_inverse(lower_part, tri_size)
    delta_updates = jnp.einsum("hab,hbv->hav", inverse, right_side, precision=highest_precision)
    query_key = jnp.einsum("hck,hdk->hcd", query_rows, key_matrix_rows, precision=highest_precision)
    state_readout = jnp.einsum(
        "zrg,zgl->zrl", query_rows, carried_state, precision=highest_precision
    )
    outputs = start_decay[..., None] * state_readout + jnp.einsum(
        "hcd,hdv->hcv", relative * query_key, delta_updates, precision=highest_precision
    )
    decay_to_final = jnp.exp(cumulative_decay_sum[:, -1:] - cumulative_decay_sum)
    following_state = jnp.exp(cumulative_decay_sum[:, -1])[
        :, None, None
    ] * carried_state + jnp.einsum(
        "pgs,pgd->psd",
        key_matrix_rows * decay_to_final[..., None],
        delta_updates,
        precision=highest_precision,
    )
    return (following_state, outputs)


def delta_rule(query_rows, key_matrix_rows, value_rows, log_gates, write_rate):
    seq_rows, head_count, key_size = query_rows.shape
    value_size = value_rows.shape[2]
    blocks = seq_rows // GROUP

    def to_blocks(tensor_in):
        reshaped = tensor_in.reshape((blocks, GROUP) + tensor_in.shape[1:])
        return jnp.swapaxes(reshaped, 1, 2)

    initial = jnp.zeros((head_count, key_size, value_size), jnp.float32)
    final_state, outputs = lax.scan(
        jax.checkpoint(group_step),
        initial,
        (
            to_blocks(query_rows),
            to_blocks(key_matrix_rows),
            to_blocks(value_rows),
            to_blocks(log_gates),
            to_blocks(write_rate),
        ),
    )
    return jnp.swapaxes(outputs, 1, 2).reshape(seq_rows, head_count, value_size)


def mixer_core(
    proj_query,
    proj_key,
    proj_value,
    proj_outgate,
    proj_decay,
    proj_beta,
    kernel_query,
    kernel_key,
    kernel_value,
    rate_log,
    rate_bias,
    norm_gain,
):
    seq_rows, head_count = proj_decay.shape
    query_rows = conv_silu(proj_query, kernel_query).reshape(seq_rows, head_count, -1)
    query_rows = unit_norm(query_rows) * query_rows.shape[-1] ** (-0.5)
    key_matrix_rows = unit_norm(conv_silu(proj_key, kernel_key).reshape(seq_rows, head_count, -1))
    value_rows = conv_silu(proj_value, kernel_value).reshape(seq_rows, head_count, -1)
    write_rate = jax.nn.sigmoid(proj_beta)
    log_gates = -jnp.exp(rate_log) * jax.nn.softplus(proj_decay + rate_bias)
    mixed = delta_rule(query_rows, key_matrix_rows, value_rows, log_gates, write_rate)
    mixed = rms_norm(mixed, norm_gain)
    return mixed.reshape(seq_rows, -1) * jax.nn.silu(proj_outgate)


def local(
    hidden_in,
    grad_out,
    mix_gain,
    w_query,
    w_key,
    w_value,
    conv_query,
    conv_key,
    conv_value,
    w_decay,
    w_beta,
    log_rate,
    decay_bias,
    w_outgate,
    head_gain,
    w_output,
    ffn_gain,
    w_gate,
    w_up,
    w_down,
):
    shard_query = w_query.astype(jnp.bfloat16)
    shard_key = w_key.astype(jnp.bfloat16)
    shard_value = w_value.astype(jnp.bfloat16)
    shard_decay = w_decay.astype(jnp.bfloat16)
    shard_beta = w_beta.astype(jnp.bfloat16)
    shard_outgate = w_outgate.astype(jnp.bfloat16)
    shard_gate = w_gate.astype(jnp.bfloat16)
    shard_up = w_up.astype(jnp.bfloat16)
    shard_conv_q = conv_query.astype(jnp.bfloat16)
    shard_conv_k = conv_key.astype(jnp.bfloat16)
    shard_conv_v = conv_value.astype(jnp.bfloat16)
    shard_output = w_output.astype(jnp.bfloat16)
    shard_down = w_down.astype(jnp.bfloat16)
    (
        full_query,
        full_key,
        full_value,
        full_decay,
        full_beta,
        full_outgate,
        full_gate,
        full_up,
        full_conv_q,
        full_conv_k,
        full_conv_v,
        full_output,
        full_down,
    ) = (
        lax.all_gather(shard_query, "dp", axis=0, tiled=True),
        lax.all_gather(shard_key, "dp", axis=0, tiled=True),
        lax.all_gather(shard_value, "dp", axis=0, tiled=True),
        lax.all_gather(shard_decay, "dp", axis=0, tiled=True),
        lax.all_gather(shard_beta, "dp", axis=0, tiled=True),
        lax.all_gather(shard_outgate, "dp", axis=0, tiled=True),
        lax.all_gather(shard_gate, "dp", axis=0, tiled=True),
        lax.all_gather(shard_up, "dp", axis=0, tiled=True),
        lax.all_gather(shard_conv_q, "dp", axis=1, tiled=True),
        lax.all_gather(shard_conv_k, "dp", axis=1, tiled=True),
        lax.all_gather(shard_conv_v, "dp", axis=1, tiled=True),
        lax.all_gather(shard_output, "dp", axis=1, tiled=True),
        lax.all_gather(shard_down, "dp", axis=1, tiled=True),
    )
    tok_rows = hidden_in.shape[0]
    rows_in = hidden_in.astype(jnp.float32)
    mix_norm, mix_norm_pull = jax.vjp(rms_norm, rows_in, mix_gain)
    normed_full = lax.all_gather(mix_norm.astype(jnp.bfloat16), "tensor", axis=0, tiled=True)

    def project(weight_low):
        return jnp.dot(normed_full, weight_low, preferred_element_type=jnp.float32)

    proj_query = project(full_query)
    proj_key = project(full_key)
    proj_value = project(full_value)
    proj_outgate = project(full_outgate)
    proj_decay = project(full_decay)
    proj_beta = project(full_beta)
    head_count = proj_decay.shape[1]
    first_head = lax.axis_index("tensor") * head_count
    local_rate = lax.dynamic_slice_in_dim(log_rate, first_head, head_count)
    local_bias = lax.dynamic_slice_in_dim(decay_bias, first_head, head_count)
    mixed, core_pull = jax.vjp(
        mixer_core,
        proj_query,
        proj_key,
        proj_value,
        proj_outgate,
        proj_decay,
        proj_beta,
        full_conv_q.astype(jnp.float32),
        full_conv_k.astype(jnp.float32),
        full_conv_v.astype(jnp.float32),
        local_rate,
        local_bias,
        head_gain,
    )
    mixed_low = mixed.astype(jnp.bfloat16)
    middle = rows_in + lax.psum_scatter(
        jnp.dot(mixed_low, full_output, preferred_element_type=jnp.float32).astype(jnp.bfloat16),
        "tensor",
        scatter_dimension=0,
        tiled=True,
    ).astype(jnp.float32)
    ffn_norm, ffn_norm_pull = jax.vjp(rms_norm, middle, ffn_gain)
    ffn_rows = lax.all_gather(ffn_norm.astype(jnp.bfloat16), "tensor", axis=0, tiled=True)
    gate_pre = jnp.dot(ffn_rows, full_gate, preferred_element_type=jnp.float32)
    up_pre = jnp.dot(ffn_rows, full_up, preferred_element_type=jnp.float32)
    activ_float, act_pull = jax.vjp(swiglu, gate_pre, up_pre)
    activ = activ_float.astype(jnp.bfloat16)
    final_rows = middle + lax.psum_scatter(
        jnp.dot(activ, full_down, preferred_element_type=jnp.float32).astype(jnp.bfloat16),
        "tensor",
        scatter_dimension=0,
        tiled=True,
    ).astype(jnp.float32)
    hidden_out = final_rows.astype(jnp.bfloat16)
    (
        full_query,
        full_key,
        full_value,
        full_decay,
        full_beta,
        full_outgate,
        full_gate,
        full_up,
        full_conv_q,
        full_conv_k,
        full_conv_v,
        full_output,
        full_down,
    ) = (
        lax.all_gather(shard_query, "dp", axis=0, tiled=True),
        lax.all_gather(shard_key, "dp", axis=0, tiled=True),
        lax.all_gather(shard_value, "dp", axis=0, tiled=True),
        lax.all_gather(shard_decay, "dp", axis=0, tiled=True),
        lax.all_gather(shard_beta, "dp", axis=0, tiled=True),
        lax.all_gather(shard_outgate, "dp", axis=0, tiled=True),
        lax.all_gather(shard_gate, "dp", axis=0, tiled=True),
        lax.all_gather(shard_up, "dp", axis=0, tiled=True),
        lax.all_gather(shard_conv_q, "dp", axis=1, tiled=True),
        lax.all_gather(shard_conv_k, "dp", axis=1, tiled=True),
        lax.all_gather(shard_conv_v, "dp", axis=1, tiled=True),
        lax.all_gather(shard_output, "dp", axis=1, tiled=True),
        lax.all_gather(shard_down, "dp", axis=1, tiled=True),
    )
    cot_full = lax.all_gather(grad_out, "tensor", axis=0, tiled=True)
    part_down = jnp.einsum("sf,sd->fd", activ, cot_full, preferred_element_type=jnp.float32)
    grad_activ = jnp.einsum("sd,fd->sf", cot_full, full_down, preferred_element_type=jnp.float32)
    grad_gate_pre, grad_up_pre = act_pull(grad_activ)
    gate_low = grad_gate_pre.astype(jnp.bfloat16)
    up_low = grad_up_pre.astype(jnp.bfloat16)
    part_gate = jnp.einsum("sd,sf->df", ffn_rows, gate_low, preferred_element_type=jnp.float32)
    part_up = jnp.einsum("sd,sf->df", ffn_rows, up_low, preferred_element_type=jnp.float32)
    first_sum = jnp.einsum("sf,df->sd", gate_low, full_gate, preferred_element_type=jnp.float32)
    grad_ffn_norm = lax.psum_scatter(
        (
            first_sum + jnp.einsum("sf,df->sd", up_low, full_up, preferred_element_type=jnp.float32)
        ).astype(jnp.bfloat16),
        "tensor",
        scatter_dimension=0,
        tiled=True,
    ).astype(jnp.float32)
    grad_middle_norm, ffn_gain_part = ffn_norm_pull(grad_ffn_norm)
    grad_middle = grad_out.astype(jnp.float32) + grad_middle_norm
    grad_w_gate, grad_w_up, grad_w_down = (
        lax.psum_scatter(
            part_gate.astype(jnp.bfloat16), "dp", scatter_dimension=0, tiled=True
        ).astype(jnp.float32),
        lax.psum_scatter(
            part_up.astype(jnp.bfloat16), "dp", scatter_dimension=0, tiled=True
        ).astype(jnp.float32),
        lax.psum_scatter(
            part_down.astype(jnp.bfloat16), "dp", scatter_dimension=1, tiled=True
        ).astype(jnp.float32),
    )
    mix_cot = lax.all_gather(grad_middle.astype(jnp.bfloat16), "tensor", axis=0, tiled=True)
    part_output = jnp.einsum("sv,sd->vd", mixed_low, mix_cot, preferred_element_type=jnp.float32)
    grad_mixed = jnp.einsum("sd,vd->sv", mix_cot, full_output, preferred_element_type=jnp.float32)
    (
        grad_pq,
        grad_pk,
        grad_pv,
        grad_po,
        grad_pa,
        grad_pb,
        part_conv_q,
        part_conv_k,
        part_conv_v,
        grad_rate_local,
        grad_bias_local,
        head_gain_part,
    ) = core_pull(grad_mixed)
    query_low = grad_pq.astype(jnp.bfloat16)
    key_low = grad_pk.astype(jnp.bfloat16)
    value_low = grad_pv.astype(jnp.bfloat16)
    outgate_low = grad_po.astype(jnp.bfloat16)
    decay_low = grad_pa.astype(jnp.bfloat16)
    beta_low = grad_pb.astype(jnp.bfloat16)

    def weight_grad(grad_low):
        return jnp.einsum("sd,sc->dc", normed_full, grad_low, preferred_element_type=jnp.float32)

    part_query = weight_grad(query_low)
    part_key = weight_grad(key_low)
    part_value = weight_grad(value_low)
    part_outgate = weight_grad(outgate_low)
    part_decay = weight_grad(decay_low)
    part_beta = weight_grad(beta_low)
    pairs = (
        (query_low, full_query),
        (key_low, full_key),
        (value_low, full_value),
        (outgate_low, full_outgate),
        (decay_low, full_decay),
        (beta_low, full_beta),
    )
    running = jnp.zeros((tok_rows * lax.axis_size("tensor"), full_query.shape[0]), jnp.float32)
    for grad_low, weight_low in pairs:
        running = running + jnp.einsum(
            "sc,dc->sd", grad_low, weight_low, preferred_element_type=jnp.float32
        )
    grad_mix_norm = lax.psum_scatter(
        running.astype(jnp.bfloat16), "tensor", scatter_dimension=0, tiled=True
    ).astype(jnp.float32)
    grad_rows, mix_gain_part = mix_norm_pull(grad_mix_norm)
    grad_in = (grad_middle + grad_rows).astype(jnp.bfloat16)
    (
        grad_w_query,
        grad_w_key,
        grad_w_value,
        grad_w_decay,
        grad_w_beta,
        grad_w_outgate,
        grad_conv_query,
        grad_conv_key,
        grad_conv_value,
        grad_w_output,
    ) = (
        lax.psum_scatter(
            part_query.astype(jnp.bfloat16), "dp", scatter_dimension=0, tiled=True
        ).astype(jnp.float32),
        lax.psum_scatter(
            part_key.astype(jnp.bfloat16), "dp", scatter_dimension=0, tiled=True
        ).astype(jnp.float32),
        lax.psum_scatter(
            part_value.astype(jnp.bfloat16), "dp", scatter_dimension=0, tiled=True
        ).astype(jnp.float32),
        lax.psum_scatter(
            part_decay.astype(jnp.bfloat16), "dp", scatter_dimension=0, tiled=True
        ).astype(jnp.float32),
        lax.psum_scatter(
            part_beta.astype(jnp.bfloat16), "dp", scatter_dimension=0, tiled=True
        ).astype(jnp.float32),
        lax.psum_scatter(
            part_outgate.astype(jnp.bfloat16), "dp", scatter_dimension=0, tiled=True
        ).astype(jnp.float32),
        lax.psum_scatter(
            part_conv_q.astype(jnp.bfloat16), "dp", scatter_dimension=1, tiled=True
        ).astype(jnp.float32),
        lax.psum_scatter(
            part_conv_k.astype(jnp.bfloat16), "dp", scatter_dimension=1, tiled=True
        ).astype(jnp.float32),
        lax.psum_scatter(
            part_conv_v.astype(jnp.bfloat16), "dp", scatter_dimension=1, tiled=True
        ).astype(jnp.float32),
        lax.psum_scatter(
            part_output.astype(jnp.bfloat16), "dp", scatter_dimension=1, tiled=True
        ).astype(jnp.float32),
    )
    rate_placed = lax.dynamic_update_slice_in_dim(
        jnp.zeros_like(log_rate), grad_rate_local, first_head, 0
    )
    bias_placed = lax.dynamic_update_slice_in_dim(
        jnp.zeros_like(decay_bias), grad_bias_local, first_head, 0
    )
    grad_mix_gain, grad_ffn_gain, grad_head_gain, grad_log_rate, grad_decay_bias = lax.psum(
        (mix_gain_part, ffn_gain_part, head_gain_part, rate_placed, bias_placed), ("dp", "tensor")
    )
    return (
        hidden_out,
        grad_in,
        grad_mix_gain,
        grad_w_query,
        grad_w_key,
        grad_w_value,
        grad_conv_query,
        grad_conv_key,
        grad_conv_value,
        grad_w_decay,
        grad_w_beta,
        grad_log_rate,
        grad_decay_bias,
        grad_w_outgate,
        grad_head_gain,
        grad_w_output,
        grad_ffn_gain,
        grad_w_gate,
        grad_w_up,
        grad_w_down,
    )


def solution(mesh):
    return jax.shard_map(
        local,
        mesh=mesh,
        in_specs=(
            P(("dp", "tensor"), None),
            P(("dp", "tensor"), None),
            P(),
            P("dp", "tensor"),
            P("dp", "tensor"),
            P("dp", "tensor"),
            P(None, ("tensor", "dp")),
            P(None, ("tensor", "dp")),
            P(None, ("tensor", "dp")),
            P("dp", "tensor"),
            P("dp", "tensor"),
            P(),
            P(),
            P("dp", "tensor"),
            P(),
            P("tensor", "dp"),
            P(),
            P("dp", "tensor"),
            P("dp", "tensor"),
            P("tensor", "dp"),
        ),
        out_specs=(
            P(("dp", "tensor"), None),
            P(("dp", "tensor"), None),
            P(),
            P("dp", "tensor"),
            P("dp", "tensor"),
            P("dp", "tensor"),
            P(None, ("tensor", "dp")),
            P(None, ("tensor", "dp")),
            P(None, ("tensor", "dp")),
            P("dp", "tensor"),
            P("dp", "tensor"),
            P(),
            P(),
            P("dp", "tensor"),
            P(),
            P("tensor", "dp"),
            P(),
            P("dp", "tensor"),
            P("dp", "tensor"),
            P("tensor", "dp"),
        ),
        check_vma=False,
    )
```

profile of v0, /device:TPU:0, one launch (start us, length us, event | category | flops | bytes accessed | tf_op | source)
XLA Modules:
  0.0 2084.5 jit_solution(14309246485265998732)
XLA Ops:
  75.4 21.4 %all-gather.15.cloned.1.call-done = bf16[1024,2048]{1,0:T(8,128)(2,1)} async-done(((bf16[256,2048]{1,0:T(8,128)(2,1)}), bf16[1024,2048]{1,0:T(8,128)(2,1)}) %all-gather.15.cloned.1.call-update) | async-done | bytes 4194320 | tf_op jit(solution)/shard_map/all_gather | solution.py:202
  113.9 14.3 all-gather.21.cloned.1.call-done
  202.6 202.4 %while.42 = (s32[]{:T(128)}, f32[4,128,256]{2,1,0:T(8,128)S(1)}, f32[16,4,64,256]{3,2,1,0:T(8,128)}, f32[16,4,128,256]{3,2,1,0:T(8,128)}, f32[16,4,64]{2,1,0:T(4...) while((s32[]{:T(128)}, f32[4,128,256]{2,1,0:T(8,128)S(1)}, ...), condition=%wide.region_5.6_spmd.clone, body=%wide.region_3.5_spmd.clone.sunk | while | flops 580263936 | bytes 8277754 | solution.py:95
  419.0 14.8 multiply_convert_fusion.2
  445.7 49.0 %reduce-scatter.28.cloned.1.call-done = bf16[256,2048]{1,0:T(8,128)(2,1)} async-done(((bf16[1024,2048]{1,0:T(8,128)(2,1)}), bf16[256,2048]{1,0:T(8,128)(2,1)}) %reduce-scatter.28.cloned.1.call-update) | async-done | bytes 1048592 | tf_op jit(solution)/shard_map/reduce_scatter | solution.py:233
  501.3 56.1 %all-gather.29.cloned.1.call-done = bf16[2048,1408]{1,0:T(8,128)(2,1)} async-done(((bf16[256,1408]{1,0:T(8,128)(2,1)}), bf16[2048,1408]{1,0:T(8,128)(2,1)}) %all-gather.29.cloned.1.call-update) | async-done | bytes 5767184 | tf_op jit(solution)/shard_map/all_gather | solution.py:191
  557.4 54.0 %all-gather.27.cloned.1.call-done = bf16[1024,2048]{1,0:T(8,128)(2,1)} async-done(((bf16[256,2048]{1,0:T(8,128)(2,1)}), bf16[1024,2048]{1,0:T(8,128)(2,1)}) %all-gather.27.cloned.1.call-update) | async-done | bytes 4194320 | tf_op jit(solution)/shard_map/all_gather | solution.py:240
  623.0 51.0 %all-gather.31.cloned.1.call-done = bf16[2048,1408]{1,0:T(8,128)(2,1)} async-done(((bf16[256,1408]{1,0:T(8,128)(2,1)}), bf16[2048,1408]{1,0:T(8,128)(2,1)}) %all-gather.31.cloned.1.call-update) | async-done | bytes 5767184 | tf_op jit(solution)/shard_map/all_gather | solution.py:192
  685.7 41.7 %all-gather.35.cloned.1.call-done = bf16[1024,2048]{1,0:T(8,128)(2,1)} async-done(((bf16[256,2048]{1,0:T(8,128)(2,1)}), bf16[1024,2048]{1,0:T(8,128)(2,1)}) %all-gather.35.cloned.1.call-update) | async-done | bytes 4194320 | tf_op jit(solution)/shard_map/all_gather | solution.py:281
  727.4 63.0 %all-gather.33.cloned.1.call-done = bf16[1408,2048]{1,0:T(8,128)(2,1)} async-done(((bf16[1408,256]{1,0:T(8,128)(2,1)}), bf16[1408,2048]{1,0:T(8,128)(2,1)}) %all-gather.33.cloned.1.call-update) | async-done | bytes 5767184 | tf_op jit(solution)/shard_map/all_gather | solution.py:197
  790.4 15.6 multiply_convert_fusion
  825.8 50.6 %reduce-scatter.32.cloned.1.call-done = bf16[256,2048]{1,0:T(8,128)(2,1)} async-done(((bf16[1024,2048]{1,0:T(8,128)(2,1)}), bf16[256,2048]{1,0:T(8,128)(2,1)}) %reduce-scatter.32.cloned.1.call-update) | async-done | bytes 1048592 | tf_op jit(solution)/shard_map/reduce_scatter | solution.py:290
  917.4 16.7 all-gather.37.cloned.1.call-done
  934.1 15.3 multiply_reduce_fusion.5
  970.8 573.0 %while.43 = (s32[]{:T(128)}, f32[4,128,256]{2,1,0:T(8,128)}, f32[16,4,64,128]{3,2,1,0:T(8,128)}, f32[16,4,64,128]{3,2,1,0:T(8,128)}, f32[16,4,64,256]{3,2,1,0:T(...) while((s32[]{:T(128)}, f32[4,128,256]{2,1,0:T(8,128)}, ...), condition=%wide.region_25.26_spmd.clone, body=%wide.region_13.25_spmd.clone.sunk | while | flops 1589642496 | bytes 29028632 | solution.py:95
  1687.1 16.4 add_convert_fusion
  1739.3 34.8 %reduce-scatter.38.cloned.1.call-done = bf16[256,512]{1,0:T(8,128)(2,1)} async-done(((bf16[2048,512]{1,0:T(8,128)(2,1)}), bf16[256,512]{1,0:T(8,128)(2,1)}) %reduce-scatter.38.cloned.1.call-update) | async-done | bytes 262160 | tf_op jit(solution)/shard_map/reduce_scatter | solution.py:377
  1775.8 35.0 %reduce-scatter.36.cloned.1.call-done = bf16[256,512]{1,0:T(8,128)(2,1)} async-done(((bf16[2048,512]{1,0:T(8,128)(2,1)}), bf16[256,512]{1,0:T(8,128)(2,1)}) %reduce-scatter.36.cloned.1.call-update) | async-done | bytes 262160 | tf_op jit(solution)/shard_map/reduce_scatter | solution.py:374
  1812.6 49.3 %reduce-scatter.44.cloned.1.call-done = bf16[1024,256]{1,0:T(8,128)(2,1)} async-done(((bf16[1024,2048]{1,0:T(8,128)(2,1)}), bf16[1024,256]{1,0:T(8,128)(2,1)}) %reduce-scatter.44.cloned.1.call-update) | async-done | bytes 524304 | tf_op jit(solution)/shard_map/reduce_scatter | solution.py:401
  1864.0 48.3 %reduce-scatter.40.cloned.1.call-done = bf16[256,1024]{1,0:T(8,128)(2,1)} async-done(((bf16[2048,1024]{1,0:T(8,128)(2,1)}), bf16[256,1024]{1,0:T(8,128)(2,1)}) %reduce-scatter.40.cloned.1.call-update) | async-done | bytes 524304 | tf_op jit(solution)/shard_map/reduce_scatter | solution.py:380
  1914.5 48.3 %reduce-scatter.42.cloned.1.call-done = bf16[256,1024]{1,0:T(8,128)(2,1)} async-done(((bf16[2048,1024]{1,0:T(8,128)(2,1)}), bf16[256,1024]{1,0:T(8,128)(2,1)}) %reduce-scatter.42.cloned.1.call-update) | async-done | bytes 524304 | tf_op jit(solution)/shard_map/reduce_scatter | solution.py:389
  1964.9 52.0 %reduce-scatter.34.cloned.1.call-done = bf16[256,2048]{1,0:T(8,128)(2,1)} async-done(((bf16[1024,2048]{1,0:T(8,128)(2,1)}), bf16[256,2048]{1,0:T(8,128)(2,1)}) %reduce-scatter.34.cloned.1.call-update) | async-done | bytes 1048592 | tf_op jit(solution)/shard_map/reduce_scatter | solution.py:357
  2019.2 40.0 %all-reduce.29 = (f32[2048]{0:T(1024)}, f32[16]{0:T(128)}, f32[16]{0:T(128)}, f32[256]{0:T(256)}, f32[2048]{0:T(1024)}) all-reduce(f32[2048]{0:T(1024)S(1)} %get-tuple-element.689, f32[16]{0:T(128)S(1)} %multiply_dynamic-update-slice_fusion, f32[16]{0:T(128)S(1)} %dynamic_update_slice.68, ...), channel_id=1, replica_groups=mesh['dp'=8,'tensor'=4] {'dp','tensor'}, use_global_device_ids=true, to_apply=%region_31.32 | all-reduce | flops 4384 | bytes 35072 | tf_op jit(solution)/shard_map/psum | solution.py:411
  2059.2 13.7 reduce-scatter.30.cloned.1.call-done
  (2647 shorter events, 1255.3 us)
Async XLA Ops:
  15.1 161.8 %all-gather.19.cloned.1.call-start = ((), (), s32[]{:S(2)}) async-start(), calls=%async_computation.19 | async-start | bytes 4718592 | tf_op jit(solution)/shard_map/all_gather | solution.py:187
  16.1 402.9 %all-gather.23.cloned.1.call-start = ((), (), s32[]{:S(2)}) async-start(), calls=%async_computation.21 | async-start | bytes 4718592 | tf_op jit(solution)/shard_map/all_gather | solution.py:190
  17.1 416.7 %all-gather.25.cloned.1.call-start = ((), (), s32[]{:S(2)}) async-start(), calls=%async_computation.22 | async-start | bytes 4718592 | tf_op jit(solution)/shard_map/all_gather | solution.py:196
  18.2 476.4 %reduce-scatter.28.cloned.1.call-start = ((), (), s32[]{:S(2)}) async-start(), calls=%async_computation.23 | async-start | bytes 5242880 | tf_op jit(solution)/shard_map/reduce_scatter | solution.py:233
  445.4 166.0 %all-gather.27.cloned.1.call-start = ((), (), s32[]{:S(2)}) async-start(), calls=%async_computation.24 | async-start | bytes 5242880 | tf_op jit(solution)/shard_map/all_gather | solution.py:240
  497.9 176.1 %all-gather.31.cloned.1.call-start = ((), (), s32[]{:S(2)}) async-start(), calls=%async_computation.26 | async-start | bytes 6488064 | tf_op jit(solution)/shard_map/all_gather | solution.py:192
  499.0 228.5 %all-gather.35.cloned.1.call-start = ((), (), s32[]{:S(2)}) async-start(), calls=%async_computation.29 | async-start | bytes 5242880 | tf_op jit(solution)/shard_map/all_gather | solution.py:281
  499.7 290.7 %all-gather.33.cloned.1.call-start = ((), (), s32[]{:S(2)}) async-start(), calls=%async_computation.27 | async-start | bytes 6488064 | tf_op jit(solution)/shard_map/all_gather | solution.py:197
  501.2 375.1 %reduce-scatter.32.cloned.1.call-start = ((), (), s32[]{:S(2)}) async-start(), calls=%async_computation.30 | async-start | bytes 5242880 | tf_op jit(solution)/shard_map/reduce_scatter | solution.py:290
  881.3 834.9 %reduce-scatter.46.cloned.1.call-start = ((), (), s32[]{:S(2)}) async-start(), calls=%async_computation.38 | async-start | bytes 6488064 | tf_op jit(solution)/shard_map/reduce_scatter | solution.py:301
  892.3 826.2 %reduce-scatter.48.cloned.1.call-start = ((), (), s32[]{:S(2)}) async-start(), calls=%async_computation.39 | async-start | bytes 6488064 | tf_op jit(solution)/shard_map/reduce_scatter | solution.py:304
  904.9 815.9 %reduce-scatter.50.cloned.1.call-start = ((), (), s32[]{:S(2)}) async-start(), calls=%async_computation.40 | async-start | bytes 6488064 | tf_op jit(solution)/shard_map/reduce_scatter | solution.py:307
  917.4 806.2 %reduce-scatter.54.cloned.1.call-start = ((), (), s32[]{:S(2)}) async-start(), calls=%async_computation.42 | async-start | bytes 147456
  1580.9 144.2 %reduce-scatter.52.cloned.1.call-start = ((), (), s32[]{:S(2)}) async-start(), calls=%async_computation.41 | async-start | bytes 147456
  1588.6 137.8 %reduce-scatter.56.cloned.1.call-start = ((), (), s32[]{:S(2)}) async-start(), calls=%async_computation.43 | async-start | bytes 294912
  1589.7 138.1 %reduce-scatter.60.cloned.1.call-start = ((), (), s32[]{:S(2)}) async-start(), calls=%async_computation.45 | async-start | bytes 589824
  1593.9 143.8 %reduce-scatter.58.cloned.1.call-start = ((), (), s32[]{:S(2)}) async-start(), calls=%async_computation.44 | async-start | bytes 589824
  1598.0 176.0 %reduce-scatter.38.cloned.1.call-start = ((), (), s32[]{:S(2)}) async-start(), calls=%async_computation.34 | async-start | bytes 2359296 | tf_op jit(solution)/shard_map/reduce_scatter | solution.py:377
  1606.1 204.7 %reduce-scatter.36.cloned.1.call-start = ((), (), s32[]{:S(2)}) async-start(), calls=%async_computation.33 | async-start | bytes 2359296 | tf_op jit(solution)/shard_map/reduce_scatter | solution.py:374
  1615.1 246.8 %reduce-scatter.44.cloned.1.call-start = ((), (), s32[]{:S(2)}) async-start(), calls=%async_computation.37 | async-start | bytes 4718592 | tf_op jit(solution)/shard_map/reduce_scatter | solution.py:401
  1623.5 288.8 %reduce-scatter.40.cloned.1.call-start = ((), (), s32[]{:S(2)}) async-start(), calls=%async_computation.35 | async-start | bytes 4718592 | tf_op jit(solution)/shard_map/reduce_scatter | solution.py:380
  1646.9 315.9 %reduce-scatter.42.cloned.1.call-start = ((), (), s32[]{:S(2)}) async-start(), calls=%async_computation.36 | async-start | bytes 4718592 | tf_op jit(solution)/shard_map/reduce_scatter | solution.py:389
  1656.9 360.1 %reduce-scatter.34.cloned.1.call-start = ((), (), s32[]{:S(2)}) async-start(), calls=%async_computation.32 | async-start | bytes 5242880 | tf_op jit(solution)/shard_map/reduce_scatter | solution.py:357
  1703.5 369.4 %reduce-scatter.30.cloned.1.call-start = ((), (), s32[]{:S(2)}) async-start(), calls=%async_computation.28 | async-start | bytes 5242880 | tf_op jit(solution)/shard_map/reduce_scatter | solution.py:245
  (452 other events, 5916.5 us)
Sparse Core Ops, SparseCore 0:
  10.2 31.9 all-gather.16
  44.6 52.1 all-gather.14
  130.2 46.6 all-gather.18
  178.9 45.8 all-gather.22
  226.8 48.1 all-gather.24
  443.2 51.3 reduce-scatter.27
  497.0 60.3 all-gather.28
  560.0 51.3 all-gather.26
  613.5 60.4 all-gather.30
  676.0 51.3 all-gather.34
  729.5 60.8 all-gather.32
  825.4 50.8 reduce-scatter.31
  881.4 52.7 all-gather.36
  936.3 64.8 reduce-scatter.45
  1003.4 63.1 reduce-scatter.47
  1068.8 63.2 reduce-scatter.49
  1581.0 30.2 reduce-scatter.53
  1740.1 33.8 reduce-scatter.37
  1776.3 34.4 reduce-scatter.35
  1813.2 48.6 reduce-scatter.43
  1864.2 48.1 reduce-scatter.39
  1914.6 48.1 reduce-scatter.41
  1966.0 50.8 reduce-scatter.33
  2019.9 52.9 reduce-scatter.29
  (5 shorter events, 143.7 us)
where the time goes:
time: 2100 us; the launch traced here: 2080 us
  matrix products  810 us (39%)
  waiting for transfers between devices  720 us (34%)
  other arithmetic  238 us (11%)
  local copies, waits for them, and re-layouts  189 us (9%)
  blocking collectives  96.5 us (5%)
    dot_general x320, matrix products, unit_lower_inverse(): jnp.einsum('hab,hbc->hac', power, power, precision=highest_precision)  107 us
    dot_general x320, matrix products, unit_lower_inverse(): jnp.einsum('hab,hbc->hac', inverse, power, precision=highest_precision)  104 us
    dot_general x64, matrix products, group_step(): jnp.einsum('zrg,zgl->zrl', key_matrix_rows, carried_state, precision=high...  88.8 us
    all_gather x1, waiting for transfers between devices, local(): lax.all_gather(shard_down, 'dp', axis=1, tiled=True)  63 us
    dot_general x64, matrix products, group_step(): jnp.einsum('zrg,zgl->zrl', query_rows, carried_state, precision=highest_p...  62.8 us
    squeeze x64, local copies, waits for them, and re-layouts, delta_rule(): lax.scan(jax.checkpoint(group_step), initial, (to_blocks(query_rows), to_...  61.7 us
    all_gather x1, waiting for transfers between devices, local(): lax.all_gather(shard_gate, 'dp', axis=0, tiled=True)  56.1 us
    dot_general x48, matrix products, group_step(): jnp.einsum('pgs,pgd->psd', key_matrix_rows * decay_to_final[..., None], d...  54.8 us
  transfers between devices with their start and end apart: 29, of which 19 were waited for; matrix products, arithmetic and copies ran while one was open for 55% of the time, Pallas kernels for 0%

commit v1 on v0

v1 whole, which is shorter than its diff:
```python
import jax
import jax.numpy as jnp
from jax import lax
from jax.experimental import pallas as pl
from jax.experimental.pallas import tpu as pltpu
from jax.sharding import PartitionSpec as P

GROUP = 64
TAIL = 8
F32 = jnp.float32
BF16 = jnp.bfloat16
HIGHEST = lax.Precision.HIGHEST


def mm(a, b, dims=((1,), (0,))):
    return lax.dot_general(a.astype(BF16), b.astype(BF16), (dims, ((), ())), preferred_element_type=F32)


NN = ((1,), (0,))
NT = ((1,), (1,))
TN = ((0,), (0,))


def mm_exact(a, b, dims=NN):
    return lax.dot_general(a, b, (dims, ((), ())), precision=HIGHEST, preferred_element_type=F32)


def halves(a):
    high = a.astype(BF16)
    return high, (a - high.astype(F32)).astype(BF16)


def mm_split(a, b):
    a_high, a_low = halves(a)
    b_high, b_low = halves(b)
    return mm(a_high, b_high) + (mm(a_high, b_low) + mm(a_low, b_high))


def sigmoid(x):
    return 1.0 / (1.0 + jnp.exp(-x))


def softplus(x):
    return jnp.maximum(x, 0.0) + jnp.log1p(jnp.exp(-jnp.abs(x)))


def grid_iota(size):
    return (
        lax.broadcasted_iota(jnp.int32, (size, size), 0),
        lax.broadcasted_iota(jnp.int32, (size, size), 1),
    )


def unit_lower_inverses(lowers, row, col):
    size = lowers[0].shape[0]
    base = 16
    eye = jnp.where(row == col, 1.0, 0.0)
    powers = [jnp.where(row // base == col // base, -lower, 0.0) for lower in lowers]
    inverses = [eye + power for power in powers]
    reach = 2
    while reach < base:
        powers = [mm_split(power, power) for power in powers]
        inverses = [inverse + mm_split(inverse, power) for inverse, power in zip(inverses, powers)]
        reach *= 2
    while base < size:
        wide = 2 * base
        off = (row // wide == col // wide) & (row // base > col // base)
        right = [mm_split(jnp.where(off, lower, 0.0), inverse) for lower, inverse in zip(lowers, inverses)]
        inverses = [inverse - mm_split(inverse, r) for inverse, r in zip(inverses, right)]
        base = wide
    return inverses


def gates(p_ab, rate, bias, heads):
    pre = p_ab[:, :heads] + bias
    return sigmoid(p_ab[:, heads:]), -jnp.exp(rate) * softplus(pre), pre


def forward_kernel(
    pqkv, po, pab, taps, rate, bias, gain,
    mixed, conved, o_out, u_out, s_out, t_out,
    ext, state,
):
    heads = rate.shape[1]
    vals = po.shape[1]
    keys = (pqkv.shape[1] - vals) // 2
    dk, dv = keys // heads, vals // heads

    @pl.when(pl.program_id(0) == 0)
    def _():
        ext[...] = jnp.zeros_like(ext)
        state[...] = jnp.zeros_like(state)

    ext[TAIL:, :] = pqkv[...]
    n_taps = taps.shape[0]
    total = None
    for i in range(n_taps):
        start = TAIL - (n_taps - 1) + i
        term = ext[start : start + GROUP, :] * taps[i : i + 1, :]
        total = term if total is None else total + term
    conved[...] = total
    ext[:TAIL, :] = ext[GROUP:, :]

    row, col = grid_iota(GROUP)
    tri = jnp.where(row >= col, 1.0, 0.0)
    beta, log_decay, _ = gates(pab[...], rate[...], bias[...], heads)
    c_col = mm_exact(tri, log_decay)
    c_row = mm_exact(log_decay, jnp.where(row <= col, 1.0, 0.0), TN)
    start_decay = jnp.exp(c_col)
    end_decay = jnp.exp(c_col[GROUP - 1 :, :] - c_col)
    last_decay = jnp.exp(c_col[GROUP - 1 :, :])

    qs, ks, vs, bs, prods, relatives, lowers = [], [], [], [], [], [], []
    for h in range(heads):
        uq = conved[:, h * dk : (h + 1) * dk]
        uk = conved[:, keys + h * dk : keys + (h + 1) * dk]
        uv = conved[:, 2 * keys + h * dv : 2 * keys + (h + 1) * dv]
        q = uq * sigmoid(uq)
        qs.append(q * (lax.rsqrt(jnp.sum(q * q, -1, keepdims=True) + 1e-6) * dk**-0.5))
        k = uk * sigmoid(uk)
        ks.append(k * lax.rsqrt(jnp.sum(k * k, -1, keepdims=True) + 1e-6))
        vs.append(uv * sigmoid(uv))
        bs.append(beta[:, h : h + 1])
    for h in range(heads):
        prods.append(mm(jnp.concatenate([ks[h], qs[h]], 0), ks[h], NT))
    for h in range(heads):
        differ = jnp.minimum(c_col[:, h : h + 1] - c_row[h : h + 1, :], 0.0)
        relatives.append(jnp.where(row >= col, jnp.exp(differ), 0.0))
        lowers.append(jnp.where(row > col, bs[h] * relatives[h] * prods[h][:GROUP], 0.0))
    invs = [inverse.astype(BF16) for inverse in unit_lower_inverses(lowers, row, col)]
    states = [state[h] for h in range(heads)]
    lows = [s.astype(BF16) for s in states]
    reads = []
    for h in range(heads):
        e = start_decay[:, h : h + 1]
        reads.append(mm(jnp.concatenate([ks[h] * e, qs[h] * e], 0), lows[h]))
    us = [mm(invs[h], bs[h] * (vs[h] - reads[h][:GROUP])).astype(BF16) for h in range(heads)]
    outs = [reads[h][GROUP:] + mm(relatives[h] * prods[h][GROUP:], us[h]) for h in range(heads)]
    nexts = [
        last_decay[:, h : h + 1] * states[h] + mm(ks[h] * end_decay[:, h : h + 1], us[h], TN) for h in range(heads)
    ]
    for h in range(heads):
        cols = slice(h * dv, (h + 1) * dv)
        state[h] = nexts[h]
        t_out[0, h] = invs[h]
        s_out[0, h] = lows[h]
        u_out[:, cols] = us[h]
        o = outs[h]
        o_out[:, cols] = o.astype(o_out.dtype)
        n = o * lax.rsqrt(jnp.mean(o * o, -1, keepdims=True) + 1e-5)
        gate = po[:, cols]
        mixed[:, cols] = (n * gain[...] * (gate * sigmoid(gate))).astype(mixed.dtype)


def core_forward(pqkv, po, pab, taps, rate, bias, gain):
    rows, width = pqkv.shape
    vals = po.shape[1]
    keys = (width - vals) // 2
    heads = rate.shape[1]
    dk, dv = keys // heads, vals // heads
    blocks = rows // GROUP
    tokens = lambda width: pl.BlockSpec((GROUP, width), lambda n: (n, 0))
    fixed = lambda a: pl.BlockSpec(a.shape, lambda n: (0, 0))
    return pl.pallas_call(
        forward_kernel,
        grid=(blocks,),
        in_specs=[tokens(a.shape[1]) for a in (pqkv, po, pab)] + [fixed(a) for a in (taps, rate, bias, gain)],
        out_specs=[
            tokens(vals),
            tokens(2 * keys + vals),
            tokens(vals),
            tokens(vals),
            pl.BlockSpec((1, heads, dk, dv), lambda n: (n, 0, 0, 0)),
            pl.BlockSpec((1, heads, GROUP, GROUP), lambda n: (n, 0, 0, 0)),
        ],
        out_shape=[
            jax.ShapeDtypeStruct((rows, vals), BF16),
            jax.ShapeDtypeStruct((rows, 2 * keys + vals), F32),
            jax.ShapeDtypeStruct((rows, vals), BF16),
            jax.ShapeDtypeStruct((rows, vals), BF16),
            jax.ShapeDtypeStruct((blocks, heads, dk, dv), BF16),
            jax.ShapeDtypeStruct((blocks, heads, GROUP, GROUP), BF16),
        ],
        scratch_shapes=[
            pltpu.VMEM((GROUP + TAIL, 2 * keys + vals), F32),
            pltpu.VMEM((heads, dk, dv), F32),
        ],
        compiler_params=pltpu.CompilerParams(dimension_semantics=("arbitrary",), vmem_limit_bytes=40 * 2**20),
        cost_estimate=pl.CostEstimate(flops=8 * 10**9, bytes_accessed=32 * 2**20, transcendentals=10**7),
        name="core_forward",
    )(pqkv, po, pab, taps, rate, bias, gain)


def backward_kernel(
    gz, pqkv, po, pab, conved, o_in, u_in, s_in, t_in, taps, rate, bias, gain,
    dpqkv, dpo, dpab, dtaps, dsmall, dgain,
    ext, dstate,
):
    heads = rate.shape[1]
    vals = po.shape[1]
    keys = (pqkv.shape[1] - vals) // 2
    dk, dv = keys // heads, vals // heads

    @pl.when(pl.program_id(0) == 0)
    def _():
        ext[...] = jnp.zeros_like(ext)
        dstate[...] = jnp.zeros_like(dstate)
        for ref in (dtaps, dsmall, dgain):
            ref[...] = jnp.zeros_like(ref)

    row, col = grid_iota(GROUP)
    tri = jnp.where(row >= col, 1.0, 0.0)
    upper = jnp.where(row <= col, 1.0, 0.0)
    beta, log_decay, pre = gates(pab[...], rate[...], bias[...], heads)
    c_col = mm_exact(tri, log_decay)
    c_row = mm_exact(log_decay, upper, TN)
    start_decay = jnp.exp(c_col)
    end_decay = jnp.exp(c_col[GROUP - 1 :, :] - c_col)
    last_decay = jnp.exp(c_col[GROUP - 1 :, :])
    lane = lax.broadcasted_iota(jnp.int32, (1, heads), 1)
    d_beta = jnp.zeros((GROUP, heads), F32)
    after = jnp.zeros((GROUP, heads), F32)
    before = jnp.zeros((GROUP, heads), F32)
    d_log = jnp.zeros((GROUP, heads), F32)
    gain_sum = jnp.zeros((1, dv), F32)

    for h in range(heads):
        ks, vs = slice(h * dk, (h + 1) * dk), slice(h * dv, (h + 1) * dv)
        kx, vx = slice(keys + h * dk, keys + (h + 1) * dk), slice(2 * keys + h * dv, 2 * keys + (h + 1) * dv)
        here = lane == h
        uq, uk, uv = conved[:, ks], conved[:, kx], conved[:, vx]
        sq, sk, sv = sigmoid(uq), sigmoid(uk), sigmoid(uv)
        q = uq * sq
        q_norm = lax.rsqrt(jnp.sum(q * q, -1, keepdims=True) + 1e-6)
        q = q * q_norm
        k = uk * sk
        k_norm = lax.rsqrt(jnp.sum(k * k, -1, keepdims=True) + 1e-6)
        k = k * k_norm
        v = uv * sv
        qs = q * dk**-0.5
        b = beta[:, h : h + 1]
        e = start_decay[:, h : h + 1]
        f = end_decay[:, h : h + 1]
        kb = k.astype(BF16)
        qb = qs.astype(BF16)

        o = o_in[:, vs].astype(F32)
        o_norm = lax.rsqrt(jnp.mean(o * o, -1, keepdims=True) + 1e-5)
        n = o * o_norm
        gate = po[:, vs]
        sg = sigmoid(gate)
        g = gz[:, vs]
        gn = g * n
        act = gate * sg
        gain_sum = gain_sum + jnp.sum(gn * act, 0, keepdims=True)
        dpo[:, vs] = (gn * gain[...] * (sg * (1.0 + gate * (1.0 - sg)))).astype(dpo.dtype)
        dn = g * gain[...] * act
        do = o_norm * (dn - n * jnp.mean(dn * n, -1, keepdims=True))

        prod = mm(jnp.concatenate([kb, qb], 0), kb, NT)
        relative = jnp.where(row >= col, jnp.exp(jnp.minimum(c_col[:, h : h + 1] - c_row[h : h + 1, :], 0.0)), 0.0)
        kk, qk = prod[:GROUP], prod[GROUP:]
        strict = jnp.where(row > col, relative, 0.0)
        mix = relative * qk
        s_prev = s_in[0, h]
        u = u_in[:, vs]
        inv = t_in[0, h]
        ds = dstate[h]
        ds_low = ds.astype(BF16)
        dob = do.astype(BF16)
        ke, qe, kd = k * e, qs * e, k * f
        du = mm(mix, dob, TN) + mm(kd, ds_low)
        dr = mm(inv, du, TN)
        pair = jnp.concatenate([dob, dr.astype(BF16)], 0)
        dstate[h] = last_decay[:, h : h + 1] * ds + mm(jnp.concatenate([qe, -(b * ke)], 0), pair, TN)
        cross = mm(pair, u, NT)
        dmix = jnp.where(row >= col, cross[:GROUP], 0.0)
        dlow = jnp.where(row > col, -cross[GROUP:], 0.0)
        back = mm(pair, s_prev, NT)
        dqe, x = back[:GROUP], back[GROUP:]
        dkd = mm(u, ds_low, NT)
        dke = -(b * x)
        rk = strict * kk
        d_beta = d_beta + jnp.where(
            here,
            jnp.sum(dr * v, -1, keepdims=True) - jnp.sum(x * ke, -1, keepdims=True) + jnp.sum(dlow * rk, -1, keepdims=True),
            0.0,
        )
        dpair = dlow * (b * rk) + dmix * mix
        spread = mm(upper, dpair)
        last_part = last_decay[:, h : h + 1] * jnp.sum(ds * s_prev.astype(F32), keepdims=True)
        d_log = d_log + jnp.where(here, jnp.sum(jnp.where(row > col, spread, 0.0), -1, keepdims=True) + last_part, 0.0)
        after = after + jnp.where(here, jnp.sum(dqe * qe + dke * ke, -1, keepdims=True), 0.0)
        before = before + jnp.where(here, jnp.sum(dkd * kd, -1, keepdims=True), 0.0)
        dqk = dmix * relative
        dkk = dlow * (b * strict)
        first = mm(jnp.concatenate([dqk, dkk], 0), kb)
        dq = e * dqe + first[:GROUP]
        dk_ = e * dke + f * dkd + first[GROUP:] + mm(jnp.concatenate([dkk, dqk], 0), jnp.concatenate([kb, qb], 0), TN)
        dq = dq * dk**-0.5
        dq = q_norm * (dq - q * jnp.sum(dq * q, -1, keepdims=True))
        dk_ = k_norm * (dk_ - k * jnp.sum(dk_ * k, -1, keepdims=True))
        ext[:GROUP, ks] = dq * (sq * (1.0 + uq * (1.0 - sq)))
        ext[:GROUP, kx] = dk_ * (sk * (1.0 + uk * (1.0 - sk)))
        ext[:GROUP, vx] = (b * dr) * (sv * (1.0 + uv * (1.0 - sv)))

    d_log = d_log + mm_exact(upper, after) + mm_exact(jnp.where(row > col, 1.0, 0.0), before)
    d_pre = d_log * (-jnp.exp(rate[...])) * sigmoid(pre)
    dpab[:, :heads] = d_pre
    dpab[:, heads:] = d_beta * beta * (1.0 - beta)
    dsmall[0:1, :heads] += jnp.sum(d_log * log_decay, 0, keepdims=True)
    dsmall[0:1, heads:] += jnp.sum(d_pre, 0, keepdims=True)
    dgain[...] += gain_sum

    n_taps = taps.shape[0]
    rows_in = pqkv[...]
    total = None
    for i in range(n_taps):
        start = n_taps - 1 - i
        piece = ext[start : start + GROUP, :]
        term = piece * taps[i : i + 1, :]
        total = term if total is None else total + term
        dtaps[i : i + 1, :] += jnp.sum(piece * rows_in, 0, keepdims=True)
    dpqkv[...] = total.astype(dpqkv.dtype)
    ext[GROUP:, :] = ext[:TAIL, :]


def core_backward(gz, pqkv, po, pab, kept, taps, rate, bias, gain):
    conved, o_in, u_in, s_in, t_in = kept
    rows, width = pqkv.shape
    vals = po.shape[1]
    keys = (width - vals) // 2
    heads = rate.shape[1]
    dk, dv = keys // heads, vals // heads
    blocks = rows // GROUP
    tokens = lambda width: pl.BlockSpec((GROUP, width), lambda n: (blocks - 1 - n, 0))
    stacked = lambda a: pl.BlockSpec((1,) + a.shape[1:], lambda n: (blocks - 1 - n, 0, 0, 0))
    fixed = lambda shape: pl.BlockSpec(shape, lambda n: (0, 0))
    small = (1, 2 * heads)
    return pl.pallas_call(
        backward_kernel,
        grid=(blocks,),
        in_specs=[tokens(a.shape[1]) for a in (gz, pqkv, po, pab, conved, o_in, u_in)]
        + [stacked(s_in), stacked(t_in)]
        + [fixed(a.shape) for a in (taps, rate, bias, gain)],
        out_specs=[tokens(a.shape[1]) for a in (pqkv, po, pab)]
        + [fixed(taps.shape), fixed(small), fixed(gain.shape)],
        out_shape=[jax.ShapeDtypeStruct(a.shape, BF16) for a in (pqkv, po)]
        + [jax.ShapeDtypeStruct(pab.shape, F32)]
        + [jax.ShapeDtypeStruct(s, F32) for s in (taps.shape, small, gain.shape)],
        scratch_shapes=[
            pltpu.VMEM((GROUP + TAIL, 2 * keys + vals), F32),
            pltpu.VMEM((heads, dk, dv), F32),
        ],
        compiler_params=pltpu.CompilerParams(dimension_semantics=("arbitrary",), vmem_limit_bytes=40 * 2**20),
        cost_estimate=pl.CostEstimate(flops=20 * 10**9, bytes_accessed=48 * 2**20, transcendentals=10**7),
        name="core_backward",
    )(gz, pqkv, po, pab, conved, o_in, u_in, s_in, t_in, taps, rate, bias, gain)


def rms_norm(values, gain_vec):
    return values * lax.rsqrt(jnp.mean(values * values, -1, keepdims=True) + 1e-05) * gain_vec


def dot(a, b, dims=NN):
    return lax.dot_general(a, b, (dims, ((), ())), preferred_element_type=F32)


def swap(piece, mask):
    return lax.ppermute(piece, "tensor", [(i, i ^ mask) for i in range(4)])


def gather_rows(own):
    if lax.axis_size("tensor") != 4:
        return lax.all_gather(own, "tensor", axis=0, tiled=True)
    half = own.shape[0] // 2
    first, second = swap(own, 1), swap(own, 2)
    return jnp.concatenate([own, first, second, swap(second[:half], 1), swap(first[half:], 2)], 0)


def scatter_rows(part):
    if lax.axis_size("tensor") != 4:
        return lax.psum_scatter(part, "tensor", scatter_dimension=0, tiled=True).astype(F32)
    rows, half = part.shape[0] // 4, part.shape[1] // 2

    def chunk(k, columns):
        return part[k * rows : (k + 1) * rows, columns]

    sums = []
    for columns, one, two in ((slice(0, half), 1, 2), (slice(half, 2 * half), 2, 1)):
        got = swap(jnp.concatenate([chunk(one, columns), chunk(3, columns)], 0), one).astype(F32)
        own = chunk(0, columns).astype(F32) + got[:rows]
        passed = (chunk(two, columns).astype(F32) + got[rows:]).astype(BF16)
        sums.append(own + swap(passed, two).astype(F32))
    return jnp.concatenate(sums, 1)


def reorder(rows_in):
    if lax.axis_size("tensor") != 4:
        return rows_in
    rows = rows_in.shape[0] // 4
    me = lax.axis_index("tensor")
    return jnp.concatenate([lax.dynamic_slice_in_dim(rows_in, (me ^ k) * rows, rows, 0) for k in range(4)], 0)


def norm_back(values, gain_vec, grad):
    factor = lax.rsqrt(jnp.mean(values * values, -1, keepdims=True) + 1e-05)
    normal = values * factor
    scaled = grad * gain_vec
    return (
        factor * (scaled - normal * jnp.mean(scaled * normal, -1, keepdims=True)),
        jnp.sum(grad * normal, 0),
    )


def gather_dp(shard, axis):
    return lax.all_gather(shard.astype(BF16), "dp", axis=axis, tiled=True)


def scatter_dp(part, axis):
    return lax.psum_scatter(part.astype(BF16), "dp", scatter_dimension=axis, tiled=True).astype(F32)


def local(
    hidden_in,
    grad_out,
    mix_gain,
    w_query,
    w_key,
    w_value,
    conv_query,
    conv_key,
    conv_value,
    w_decay,
    w_beta,
    log_rate,
    decay_bias,
    w_outgate,
    head_gain,
    w_output,
    ffn_gain,
    w_gate,
    w_up,
    w_down,
):
    dp = lax.axis_size("dp")
    model = hidden_in.shape[1]
    keys, vals, hidden = w_query.shape[1], w_value.shape[1], w_gate.shape[1]
    heads = w_decay.shape[1]
    first_head = lax.axis_index("tensor") * heads
    rate = lax.dynamic_slice_in_dim(log_rate, first_head, heads)[None]
    bias = lax.dynamic_slice_in_dim(decay_bias, first_head, heads)[None]
    gain = head_gain[None]

    narrow = jnp.concatenate([w_decay, w_beta], 1).T
    kernels = jnp.concatenate([conv_query, conv_key, conv_value], 1)
    wide = max(narrow.shape[1], kernels.shape[1])
    pad = lambda a: jnp.pad(a, ((0, 0), (0, wide - a.shape[1])))
    few = lax.all_gather(jnp.concatenate([pad(narrow), pad(kernels)], 0).astype(BF16), "dp")
    unroll = lambda a: jnp.swapaxes(a, 0, 1).reshape(a.shape[1], -1)
    full_narrow = unroll(few[:, : 2 * heads, : narrow.shape[1]])
    pieces = few[:, 2 * heads :, : kernels.shape[1]]
    cut = (conv_query.shape[1], conv_query.shape[1] + conv_key.shape[1])
    taps = jnp.concatenate(
        [unroll(pieces[:, :, : cut[0]]), unroll(pieces[:, :, cut[0] : cut[1]]), unroll(pieces[:, :, cut[1] :])], 1
    ).astype(F32)

    full_qkv = gather_dp(jnp.concatenate([w_query, w_key, w_value], 1), 0)
    full_outgate = gather_dp(w_outgate, 0)
    full_output = gather_dp(w_output, 1)
    full_pair = gather_dp(jnp.concatenate([w_gate, w_up], 1), 0)
    full_down = gather_dp(w_down, 1)

    rows_in = hidden_in.astype(F32)
    normed = reorder(gather_rows(rms_norm(rows_in, mix_gain).astype(BF16)))
    pqkv = dot(normed, full_qkv)
    pab = dot(normed, full_narrow, NT)
    po = dot(normed, full_outgate)
    mixed, *kept = core_forward(pqkv, po, pab, taps, rate, bias, gain)
    middle = rows_in + scatter_rows(reorder(dot(mixed, full_output).astype(BF16)))

    ffn_rows = gather_rows(rms_norm(middle, ffn_gain).astype(BF16))
    pre = dot(ffn_rows, full_pair)
    gate_pre, up_pre = pre[:, :hidden], pre[:, hidden:]
    gate_sig = jax.nn.sigmoid(gate_pre)
    activ = (gate_pre * gate_sig * up_pre).astype(BF16)
    cot = gather_rows(grad_out)
    grad_w_down = scatter_dp(dot(activ, cot, TN), 1)
    hidden_out = (middle + scatter_rows(dot(activ, full_down).astype(BF16))).astype(BF16)
    grad_activ = dot(cot, full_down, NT)
    grad_gate_pre = (grad_activ * up_pre * gate_sig * (1.0 + gate_pre * (1.0 - gate_sig))).astype(BF16)
    grad_up_pre = (grad_activ * (gate_pre * gate_sig)).astype(BF16)
    grad_pre = jnp.concatenate([grad_gate_pre, grad_up_pre], 1)
    grad_pair = scatter_dp(dot(ffn_rows, grad_pre, TN), 0)
    grad_ffn_norm = scatter_rows(dot(grad_pre, full_pair, NT).astype(BF16))
    grad_middle_norm, ffn_gain_part = norm_back(middle, ffn_gain, grad_ffn_norm)
    grad_middle = grad_out.astype(F32) + grad_middle_norm

    mix_cot = reorder(gather_rows(grad_middle.astype(BF16)))
    grad_mixed = dot(mix_cot, full_output, NT)
    grad_w_output = scatter_dp(dot(mixed, mix_cot, TN), 1)
    grad_pqkv, grad_po, grad_pab, grad_taps, grad_small, grad_gain = core_backward(
        grad_mixed, pqkv, po, pab, kept, taps, rate, bias, gain
    )
    grad_w_outgate = scatter_dp(dot(normed, grad_po, TN), 0)
    grad_qkv = scatter_dp(dot(normed, grad_pqkv, TN), 0)
    low_pab = grad_pab.astype(BF16)
    grad_normed = dot(grad_pqkv, full_qkv, NT) + dot(grad_po, full_outgate, NT) + dot(low_pab, full_narrow)
    grad_mix_norm = scatter_rows(reorder(grad_normed.astype(BF16)))
    grad_rows, mix_gain_part = norm_back(rows_in, mix_gain, grad_mix_norm)
    grad_in = (grad_middle + grad_rows).astype(BF16)

    grad_narrow = dot(low_pab, normed, TN)
    roll = lambda a: jnp.swapaxes(a.reshape(a.shape[0], dp, -1), 0, 1)
    grad_kernels = jnp.concatenate(
        [roll(grad_taps[:, :keys]), roll(grad_taps[:, keys : 2 * keys]), roll(grad_taps[:, 2 * keys :])], 2
    )
    pad3 = lambda a: jnp.pad(a, ((0, 0), (0, 0), (0, wide - a.shape[2])))
    few_grads = lax.psum_scatter(
        jnp.concatenate([pad3(roll(grad_narrow)), pad3(grad_kernels)], 1), "dp", scatter_dimension=0, tiled=False
    )
    grad_narrow = few_grads[: 2 * heads, : narrow.shape[1]].T
    grad_kernels = few_grads[2 * heads :, : kernels.shape[1]]

    place = lambda a: lax.dynamic_update_slice_in_dim(jnp.zeros_like(log_rate), a, first_head, 0)
    sums = lax.psum(
        jnp.concatenate(
            [
                mix_gain_part,
                ffn_gain_part,
                grad_gain[0],
                place(grad_small[0, :heads]),
                place(grad_small[0, heads:]),
            ]
        ),
        ("dp", "tensor"),
    )
    ends = [model, 2 * model, 2 * model + head_gain.shape[0], 2 * model + head_gain.shape[0] + log_rate.shape[0]]
    grad_mix_gain, grad_ffn_gain, grad_head_gain, grad_log_rate, grad_decay_bias = jnp.split(sums, ends)
    return (
        hidden_out,
        grad_in,
        grad_mix_gain,
        grad_qkv[:, :keys],
        grad_qkv[:, keys : 2 * keys],
        grad_qkv[:, 2 * keys :],
        grad_kernels[:, : cut[0]],
        grad_kernels[:, cut[0] : cut[1]],
        grad_kernels[:, cut[1] :],
        grad_narrow[:, :heads],
        grad_narrow[:, heads:],
        grad_log_rate,
        grad_decay_bias,
        grad_w_outgate,
        grad_head_gain,
        grad_w_output,
        grad_ffn_gain,
        grad_pair[:, :hidden],
        grad_pair[:, hidden:],
        grad_w_down,
    )


def solution(mesh):
    rows, both, flat = P(("dp", "tensor"), None), P("dp", "tensor"), P(None, ("tensor", "dp"))
    turned = P("tensor", "dp")
    return jax.shard_map(
        local,
        mesh=mesh,
        in_specs=(
            *(rows, rows, P()),
            *(both, both, both, flat, flat, flat, both, both),
            *(P(), P(), both, P(), turned, P(), both, both, turned),
        ),
        out_specs=(
            *(rows, rows, P()),
            *(both, both, both, flat, flat, flat, both, both),
            *(P(), P(), both, P(), turned, P(), both, both, turned),
        ),
        check_vma=False,
    )
```

time: 2100 us -> 1030 us (0.49)
  matrix products: 810 us -> 186 us
  other arithmetic: 238 us -> 39.3 us
  waiting for transfers between devices: 720 us -> 542 us
  local copies, waits for them, and re-layouts: 189 us -> 42.5 us
  Pallas kernels: 0 us -> 103 us
  blocking collectives: 96.5 us -> 52.7 us
  starting transfers between devices: 2.79 us -> 43.8 us
    dot_general x1086 -> x18, matrix products: 810 us -> 186 us  [dot(): return lax.dot_general(a, b, (dims, ((), ())), preferred_element_type=F32)]
    all_gather x12 -> x5, waiting for transfers between devices: 329 us -> 72.7 us  [gather_dp(): return lax.all_gather(shard.astype(BF16), 'dp', axis=axis, tiled=True)]
    ppermute x0 -> x32, waiting for transfers between devices: none -> 250 us  [swap(): return lax.ppermute(piece, 'tensor', [(i, i ^ mask) for i in range(4)])]
    reduce_scatter x12 -> x6, waiting for transfers between devices: 381 us -> 219 us  [the longest x5 219 us: scatter_dp(): lax.psum_scatter(part.astype(BF16), 'dp', scatter_dimension=axis, tiled=T...]
    pallas_call x0 -> x2, Pallas kernels: none -> 103 us  [the longest x1 60.3 us: core_backward(): pl.pallas_call(backward_kernel, grid=(blocks,), in_specs=[tokens(a.shape[...]
    reduce_sum x76 -> x2, other arithmetic: 74.3 us -> 2.39 us  [norm_back(): jnp.sum(grad * normal, 0)]
    squeeze x64 -> x0, local copies, waits for them, and re-layouts: 61.7 us -> none  [delta_rule(): lax.scan(jax.checkpoint(group_step), initial, (to_blocks(query_rows), to_...]
    ppermute x0 -> x32, starting transfers between devices: none -> 42.8 us  [swap(): return lax.ppermute(piece, 'tensor', [(i, i ^ mask) for i in range(4)])]
  transfers between devices with their start and end apart: 29 -> 43, of which waited for: 19 -> 29; matrix products, arithmetic and copies ran while one was open for 55% -> 20% of each run, Pallas kernels for 0% -> 4%
where the time goes in v1:
time: 1030 us; the launch traced here: 1020 us
  waiting for transfers between devices  542 us (53%)
  matrix products  186 us (18%)
  Pallas kernels  103 us (10%)
  blocking collectives  52.7 us (5%)
  starting transfers between devices  43.8 us (4%)
  local copies, waits for them, and re-layouts  42.5 us (4%)
  other arithmetic  39.3 us (4%)
  between operations  15.2 us (1%)
    ppermute x32, waiting for transfers between devices, swap(): return lax.ppermute(piece, 'tensor', [(i, i ^ mask) for i in range(4)])  250 us
    reduce_scatter x5, waiting for transfers between devices, scatter_dp(): lax.psum_scatter(part.astype(BF16), 'dp', scatter_dimension=axis, tiled=T...  219 us
    dot_general x18, matrix products, dot(): return lax.dot_general(a, b, (dims, ((), ())), preferred_element_type=F32)  186 us
    all_gather x5, waiting for transfers between devices, gather_dp(): return lax.all_gather(shard.astype(BF16), 'dp', axis=axis, tiled=True)  72.7 us
    pallas_call x1, Pallas kernels, core_backward(): pl.pallas_call(backward_kernel, grid=(blocks,), in_specs=[tokens(a.shape[...  60.3 us
    ppermute x32, starting transfers between devices, swap(): return lax.ppermute(piece, 'tensor', [(i, i ^ mask) for i in range(4)])  42.8 us
    pallas_call x1, Pallas kernels, core_forward(): pl.pallas_call(forward_kernel, grid=(blocks,), in_specs=[tokens(a.shape[1...  42.4 us
    psum x1, blocking collectives, local(): lax.psum(jnp.concatenate([mix_gain_part, ffn_gain_part, grad_gain[0], pla...  38.2 us
  transfers between devices with their start and end apart: 43, of which 29 were waited for; matrix products, arithmetic and copies ran while one was open for 20% of the time, Pallas kernels for 4%

profile of v1, /device:TPU:0, one launch (start us, length us, event | category | flops | bytes accessed | tf_op | source)
XLA Modules:
  0.0 1024.2 jit_solution(8696376830367108233)
XLA Ops:
  25.7 14.5 %all_gather.21 = bf16[8,12,256]{2,1,0:T(8,128)(2,1)S(1)} all-gather(bf16[1,12,256]{2,1,0:T(8,128)(2,1)S(1)} %pad_maximum_fusion.17), channel_id=1, replica_groups=mesh['dp'=8,'tensor'=4] {'dp'}, dimensions={0}, use_global_device_ids=true | all-gather | bytes 55296 | tf_op jit(solution)/shard_map/all_gather | solution.py:459
  77.1 66.5 %all-gather.6.cloned.1.call-done = bf16[2048,2048]{1,0:T(8,128)(2,1)} async-done(((bf16[256,2048]{1,0:T(8,128)(2,1)}), bf16[2048,2048]{1,0:T(8,128)(2,1)}) %all-gather.6.cloned.1.call-update) | async-done | bytes 8388624 | tf_op jit(solution)/shard_map/all_gather | solution.py:417
  143.6 14.1 %fusion.40.pqkv = f32[1024,2048]{1,0:T(8,128)} fusion(bf16[2048,2048]{1,0:T(8,128)(2,1)} %all-gather.6.cloned.1.call-done, bf16[256,2048]{1,0:T(8,128)(2,1)S(1)} %get-tuple-element.85, bf16[256,2048]{1,0:T(8,128)(2,1)} %copy-done.25, bf16[256,2048]{1,0:T(8,128)(2,1)} %copy-done.27, bf16[256,2048]{1,0:T(8,128)(2,1)S(1)} %get-tuple-element.84), kind=kOutput, calls=%fused_computation.144 | convolution fusion | flops 8606711808 | bytes 20971520 | tf_op jit(solution)/shard_map/dot_general | solution.py:366
  157.7 42.4 %core_forward.1 = (bf16[1024,1024]{1,0:T(8,128)(2,1)S(1)}, f32[1024,2048]{1,0:T(8,128)}, bf16[1024,1024]{1,0:T(8,128)(2,1)S(1)}, bf16[1024,1024]{1,0:T(8,128)(2,...) custom-call(f32[1024,2048]{1,0:T(8,128)} %fusion.40.pqkv, f32[1024,1024]{1,0:T(8,128)} %fusion.39.po, ...), custom_call_target="tpu_custom_call" | custom-call | flops 8000000000 | bytes 33554432 | tf_op jit(solution)/shard_map/core_forward/pallas_call | solution.py:164
  217.0 22.3 %collective-permute-done.4 = bf16[512,1024]{1,0:T(8,128)(2,1)S(1)} collective-permute-done((bf16[512,1024]{1,0:T(8,128)(2,1)S(1)}, bf16[512,1024]{1,0:T(8,128)(2,1)S(1)}, u32[]{:S(2)}, u32[]{:S(2)}) %collective-permute-start.4) | collective-permute-done | bytes 1048608 | tf_op jit(solution)/shard_map/ppermute | solution.py:370
  241.6 11.7 %collective-permute-done.5 = bf16[256,1024]{1,0:T(8,128)(2,1)S(1)} collective-permute-done((bf16[256,1024]{1,0:T(8,128)(2,1)S(1)}, bf16[256,1024]{1,0:T(8,128)(2,1)S(1)}, u32[]{:S(2)}, u32[]{:S(2)}) %collective-permute-start.5) | collective-permute-done | bytes 524320 | tf_op jit(solution)/shard_map/ppermute | solution.py:370
  257.3 11.3 %collective-permute-done.7 = bf16[256,1024]{1,0:T(8,128)(2,1)S(1)} collective-permute-done((bf16[256,1024]{1,0:T(8,128)(2,1)S(1)}, bf16[256,1024]{1,0:T(8,128)(2,1)S(1)}, u32[]{:S(2)}, u32[]{:S(2)}) %collective-permute-start.7) | collective-permute-done | bytes 524320 | tf_op jit(solution)/shard_map/ppermute | solution.py:370
  312.9 11.9 %collective-permute-done.8 = bf16[256,2048]{1,0:T(8,128)(2,1)S(1)} collective-permute-done((bf16[256,2048]{1,0:T(8,128)(2,1)S(1)}, bf16[256,2048]{1,0:T(8,128)(2,1)S(1)}, u32[]{:S(2)}, u32[]{:S(2)}) %collective-permute-start.8) | collective-permute-done | bytes 1048608 | tf_op jit(solution)/shard_map/ppermute | solution.py:370
  335.6 19.4 %fusion.51 = f32[1024,2816]{1,0:T(8,128)} fusion(bf16[1024,2048]{1,0:T(8,128)(2,1)} %constant_dynamic-update-slice_fusion.5, bf16[2048,2816]{1,0:T(8,128)(2,1)} %all-gather.12.cloned.1.call-done), kind=kOutput, calls=%fused_computation.154 | convolution fusion | flops 11811160064 | bytes 27262976 | tf_op jit(solution)/shard_map/dot_general | solution.py:366
  361.2 16.7 %multiply_convert_fusion.1 = (bf16[1024,1408]{1,0:T(8,128)(2,1)}, bf16[1024,1408]{1,0:T(8,128)(2,1)}, bf16[1024,1408]{1,0:T(8,128)(2,1)S(1)}) fusion(f32[1024,2816]{1,0:T(8,128)} %fusion.51, bf16[1024,2048]{1,0:T(8,128)(2,1)} %copy-done.35, bf16[1408,2048]{1,0:T(8,128)(2,1)} %all-gather.14.cloned.1.call-done), kind=kOutput, calls=%fused_computation.6 | convolution fusion | flops 5927206912 | bytes 30146560 | tf_op jit(solution)/shard_map/dot_general | solution.py:366
  390.8 18.2 %convolution_convert_fusion.3 = bf16[1024,2048]{1,0:T(8,128)(2,1)} fusion(bf16[2048,2816]{1,0:T(8,128)(2,1)} %all-gather.12.cloned.1.call-done, bf16[1024,1408]{1,0:T(8,128)(2,1)} %get-tuple-element.58, bf16[1024,1408]{1,0:T(8,128)(2,1)} %get-tuple-element.57), kind=kOutput, calls=%fused_computation.12 | convolution fusion | flops 11824791552 | bytes 21495808 | tf_op jit(solution)/shard_map/dot_general | solution.py:366
  417.5 19.9 %collective-permute-done.20 = bf16[512,1024]{1,0:T(8,128)(2,1)S(1)} collective-permute-done((bf16[512,1024]{1,0:T(8,128)(2,1)S(1)}, bf16[512,1024]{1,0:T(8,128)(2,1)S(1)}, u32[]{:S(2)}, u32[]{:S(2)}) %collective-permute-start.20) | collective-permute-done | bytes 1048608 | tf_op jit(solution)/shard_map/ppermute | solution.py:370
  439.5 20.3 %collective-permute-done.22 = bf16[512,1024]{1,0:T(8,128)(2,1)S(1)} collective-permute-done((bf16[512,1024]{1,0:T(8,128)(2,1)S(1)}, bf16[512,1024]{1,0:T(8,128)(2,1)S(1)}, u32[]{:S(2)}, u32[]{:S(2)}) %collective-permute-start.22) | collective-permute-done | bytes 1048608 | tf_op jit(solution)/shard_map/ppermute | solution.py:370
  460.0 11.0 %collective-permute-done.13 = bf16[256,1024]{1,0:T(8,128)(2,1)S(1)} collective-permute-done((bf16[256,1024]{1,0:T(8,128)(2,1)S(1)}, bf16[256,1024]{1,0:T(8,128)(2,1)S(1)}, u32[]{:S(2)}, u32[]{:S(2)}) %collective-permute-start.13) | collective-permute-done | bytes 524320 | tf_op jit(solution)/shard_map/ppermute | solution.py:370
  500.9 20.0 %collective-permute-done.25 = bf16[256,2048]{1,0:T(8,128)(2,1)S(1)} collective-permute-done((bf16[256,2048]{1,0:T(8,128)(2,1)S(1)}, bf16[256,2048]{1,0:T(8,128)(2,1)S(1)}, u32[]{:S(2)}, u32[]{:S(2)}) %collective-permute-start.25) | collective-permute-done | bytes 1048608 | tf_op jit(solution)/shard_map/ppermute | solution.py:370
  545.9 60.3 %core_backward.1 = (bf16[1024,2048]{1,0:T(8,128)(2,1)S(1)}, bf16[1024,1024]{1,0:T(8,128)(2,1)S(1)}, f32[1024,8]{1,0:T(8,128)S(1)}, f32[4,2048]{1,0:T(4,128)S(1)}...) custom-call(f32[1024,1024]{1,0:T(8,128)} %fusion.30.gz, f32[1024,2048]{1,0:T(8,128)} %fusion.40.pqkv, f32[1024,1024]{1,0:T(8,128)} %fusion.39.po, ...), custom_call_target="tpu_custom_call" | custom-call | flops 20000000000 | bytes 50331648 | tf_op jit(solution)/shard_map/core_backward/pallas_call | solution.py:340
  638.4 14.0 %convolution_convert_fusion.2 = bf16[2048,2048]{1,0:T(8,128)(2,1)} fusion(bf16[1024,2048]{1,0:T(8,128)(2,1)} %copy-done.9, bf16[256,2048]{1,0:T(8,128)(2,1)} %copy-done.23, bf16[256,2048]{1,0:T(8,128)(2,1)} %copy-done.25, bf16[256,2048]{1,0:T(8,128)(2,1)} %copy-done.27, bf16[256,2048]{1,0:T(8,128)(2,1)} %copy-done.21), kind=kOutput, calls=%fused_computation.3 | convolution fusion | flops 8610906112 | bytes 16777216 | tf_op jit(solution)/shard_map/dot_general | solution.py:366
  652.7 18.4 %convolution_convert_fusion = bf16[2048,2816]{1,0:T(8,128)(2,1)} fusion(bf16[1024,2048]{1,0:T(8,128)(2,1)} %constant_dynamic-update-slice_fusion.5, bf16[1024,1408]{1,0:T(8,128)(2,1)} %get-tuple-element.58, bf16[1024,1408]{1,0:T(8,128)(2,1)} %get-tuple-element.57), kind=kOutput, calls=%fused_computation | convolution fusion | flops 11828461568 | bytes 21495808 | tf_op jit(solution)/shard_map/dot_general | solution.py:366
  677.8 11.6 %fusion.52 = f32[1024,2048]{1,0:T(8,128)S(1)} fusion(bf16[1024,2048]{1,0:T(8,128)(2,1)S(1)} %copy-done.10, bf16[2048,2048]{1,0:T(8,128)(2,1)} %all-gather.6.cloned.1.call-done), kind=kOutput, calls=%fused_computation.155 | convolution fusion | flops 8589934592 | bytes 20971520 | tf_op jit(solution)/shard_map/dot_general | solution.py:366
  693.3 20.4 %collective-permute-done.28 = bf16[512,1024]{1,0:T(8,128)(2,1)S(1)} collective-permute-done((bf16[512,1024]{1,0:T(8,128)(2,1)S(1)}, bf16[512,1024]{1,0:T(8,128)(2,1)S(1)}, u32[]{:S(2)}, u32[]{:S(2)}) %collective-permute-start.28) | collective-permute-done | bytes 1048608 | tf_op jit(solution)/shard_map/ppermute | solution.py:370
  740.7 38.2 %psum.7 = f32[4384]{0:T(1024)S(1)} all-reduce(f32[4384]{0:T(1024)S(1)} %concatenate.127), channel_id=1, replica_groups=mesh['dp'=8,'tensor'=4] {'dp','tensor'}, use_global_device_ids=true, to_apply=%region_6.7 | all-reduce | flops 4384 | bytes 35072 | tf_op jit(solution)/shard_map/psum | solution.py:526
  788.6 15.2 %reduce-scatter.11.cloned.1.call-done = bf16[256,1024]{1,0:T(8,128)(2,1)} async-done(((bf16[2048,1024]{1,0:T(8,128)(2,1)}), bf16[256,1024]{1,0:T(8,128)(2,1)}) %reduce-scatter.11.cloned.1.call-update) | async-done | bytes 524304 | tf_op jit(solution)/shard_map/reduce_scatter | solution.py:421
  806.0 88.2 %reduce-scatter.7.cloned.1.call-done = bf16[256,2048]{1,0:T(8,128)(2,1)} async-done(((bf16[2048,2048]{1,0:T(8,128)(2,1)}), bf16[256,2048]{1,0:T(8,128)(2,1)}) %reduce-scatter.7.cloned.1.call-update) | async-done | bytes 1048592 | tf_op jit(solution)/shard_map/reduce_scatter | solution.py:421
  898.4 115.9 %reduce-scatter.15.cloned.1.call-done = bf16[256,2816]{1,0:T(8,128)(2,1)} async-done(((bf16[2048,2816]{1,0:T(8,128)(2,1)}), bf16[256,2816]{1,0:T(8,128)(2,1)}) %reduce-scatter.15.cloned.1.call-update) | async-done | bytes 1441808 | tf_op jit(solution)/shard_map/reduce_scatter | solution.py:421
  (325 shorter events, 306.6 us)
Async XLA Ops:
  7.2 60.0 %all-gather.8.cloned.1.call-start = ((), (), s32[]{:S(2)}) async-start(), calls=%async_computation.7 | async-start | bytes 4718592 | tf_op jit(solution)/shard_map/all_gather | solution.py:417
  9.5 134.1 %all-gather.6.cloned.1.call-start = ((), (), s32[]{:S(2)}) async-start(), calls=%async_computation.6 | async-start | bytes 9437184 | tf_op jit(solution)/shard_map/all_gather | solution.py:417
  13.2 192.7 %all-gather.10.cloned.1.call-start = ((), (), s32[]{:S(2)}) async-start(), calls=%async_computation.8 | async-start | bytes 4718592 | tf_op jit(solution)/shard_map/all_gather | solution.py:417
  14.1 321.5 %all-gather.12.cloned.1.call-start = ((), (), s32[]{:S(2)}) async-start(), calls=%async_computation.9 | async-start | bytes 12976128 | tf_op jit(solution)/shard_map/all_gather | solution.py:417
  17.1 344.1 %all-gather.14.cloned.1.call-start = ((), (), s32[]{:S(2)}) async-start(), calls=%async_computation.10 | async-start | bytes 6488064 | tf_op jit(solution)/shard_map/all_gather | solution.py:417
  18.7 26.1 %collective-permute-start.1 = (bf16[256,2048]{1,0:T(8,128)(2,1)S(1)}, bf16[256,2048]{1,0:T(8,128)(2,1)S(1)}, u32[]{:S(2)}, u32[]{:S(2)}) collective-permute-start(bf16[256,2048]{1,0:T(8,128)(2,1)S(1)} %get-tuple-element.56), channel_id=1, source_target_pairs={{0,2},{1,3},{2,0},{3,1},{4,6},{5,7},{6,4},{7,5},{8,10},{9,11},{10,... | collective-permute-start | bytes 3145736 | tf_op jit(solution)/shard_map/ppermute | solution.py:370
  25.5 690.0 %reduce-scatter.9.cloned.1.call-start = ((), (), s32[]{:S(2)}) async-start(), calls=%async_computation.12 | async-start | bytes 147456 | tf_op jit(solution)/shard_map/reduce_scatter | solution.py:519
  215.5 25.9 %collective-permute-start.6 = (bf16[512,1024]{1,0:T(8,128)(2,1)S(1)}, bf16[512,1024]{1,0:T(8,128)(2,1)S(1)}, u32[]{:S(2)}, u32[]{:S(2)}) collective-permute-start(bf16[512,1024]{1,0:T(8,128)(2,1)S(1)} %pad_maximum_fusion.10), channel_id=1, source_target_pairs={{0,2},{1,3},{2,0},{3,1},{4,6},{5,7},{6,4},{7,5},{8,10},{9,11},{10,... | collective-permute-start | bytes 3145736 | tf_op jit(solution)/shard_map/ppermute | solution.py:370
  255.3 35.8 %collective-permute-start.16 = (bf16[256,2048]{1,0:T(8,128)(2,1)S(1)}, bf16[256,2048]{1,0:T(8,128)(2,1)S(1)}, u32[]{:S(2)}, u32[]{:S(2)}) collective-permute-start(bf16[256,2048]{1,0:T(8,128)(2,1)S(1)} %copy-done.17), channel_id=1, source_target_pairs={{0,1},{1,0},{2,3},{3,2},{4,5},{5,4},{6,7},{7,6},{8,9},{9,8},{10,11... | collective-permute-start | bytes 3145736 | tf_op jit(solution)/shard_map/ppermute | solution.py:370
  255.8 26.1 %collective-permute-start.17 = (bf16[256,2048]{1,0:T(8,128)(2,1)S(1)}, bf16[256,2048]{1,0:T(8,128)(2,1)S(1)}, u32[]{:S(2)}, u32[]{:S(2)}) collective-permute-start(bf16[256,2048]{1,0:T(8,128)(2,1)S(1)} %copy-done.17), channel_id=1, source_target_pairs={{0,2},{1,3},{2,0},{3,1},{4,6},{5,7},{6,4},{7,5},{8,10},{9,11},{10,... | collective-permute-start | bytes 3145736 | tf_op jit(solution)/shard_map/ppermute | solution.py:370
  270.5 33.9 %collective-permute-start.9 = (bf16[256,2048]{1,0:T(8,128)(2,1)S(1)}, bf16[256,2048]{1,0:T(8,128)(2,1)S(1)}, u32[]{:S(2)}, u32[]{:S(2)}) collective-permute-start(bf16[256,2048]{1,0:T(8,128)(2,1)S(1)} %get-tuple-element.52), channel_id=1, source_target_pairs={{0,2},{1,3},{2,0},{3,1},{4,6},{5,7},{6,4},{7,5},{8,10},{9,11},{10,... | collective-permute-start | bytes 3145736 | tf_op jit(solution)/shard_map/ppermute | solution.py:370
  283.5 41.3 %collective-permute-start.8 = (bf16[256,2048]{1,0:T(8,128)(2,1)S(1)}, bf16[256,2048]{1,0:T(8,128)(2,1)S(1)}, u32[]{:S(2)}, u32[]{:S(2)}) collective-permute-start(bf16[256,2048]{1,0:T(8,128)(2,1)S(1)} %get-tuple-element.52), channel_id=1, source_target_pairs={{0,1},{1,0},{2,3},{3,2},{4,5},{5,4},{6,7},{7,6},{8,9},{9,8},{10,11... | collective-permute-start | bytes 3145736 | tf_op jit(solution)/shard_map/ppermute | solution.py:370
  304.4 29.4 %collective-permute-start.10 = (bf16[128,2048]{1,0:T(8,128)(2,1)S(1)}, bf16[128,2048]{1,0:T(8,128)(2,1)S(1)}, u32[]{:S(2)}, u32[]{:S(2)}) collective-permute-start(bf16[128,2048]{1,0:T(8,128)(2,1)S(1)} %slice.328), channel_id=1, source_target_pairs={{0,1},{1,0},{2,3},{3,2},{4,5},{5,4},{6,7},{7,6},{8,9},{9,8},{10,11... | collective-permute-start | bytes 1572872 | tf_op jit(solution)/shard_map/ppermute | solution.py:370
  389.3 26.2 %collective-permute-start.12 = (bf16[512,1024]{1,0:T(8,128)(2,1)}, bf16[512,1024]{1,0:T(8,128)(2,1)S(1)}, u32[]{:S(2)}, u32[]{:S(2)}) collective-permute-start(bf16[512,1024]{1,0:T(8,128)(2,1)} %pad_maximum_fusion.11), channel_id=1, source_target_pairs={{0,1},{1,0},{2,3},{3,2},{4,5},{5,4},{6,7},{7,6},{8,9},{9,8},{10,11... | collective-permute-start | bytes 3145736 | tf_op jit(solution)/shard_map/ppermute | solution.py:370
  410.4 26.9 %collective-permute-start.20 = (bf16[512,1024]{1,0:T(8,128)(2,1)S(1)}, bf16[512,1024]{1,0:T(8,128)(2,1)S(1)}, u32[]{:S(2)}, u32[]{:S(2)}) collective-permute-start(bf16[512,1024]{1,0:T(8,128)(2,1)S(1)} %pad_maximum_fusion.12), channel_id=1, source_target_pairs={{0,1},{1,0},{2,3},{3,2},{4,5},{5,4},{6,7},{7,6},{8,9},{9,8},{10,11... | collective-permute-start | bytes 3145736 | tf_op jit(solution)/shard_map/ppermute | solution.py:370
  411.2 28.1 %collective-permute-start.14 = (bf16[512,1024]{1,0:T(8,128)(2,1)S(1)}, bf16[512,1024]{1,0:T(8,128)(2,1)S(1)}, u32[]{:S(2)}, u32[]{:S(2)}) collective-permute-start(bf16[512,1024]{1,0:T(8,128)(2,1)S(1)} %concatenate.130), channel_id=1, source_target_pairs={{0,2},{1,3},{2,0},{3,1},{4,6},{5,7},{6,4},{7,5},{8,10},{9,11},{10,... | collective-permute-start | bytes 3145736 | tf_op jit(solution)/shard_map/ppermute | solution.py:370
  412.8 47.0 %collective-permute-start.22 = (bf16[512,1024]{1,0:T(8,128)(2,1)S(1)}, bf16[512,1024]{1,0:T(8,128)(2,1)S(1)}, u32[]{:S(2)}, u32[]{:S(2)}) collective-permute-start(bf16[512,1024]{1,0:T(8,128)(2,1)S(1)} %concatenate.131), channel_id=1, source_target_pairs={{0,2},{1,3},{2,0},{3,1},{4,6},{5,7},{6,4},{7,5},{8,10},{9,11},{10,... | collective-permute-start | bytes 3145736 | tf_op jit(solution)/shard_map/ppermute | solution.py:370
  415.9 55.1 %collective-permute-start.13 = (bf16[256,1024]{1,0:T(8,128)(2,1)S(1)}, bf16[256,1024]{1,0:T(8,128)(2,1)S(1)}, u32[]{:S(2)}, u32[]{:S(2)}) collective-permute-start(bf16[256,1024]{1,0:T(8,128)(2,1)S(1)} %fusion.24), channel_id=1, source_target_pairs={{0,2},{1,3},{2,0},{3,1},{4,6},{5,7},{6,4},{7,5},{8,10},{9,11},{10,... | collective-permute-start | bytes 1572872 | tf_op jit(solution)/shard_map/ppermute | solution.py:370
  437.7 43.2 %collective-permute-start.21 = (bf16[256,1024]{1,0:T(8,128)(2,1)S(1)}, bf16[256,1024]{1,0:T(8,128)(2,1)S(1)}, u32[]{:S(2)}, u32[]{:S(2)}) collective-permute-start(bf16[256,1024]{1,0:T(8,128)(2,1)S(1)} %fusion.20), channel_id=1, source_target_pairs={{0,2},{1,3},{2,0},{3,1},{4,6},{5,7},{6,4},{7,5},{8,10},{9,11},{10,... | collective-permute-start | bytes 1572872 | tf_op jit(solution)/shard_map/ppermute | solution.py:370
  609.1 175.1 %reduce-scatter.17.cloned.1.call-start = ((), (), s32[]{:S(2)}) async-start(), calls=%async_computation.16 | async-start | bytes 6488064 | tf_op jit(solution)/shard_map/reduce_scatter | solution.py:421
  619.6 166.9 %reduce-scatter.13.cloned.1.call-start = ((), (), s32[]{:S(2)}) async-start(), calls=%async_computation.14 | async-start | bytes 4718592 | tf_op jit(solution)/shard_map/reduce_scatter | solution.py:421
  629.1 174.8 %reduce-scatter.11.cloned.1.call-start = ((), (), s32[]{:S(2)}) async-start(), calls=%async_computation.13 | async-start | bytes 4718592 | tf_op jit(solution)/shard_map/reduce_scatter | solution.py:421
  638.4 255.8 %reduce-scatter.7.cloned.1.call-start = ((), (), s32[]{:S(2)}) async-start(), calls=%async_computation.11 | async-start | bytes 9437184 | tf_op jit(solution)/shard_map/reduce_scatter | solution.py:421
  652.5 361.8 %reduce-scatter.15.cloned.1.call-start = ((), (), s32[]{:S(2)}) async-start(), calls=%async_computation.15 | async-start | bytes 12976128 | tf_op jit(solution)/shard_map/reduce_scatter | solution.py:421
  (72 other events, 1265.7 us)
Sparse Core Ops, SparseCore 0:
  10.2 50.2 all-gather.7
  62.7 80.8 all-gather.5
  145.2 46.3 all-gather.9
  193.6 106.2 all-gather.11
  302.0 59.1 all-gather.13
  609.2 27.3 reduce-scatter.8
  639.0 63.0 reduce-scatter.16
  704.5 48.3 reduce-scatter.12
  755.3 48.4 reduce-scatter.10
  806.1 88.0 reduce-scatter.6
  896.6 117.6 reduce-scatter.14

commit v2 on v1

--- a/solution.py
+++ b/solution.py
@@ -77,12 +77,12 @@
 
 
 def forward_kernel(
-    pqkv, po, pab, taps, rate, bias, gain,
-    mixed, conved, o_out, u_out, s_out, t_out,
+    pqkv, pab, taps, rate, bias,
+    n_out, norm_out, conved, u_out, s_out, t_out,
     ext, state,
 ):
     heads = rate.shape[1]
-    vals = po.shape[1]
+    vals = n_out.shape[1]
     keys = (pqkv.shape[1] - vals) // 2
     dk, dv = keys // heads, vals // heads
 
@@ -146,16 +146,14 @@
         s_out[0, h] = lows[h]
         u_out[:, cols] = us[h]
         o = outs[h]
-        o_out[:, cols] = o.astype(o_out.dtype)
-        n = o * lax.rsqrt(jnp.mean(o * o, -1, keepdims=True) + 1e-5)
-        gate = po[:, cols]
-        mixed[:, cols] = (n * gain[...] * (gate * sigmoid(gate))).astype(mixed.dtype)
-
-
-def core_forward(pqkv, po, pab, taps, rate, bias, gain):
+        norm = lax.rsqrt(jnp.mean(o * o, -1, keepdims=True) + 1e-5)
+        n_out[:, cols] = (o * norm).astype(n_out.dtype)
+        norm_out[:, h : h + 1] = norm
+
+
+def core_forward(pqkv, pab, taps, rate, bias, keys):
     rows, width = pqkv.shape
-    vals = po.shape[1]
-    keys = (width - vals) // 2
+    vals = width - 2 * keys
     heads = rate.shape[1]
     dk, dv = keys // heads, vals // heads
     blocks = rows // GROUP
@@ -164,19 +162,19 @@
     return pl.pallas_call(
         forward_kernel,
         grid=(blocks,),
-        in_specs=[tokens(a.shape[1]) for a in (pqkv, po, pab)] + [fixed(a) for a in (taps, rate, bias, gain)],
+        in_specs=[tokens(a.shape[1]) for a in (pqkv, pab)] + [fixed(a) for a in (taps, rate, bias)],
         out_specs=[
             tokens(vals),
-            tokens(2 * keys + vals),
-            tokens(vals),
+            tokens(heads),
+            tokens(width),
             tokens(vals),
             pl.BlockSpec((1, heads, dk, dv), lambda n: (n, 0, 0, 0)),
             pl.BlockSpec((1, heads, GROUP, GROUP), lambda n: (n, 0, 0, 0)),
         ],
         out_shape=[
             jax.ShapeDtypeStruct((rows, vals), BF16),
-            jax.ShapeDtypeStruct((rows, 2 * keys + vals), F32),
-            jax.ShapeDtypeStruct((rows, vals), BF16),
+            jax.ShapeDtypeStruct((rows, heads), F32),
+            jax.ShapeDtypeStruct((rows, width), F32),
             jax.ShapeDtypeStruct((rows, vals), BF16),
             jax.ShapeDtypeStruct((blocks, heads, dk, dv), BF16),
             jax.ShapeDtypeStruct((blocks, heads, GROUP, GROUP), BF16),
@@ -188,16 +186,16 @@
         compiler_params=pltpu.CompilerParams(dimension_semantics=("arbitrary",), vmem_limit_bytes=40 * 2**20),
         cost_estimate=pl.CostEstimate(flops=8 * 10**9, bytes_accessed=32 * 2**20, transcendentals=10**7),
         name="core_forward",
-    )(pqkv, po, pab, taps, rate, bias, gain)
+    )(pqkv, pab, taps, rate, bias)
 
 
 def backward_kernel(
-    gz, pqkv, po, pab, conved, o_in, u_in, s_in, t_in, taps, rate, bias, gain,
-    dpqkv, dpo, dpab, dtaps, dsmall, dgain,
+    dn_in, pqkv, pab, n_in, norm_in, conved, u_in, s_in, t_in, taps, rate, bias,
+    dpqkv, dpab, dtaps, dsmall, dgain,
     ext, dstate,
 ):
     heads = rate.shape[1]
-    vals = po.shape[1]
+    vals = dn_in.shape[1]
     keys = (pqkv.shape[1] - vals) // 2
     dk, dv = keys // heads, vals // heads
 
@@ -244,18 +242,11 @@
         kb = k.astype(BF16)
         qb = qs.astype(BF16)
 
-        o = o_in[:, vs].astype(F32)
-        o_norm = lax.rsqrt(jnp.mean(o * o, -1, keepdims=True) + 1e-5)
-        n = o * o_norm
-        gate = po[:, vs]
-        sg = sigmoid(gate)
-        g = gz[:, vs]
-        gn = g * n
-        act = gate * sg
-        gain_sum = gain_sum + jnp.sum(gn * act, 0, keepdims=True)
-        dpo[:, vs] = (gn * gain[...] * (sg * (1.0 + gate * (1.0 - sg)))).astype(dpo.dtype)
-        dn = g * gain[...] * act
-        do = o_norm * (dn - n * jnp.mean(dn * n, -1, keepdims=True))
+        n = n_in[:, vs].astype(F32)
+        dn = dn_in[:, vs]
+        dnn = dn * n
+        gain_sum = gain_sum + jnp.sum(dnn, 0, keepdims=True)
+        do = norm_in[:, h : h + 1] * (dn - n * jnp.mean(dnn, -1, keepdims=True))
 
         prod = mm(jnp.concatenate([kb, qb], 0), kb, NT)
         relative = jnp.where(row >= col, jnp.exp(jnp.minimum(c_col[:, h : h + 1] - c_row[h : h + 1, :], 0.0)), 0.0)
@@ -325,10 +316,10 @@
     ext[GROUP:, :] = ext[:TAIL, :]
 
 
-def core_backward(gz, pqkv, po, pab, kept, taps, rate, bias, gain):
-    conved, o_in, u_in, s_in, t_in = kept
+def core_backward(dn, pqkv, pab, kept, taps, rate, bias):
+    n_in, norm_in, conved, u_in, s_in, t_in = kept
     rows, width = pqkv.shape
-    vals = po.shape[1]
+    vals = dn.shape[1]
     keys = (width - vals) // 2
     heads = rate.shape[1]
     dk, dv = keys // heads, vals // heads
@@ -340,14 +331,13 @@
     return pl.pallas_call(
         backward_kernel,
         grid=(blocks,),
-        in_specs=[tokens(a.shape[1]) for a in (gz, pqkv, po, pab, conved, o_in, u_in)]
+        in_specs=[tokens(a.shape[1]) for a in (dn, pqkv, pab, n_in, norm_in, conved, u_in)]
         + [stacked(s_in), stacked(t_in)]
-        + [fixed(a.shape) for a in (taps, rate, bias, gain)],
-        out_specs=[tokens(a.shape[1]) for a in (pqkv, po, pab)]
-        + [fixed(taps.shape), fixed(small), fixed(gain.shape)],
-        out_shape=[jax.ShapeDtypeStruct(a.shape, BF16) for a in (pqkv, po)]
-        + [jax.ShapeDtypeStruct(pab.shape, F32)]
-        + [jax.ShapeDtypeStruct(s, F32) for s in (taps.shape, small, gain.shape)],
+        + [fixed(a.shape) for a in (taps, rate, bias)],
+        out_specs=[tokens(a.shape[1]) for a in (pqkv, pab)]
+        + [fixed(taps.shape), fixed(small), fixed((1, dv))],
+        out_shape=[jax.ShapeDtypeStruct(pqkv.shape, BF16), jax.ShapeDtypeStruct(pab.shape, F32)]
+        + [jax.ShapeDtypeStruct(s, F32) for s in (taps.shape, small, (1, dv))],
         scratch_shapes=[
             pltpu.VMEM((GROUP + TAIL, 2 * keys + vals), F32),
             pltpu.VMEM((heads, dk, dv), F32),
@@ -355,7 +345,7 @@
         compiler_params=pltpu.CompilerParams(dimension_semantics=("arbitrary",), vmem_limit_bytes=40 * 2**20),
         cost_estimate=pl.CostEstimate(flops=20 * 10**9, bytes_accessed=48 * 2**20, transcendentals=10**7),
         name="core_backward",
-    )(gz, pqkv, po, pab, conved, o_in, u_in, s_in, t_in, taps, rate, bias, gain)
+    )(dn, pqkv, pab, n_in, norm_in, conved, u_in, s_in, t_in, taps, rate, bias)
 
 
 def rms_norm(values, gain_vec):
@@ -378,21 +368,41 @@
     return jnp.concatenate([own, first, second, swap(second[:half], 1), swap(first[half:], 2)], 0)
 
 
-def scatter_rows(part):
+def scatter_rows(part, beside=None):
     if lax.axis_size("tensor") != 4:
-        return lax.psum_scatter(part, "tensor", scatter_dimension=0, tiled=True).astype(F32)
+        total = lax.psum_scatter(part, "tensor", scatter_dimension=0, tiled=True).astype(F32)
+        return total if beside is None else (total, beside)
     rows, half = part.shape[0] // 4, part.shape[1] // 2
 
     def chunk(k, columns):
         return part[k * rows : (k + 1) * rows, columns]
 
-    sums = []
-    for columns, one, two in ((slice(0, half), 1, 2), (slice(half, 2 * half), 2, 1)):
-        got = swap(jnp.concatenate([chunk(one, columns), chunk(3, columns)], 0), one).astype(F32)
-        own = chunk(0, columns).astype(F32) + got[:rows]
-        passed = (chunk(two, columns).astype(F32) + got[rows:]).astype(BF16)
-        sums.append(own + swap(passed, two).astype(F32))
-    return jnp.concatenate(sums, 1)
+    plans = ((slice(0, half), 1, 2), (slice(half, 2 * half), 2, 1))
+    arrived = [swap(jnp.concatenate([chunk(one, columns), chunk(3, columns)], 0), one) for columns, one, _ in plans]
+    if beside is not None:
+        arrived, beside = lax.optimization_barrier((arrived, beside))
+    owns, passed = [], []
+    for (columns, _, two), got in zip(plans, arrived):
+        got = got.astype(F32)
+        owns.append(chunk(0, columns).astype(F32) + got[:rows])
+        passed.append((chunk(two, columns).astype(F32) + got[rows:]).astype(BF16))
+    passed = lax.optimization_barrier(passed)
+    sums = [own + swap(piece, two).astype(F32) for own, piece, (_, _, two) in zip(owns, passed, plans)]
+    total = jnp.concatenate(sums, 1)
+    return total if beside is None else (total, beside)
+
+
+def sum_everywhere(values):
+    for axis in ("dp", "tensor"):
+        size = lax.axis_size(axis)
+        if size & (size - 1):
+            values = lax.psum(values, axis)
+            continue
+        mask = 1
+        while mask < size:
+            values = values + lax.ppermute(values, axis, [(i, i ^ mask) for i in range(size)])
+            mask *= 2
+    return values
 
 
 def reorder(rows_in):
@@ -418,7 +428,7 @@
 
 
 def scatter_dp(part, axis):
-    return lax.psum_scatter(part.astype(BF16), "dp", scatter_dimension=axis, tiled=True).astype(F32)
+    return lax.psum_scatter(part, "dp", scatter_dimension=axis, tiled=True)
 
 
 def local(
@@ -450,7 +460,7 @@
     first_head = lax.axis_index("tensor") * heads
     rate = lax.dynamic_slice_in_dim(log_rate, first_head, heads)[None]
     bias = lax.dynamic_slice_in_dim(decay_bias, first_head, heads)[None]
-    gain = head_gain[None]
+    gain = jnp.tile(head_gain, heads)
 
     narrow = jnp.concatenate([w_decay, w_beta], 1).T
     kernels = jnp.concatenate([conv_query, conv_key, conv_value], 1)
@@ -466,44 +476,58 @@
     ).astype(F32)
 
     full_qkv = gather_dp(jnp.concatenate([w_query, w_key, w_value], 1), 0)
-    full_outgate = gather_dp(w_outgate, 0)
-    full_output = gather_dp(w_output, 1)
+    full_gate_out = gather_dp(jnp.concatenate([w_outgate, w_output.T], 1), 0)
+    full_outgate, full_output = full_gate_out[:, :vals], full_gate_out[:, vals:]
     full_pair = gather_dp(jnp.concatenate([w_gate, w_up], 1), 0)
     full_down = gather_dp(w_down, 1)
 
+    hold = lax.optimization_barrier
     rows_in = hidden_in.astype(F32)
     normed = reorder(gather_rows(rms_norm(rows_in, mix_gain).astype(BF16)))
+    cot_own, _ = hold((grad_out, normed))
+    cot = gather_rows(cot_own)
     pqkv = dot(normed, full_qkv)
     pab = dot(normed, full_narrow, NT)
+    pqkv, cot = hold((pqkv, cot))
+    kept = core_forward(pqkv, pab, taps, rate, bias, keys)
     po = dot(normed, full_outgate)
-    mixed, *kept = core_forward(pqkv, po, pab, taps, rate, bias, gain)
-    middle = rows_in + scatter_rows(reorder(dot(mixed, full_output).astype(BF16)))
+    po_sig = jax.nn.sigmoid(po)
+    mixed = (kept[0].astype(F32) * gain * (po * po_sig)).astype(BF16)
+    middle = rows_in + scatter_rows(reorder(dot(mixed, full_output, NT).astype(BF16)))
 
     ffn_rows = gather_rows(rms_norm(middle, ffn_gain).astype(BF16))
     pre = dot(ffn_rows, full_pair)
     gate_pre, up_pre = pre[:, :hidden], pre[:, hidden:]
     gate_sig = jax.nn.sigmoid(gate_pre)
     activ = (gate_pre * gate_sig * up_pre).astype(BF16)
-    cot = gather_rows(grad_out)
-    grad_w_down = scatter_dp(dot(activ, cot, TN), 1)
-    hidden_out = (middle + scatter_rows(dot(activ, full_down).astype(BF16))).astype(BF16)
+    cot, part_down = hold((cot, dot(activ, cot, TN).astype(BF16)))
+    grad_w_down = scatter_dp(part_down, 1)
     grad_activ = dot(cot, full_down, NT)
     grad_gate_pre = (grad_activ * up_pre * gate_sig * (1.0 + gate_pre * (1.0 - gate_sig))).astype(BF16)
     grad_up_pre = (grad_activ * (gate_pre * gate_sig)).astype(BF16)
     grad_pre = jnp.concatenate([grad_gate_pre, grad_up_pre], 1)
-    grad_pair = scatter_dp(dot(ffn_rows, grad_pre, TN), 0)
-    grad_ffn_norm = scatter_rows(dot(grad_pre, full_pair, NT).astype(BF16))
+    grad_ffn_norm, part_pair = scatter_rows(
+        dot(grad_pre, full_pair, NT).astype(BF16), dot(ffn_rows, grad_pre, TN).astype(BF16)
+    )
+    grad_pair = scatter_dp(part_pair, 0)
     grad_middle_norm, ffn_gain_part = norm_back(middle, ffn_gain, grad_ffn_norm)
     grad_middle = grad_out.astype(F32) + grad_middle_norm
 
     mix_cot = reorder(gather_rows(grad_middle.astype(BF16)))
-    grad_mixed = dot(mix_cot, full_output, NT)
-    grad_w_output = scatter_dp(dot(mixed, mix_cot, TN), 1)
-    grad_pqkv, grad_po, grad_pab, grad_taps, grad_small, grad_gain = core_backward(
-        grad_mixed, pqkv, po, pab, kept, taps, rate, bias, gain
-    )
-    grad_w_outgate = scatter_dp(dot(normed, grad_po, TN), 0)
-    grad_qkv = scatter_dp(dot(normed, grad_pqkv, TN), 0)
+    grad_mixed = dot(mix_cot, full_output)
+    grad_po = grad_mixed * kept[0].astype(F32) * gain * (po_sig * (1.0 + po * (1.0 - po_sig)))
+    grad_po = grad_po.astype(BF16)
+    grad_n = grad_mixed * gain * (po * po_sig)
+    part_gate_out = jnp.concatenate([dot(normed, grad_po, TN), dot(mix_cot, mixed, TN)], 1).astype(BF16)
+    grad_n, activ_late, grad_w_down, part_gate_out = hold((grad_n, activ, grad_w_down, part_gate_out))
+    grad_gate_out = scatter_dp(part_gate_out, 0)
+    out_part = dot(activ_late, full_down).astype(BF16)
+    grad_n, out_part = hold((grad_n, out_part))
+    hidden_out = (middle + scatter_rows(out_part)).astype(BF16)
+    grad_pqkv, grad_pab, grad_taps, grad_small, grad_gain = core_backward(grad_n, pqkv, pab, kept, taps, rate, bias)
+    grad_pqkv, grad_pair = hold((grad_pqkv, grad_pair))
+    grad_pqkv, part_qkv = hold((grad_pqkv, dot(normed, grad_pqkv, TN).astype(BF16)))
+    grad_qkv = scatter_dp(part_qkv, 0)
     low_pab = grad_pab.astype(BF16)
     grad_normed = dot(grad_pqkv, full_qkv, NT) + dot(grad_po, full_outgate, NT) + dot(low_pab, full_narrow)
     grad_mix_norm = scatter_rows(reorder(grad_normed.astype(BF16)))
@@ -516,27 +540,26 @@
         [roll(grad_taps[:, :keys]), roll(grad_taps[:, keys : 2 * keys]), roll(grad_taps[:, 2 * keys :])], 2
     )
     pad3 = lambda a: jnp.pad(a, ((0, 0), (0, 0), (0, wide - a.shape[2])))
-    few_grads = lax.psum_scatter(
-        jnp.concatenate([pad3(roll(grad_narrow)), pad3(grad_kernels)], 1), "dp", scatter_dimension=0, tiled=False
-    )
+    few_parts = jnp.concatenate([pad3(roll(grad_narrow)), pad3(grad_kernels)], 1)
+    few_grads = jnp.sum(lax.all_to_all(few_parts, "dp", 0, 0, tiled=True), 0)
     grad_narrow = few_grads[: 2 * heads, : narrow.shape[1]].T
     grad_kernels = few_grads[2 * heads :, : kernels.shape[1]]
 
     place = lambda a: lax.dynamic_update_slice_in_dim(jnp.zeros_like(log_rate), a, first_head, 0)
-    sums = lax.psum(
+    sums = sum_everywhere(
         jnp.concatenate(
             [
                 mix_gain_part,
                 ffn_gain_part,
-                grad_gain[0],
+                grad_gain[0] / head_gain,
                 place(grad_small[0, :heads]),
                 place(grad_small[0, heads:]),
             ]
-        ),
-        ("dp", "tensor"),
+        )
     )
     ends = [model, 2 * model, 2 * model + head_gain.shape[0], 2 * model + head_gain.shape[0] + log_rate.shape[0]]
     grad_mix_gain, grad_ffn_gain, grad_head_gain, grad_log_rate, grad_decay_bias = jnp.split(sums, ends)
+    grad_qkv, grad_gate_out, grad_pair = grad_qkv.astype(F32), grad_gate_out.astype(F32), grad_pair.astype(F32)
     return (
         hidden_out,
         grad_in,
@@ -551,13 +574,13 @@
         grad_narrow[:, heads:],
         grad_log_rate,
         grad_decay_bias,
-        grad_w_outgate,
+        grad_gate_out[:, :vals],
         grad_head_gain,
-        grad_w_output,
+        grad_gate_out[:, vals:].T,
         grad_ffn_gain,
         grad_pair[:, :hidden],
         grad_pair[:, hidden:],
-        grad_w_down,
+        grad_w_down.astype(F32),
     )
 
 

time: 1030 us -> 734 us (0.71)
  waiting for transfers between devices: 542 us -> 249 us
  blocking collectives: 52.7 us -> 14.4 us
  other arithmetic: 39.3 us -> 58.5 us
  local copies, waits for them, and re-layouts: 42.5 us -> 56.6 us
    reduce_scatter x6 -> x4, waiting for transfers between devices: 219 us -> 14.7 us  [scatter_dp(): return lax.psum_scatter(part, 'dp', scatter_dimension=axis, tiled=True)]
    ppermute x32, waiting for transfers between devices: 250 us -> 169 us  [swap(): return lax.ppermute(piece, 'tensor', [(i, i ^ mask) for i in range(4)])]
    psum x1 -> x0, blocking collectives: 38.2 us -> none  [local(): lax.psum(jnp.concatenate([mix_gain_part, ffn_gain_part, grad_gain[0], pla...]
    all_gather x5 -> x4, waiting for transfers between devices: 72.7 us -> 47.3 us  [gather_dp(): return lax.all_gather(shard.astype(BF16), 'dp', axis=axis, tiled=True)]
    concatenate x0 -> x4, other arithmetic: none -> 12.2 us  [the longest x1 8.5 us: local(): jnp.concatenate([dot(normed, grad_po, TN), dot(mix_cot, mixed, TN)], 1)]
    ppermute x0 -> x5, waiting for transfers between devices: none -> 11.3 us  [sum_everywhere(): lax.ppermute(values, axis, [(i, i ^ mask) for i in range(size)])]
    unnamed x119 -> x167, local copies, waits for them, and re-layouts: 22 us -> 33 us
  transfers between devices with their start and end apart: 43 -> 46, of which waited for: 29 -> 34; matrix products, arithmetic and copies ran while one was open for 20% -> 38% of each run, Pallas kernels for 4% -> 14%
where the time goes in v2:
time: 734 us; the launch traced here: 730 us
  waiting for transfers between devices  249 us (34%)
  matrix products  189 us (26%)
  Pallas kernels  101 us (14%)
  other arithmetic  58.5 us (8%)
  local copies, waits for them, and re-layouts  56.6 us (8%)
  starting transfers between devices  46.3 us (6%)
  between operations  15.6 us (2%)
  blocking collectives  14.4 us (2%)
    dot_general x18, matrix products, dot(): return lax.dot_general(a, b, (dims, ((), ())), preferred_element_type=F32)  189 us
    ppermute x32, waiting for transfers between devices, swap(): return lax.ppermute(piece, 'tensor', [(i, i ^ mask) for i in range(4)])  169 us
    pallas_call x1, Pallas kernels, core_backward(): pl.pallas_call(backward_kernel, grid=(blocks,), in_specs=[tokens(a.shape[...  58.9 us
    all_gather x4, waiting for transfers between devices, gather_dp(): return lax.all_gather(shard.astype(BF16), 'dp', axis=axis, tiled=True)  47.3 us
    pallas_call x1, Pallas kernels, core_forward(): pl.pallas_call(forward_kernel, grid=(blocks,), in_specs=[tokens(a.shape[1...  42 us
    ppermute x32, starting transfers between devices, swap(): return lax.ppermute(piece, 'tensor', [(i, i ^ mask) for i in range(4)])  40.6 us
    unnamed x167, local copies, waits for them, and re-layouts  33 us
    reduce_scatter x4, waiting for transfers between devices, scatter_dp(): return lax.psum_scatter(part, 'dp', scatter_dimension=axis, tiled=True)  14.7 us
  transfers between devices with their start and end apart: 46, of which 34 were waited for; matrix products, arithmetic and copies ran while one was open for 38% of the time, Pallas kernels for 14%

profile of v2, /device:TPU:0, one launch (start us, length us, event | category | flops | bytes accessed | tf_op | source)
XLA Modules:
  0.0 730.2 jit_solution(10778241507503195489)
XLA Ops:
  23.9 14.4 %all_gather.17 = bf16[8,12,256]{2,1,0:T(8,128)(2,1)S(1)} all-gather(bf16[1,12,256]{2,1,0:T(8,128)(2,1)S(1)} %pad_maximum_fusion.21), channel_id=1, replica_groups=mesh['dp'=8,'tensor'=4] {'dp'}, dimensions={0}, use_global_device_ids=true | all-gather | bytes 55296 | tf_op jit(solution)/shard_map/all_gather | solution.py:469
  74.6 16.8 %collective-permute-done.5 = bf16[256,2048]{1,0:T(8,128)(2,1)S(1)} collective-permute-done((bf16[256,2048]{1,0:T(8,128)(2,1)S(1)}, bf16[256,2048]{1,0:T(8,128)(2,1)S(1)}, u32[]{:S(2)}, u32[]{:S(2)}) %collective-permute-start.5) | collective-permute-done | bytes 1048608 | tf_op jit(solution)/shard_map/ppermute | solution.py:360
  106.5 15.0 %fusion.60.pqkv = f32[1024,2048]{1,0:T(8,128)} fusion(bf16[1024,2048]{1,0:T(8,128)(2,1)} %pad_maximum_fusion.2, bf16[2048,2048]{1,0:T(8,128)(2,1)} %all-gather.5.cloned.1.call-done), kind=kOutput, calls=%fused_computation.171 | convolution fusion | flops 8589934592 | bytes 20971520 | tf_op jit(solution)/shard_map/dot_general | solution.py:356
  121.5 42.0 %core_forward.1 = (bf16[1024,1024]{1,0:T(8,128)(2,1)S(1)}, f32[1024,4]{1,0:T(8,128)S(1)}, f32[1024,2048]{1,0:T(8,128)}, bf16[1024,1024]{1,0:T(8,128)(2,1)S(1)}, ...) custom-call(f32[1024,2048]{1,0:T(8,128)} %fusion.60.pqkv, f32[1024,8]{1,0:T(8,128)S(1)} %fusion.61.pab, ...), custom_call_target="tpu_custom_call" | custom-call | flops 8000000000 | bytes 33554432 | tf_op jit(solution)/shard_map/core_forward/pallas_call | solution.py:162
  168.6 11.9 %all-gather.7.cloned.1.call-done = bf16[2048,2048]{0,1:T(8,128)(2,1)} async-done(((bf16[256,2048]{0,1:T(8,128)(2,1)}), bf16[2048,2048]{0,1:T(8,128)(2,1)}) %all-gather.7.cloned.1.call-update) | async-done | bytes 8388624 | tf_op jit(solution)/shard_map/all_gather | solution.py:427
  180.5 10.7 %fusion.2 = (bf16[1024,1024]{1,0:T(8,128)(2,1)S(1)}, f32[1024,1024]{1,0:T(8,128)}) fusion(bf16[1024,1024]{1,0:T(8,128)(2,1)S(1)} %get-tuple-element.59.n_in, f32[1024]{0:T(1024)S(1)} %bitcast.83, bf16[1024,2048]{1,0:T(8,128)(2,1)} %pad_maximum_fusion.2, bf16[2048,2048]{0,1:T(8,128)(2,1)} %all-gather.7.cloned.1.call-done), kind=kOutput, calls=%fused_computation.14 | convolution fusion | flops 4303355904 | bytes 16781312 | tf_op jit(solution)/shard_map/dot_general | solution.py:356
  199.6 22.2 %collective-permute-done.8 = bf16[512,1024]{1,0:T(8,128)(2,1)S(1)} collective-permute-done((bf16[512,1024]{1,0:T(8,128)(2,1)S(1)}, bf16[512,1024]{1,0:T(8,128)(2,1)S(1)}, u32[]{:S(2)}, u32[]{:S(2)}) %collective-permute-start.8) | collective-permute-done | bytes 1048608 | tf_op jit(solution)/shard_map/ppermute | solution.py:360
  228.3 10.1 %collective-permute-done.10 = bf16[256,1024]{1,0:T(8,128)(2,1)} collective-permute-done((bf16[256,1024]{1,0:T(8,128)(2,1)}, bf16[256,1024]{1,0:T(8,128)(2,1)}, u32[]{:S(2)}, u32[]{:S(2)}) %collective-permute-start.10) | collective-permute-done | bytes 524320 | tf_op jit(solution)/shard_map/ppermute | solution.py:360
  246.0 21.3 %collective-permute-done.13 = bf16[256,2048]{1,0:T(8,128)(2,1)S(1)} collective-permute-done((bf16[256,2048]{1,0:T(8,128)(2,1)S(1)}, bf16[256,2048]{1,0:T(8,128)(2,1)S(1)}, u32[]{:S(2)}, u32[]{:S(2)}) %collective-permute-start.13) | collective-permute-done | bytes 1048608 | tf_op jit(solution)/shard_map/ppermute | solution.py:360
  289.0 17.2 %fusion.62 = f32[1024,2816]{1,0:T(8,128)S(1)} fusion(bf16[1024,2048]{1,0:T(8,128)(2,1)} %constant_dynamic-update-slice_fusion.10, bf16[2048,2816]{1,0:T(8,128)(2,1)} %all-gather.9.cloned.1.call-done), kind=kOutput, calls=%fused_computation.173 | convolution fusion | flops 11811160064 | bytes 27262976 | tf_op jit(solution)/shard_map/dot_general | solution.py:356
  311.9 10.7 %convolution_convert_fusion.2 = bf16[1408,2048]{1,0:T(8,128)(2,1)} fusion(bf16[1024,1408]{1,0:T(8,128)(2,1)S(1)} %multiply_convert_fusion.2, bf16[1024,2048]{1,0:T(8,128)(2,1)} %constant_dynamic-update-slice_fusion.5), kind=kOutput, calls=%fused_computation.4 | convolution fusion | flops 5908463616 | bytes 12845056 | tf_op jit(solution)/shard_map/dot_general | solution.py:356
  322.7 27.4 %all-gather.11.cloned.1.call-done = bf16[1408,2048]{1,0:T(8,128)(2,1)} async-done(((bf16[1408,256]{1,0:T(8,128)(2,1)}), bf16[1408,2048]{1,0:T(8,128)(2,1)}) %all-gather.11.cloned.1.call-update) | async-done | bytes 5767184 | tf_op jit(solution)/shard_map/all_gather | solution.py:427
  350.2 15.7 %multiply_convert_fusion.1 = (bf16[1024,1408]{1,0:T(8,128)(2,1)S(1)}, bf16[1024,1408]{1,0:T(8,128)(2,1)}) fusion(f32[1024,2816]{1,0:T(8,128)} %copy-done.26, bf16[1024,2048]{1,0:T(8,128)(2,1)} %constant_dynamic-update-slice_fusion.5, bf16[1408,2048]{1,0:T(8,128)(2,1)} %all-gather.11.cloned.1.call-done), kind=kOutput, calls=%fused_computation.7 | convolution fusion | flops 5924323328 | bytes 27262976 | tf_op jit(solution)/shard_map/dot_general | solution.py:356
  365.9 16.9 %convolution_convert_fusion.3 = bf16[1024,2048]{1,0:T(8,128)(2,1)S(1)} fusion(bf16[2048,2816]{1,0:T(8,128)(2,1)} %all-gather.9.cloned.1.call-done, bf16[1024,1408]{1,0:T(8,128)(2,1)} %get-tuple-element.148, bf16[1024,1408]{1,0:T(8,128)(2,1)S(1)} %get-tuple-element.147), kind=kOutput, calls=%fused_computation.23 | convolution fusion | flops 11824791552 | bytes 21495808 | tf_op jit(solution)/shard_map/dot_general | solution.py:356
  389.2 17.7 %convolution_convert_fusion = bf16[2048,2816]{1,0:T(8,128)(2,1)} fusion(bf16[1024,2048]{1,0:T(8,128)(2,1)} %constant_dynamic-update-slice_fusion.10, bf16[1024,1408]{1,0:T(8,128)(2,1)} %get-tuple-element.148, bf16[1024,1408]{1,0:T(8,128)(2,1)S(1)} %copy-done.69), kind=kOutput, calls=%fused_computation | convolution fusion | flops 11828461568 | bytes 21495808 | tf_op jit(solution)/shard_map/dot_general | solution.py:356
  418.3 10.9 %collective-permute-done.18 = bf16[256,1024]{1,0:T(8,128)(2,1)S(1)} collective-permute-done((bf16[256,1024]{1,0:T(8,128)(2,1)S(1)}, bf16[256,1024]{1,0:T(8,128)(2,1)S(1)}, u32[]{:S(2)}, u32[]{:S(2)}) %collective-permute-start.18) | collective-permute-done | bytes 524320 | tf_op jit(solution)/shard_map/ppermute | solution.py:360
  435.2 21.9 %collective-permute-done.21 = bf16[256,2048]{1,0:T(8,128)(2,1)S(1)} collective-permute-done((bf16[256,2048]{1,0:T(8,128)(2,1)S(1)}, bf16[256,2048]{1,0:T(8,128)(2,1)S(1)}, u32[]{:S(2)}, u32[]{:S(2)}) %collective-permute-start.21) | collective-permute-done | bytes 1048608 | tf_op jit(solution)/shard_map/ppermute | solution.py:360
  477.0 13.4 %fusion.5 = (bf16[1024,1024]{1,0:T(8,128)(2,1)S(1)}, f32[1024,1024]{1,0:T(8,128)}) fusion(bf16[1024,1024]{1,0:T(8,128)(2,1)S(1)} %get-tuple-element.59.n_in, f32[1024,1024]{1,0:T(8,128)} %get-tuple-element.204, f32[1024]{0:T(1024)S(1)} %bitcast.84, bf16[2048,2048]{0,1:T(8,128)(2,1)} %all-gather.7.cloned.1.call-done, ...), kind=kOutput, calls=%fused_computation.17 | convolution fusion | flops 4327473152 | bytes 20975616 | tf_op jit(solution)/shard_map/dot_general | solution.py:356
  506.8 11.7 %convolution_convert_fusion.4 = bf16[1024,2048]{1,0:T(8,128)(2,1)} fusion(bf16[1024,1408]{1,0:T(8,128)(2,1)} %copy-done.44, bf16[1408,2048]{1,0:T(8,128)(2,1)} %all-gather.11.cloned.1.call-done), kind=kOutput, calls=%fused_computation.24 | convolution fusion | flops 5907677184 | bytes 12845056 | tf_op jit(solution)/shard_map/dot_general | solution.py:356
  518.5 58.9 %core_backward.1 = (bf16[1024,2048]{1,0:T(8,128)(2,1)S(1)}, f32[1024,8]{1,0:T(8,128)S(1)}, f32[4,2048]{1,0:T(4,128)S(1)}, f32[1,8]{1,0:T(1,128)S(1)}, f32[1,256]{1,0:T(1,128)S(1)}) custom-call(f32[1024,1024]{1,0:T(8,128)} %get-tuple-element.74.dn_in, f32[1024,2048]{1,0:T(8,128)} %fusion.60.pqkv, f32[1024,8]{1,0:T(8,128)S(1)} %copy-done.7, ...), custom_call_target="tpu_custom_call" | custom-call | flops 20000000000 | bytes 50331648 | tf_op jit(solution)/shard_map/core_backward/pallas_call | solution.py:331
  579.5 14.1 %convolution_convert_fusion.1 = bf16[2048,2048]{1,0:T(8,128)(2,1)} fusion(bf16[1024,2048]{1,0:T(8,128)(2,1)} %pad_maximum_fusion.2, bf16[1024,2048]{1,0:T(8,128)(2,1)} %copy-done.13), kind=kOutput, calls=%fused_computation.3 | convolution fusion | flops 8594128896 | bytes 16777216 | tf_op jit(solution)/shard_map/dot_general | solution.py:356
  595.2 9.1 %fusion.10 = f32[1024,2048]{1,0:T(8,128)} fusion(bf16[1024,1024]{1,0:T(8,128)(2,1)S(1)} %copy-done.67, bf16[2048,2048]{0,1:T(8,128)(2,1)} %all-gather.7.cloned.1.call-done), kind=kOutput, calls=%fused_computation.31 | convolution fusion | flops 4294967296 | bytes 14680064 | tf_op jit(solution)/shard_map/dot_general | solution.py:356
  612.1 11.6 %fusion.63 = f32[1024,2048]{1,0:T(8,128)S(1)} fusion(bf16[1024,2048]{1,0:T(8,128)(2,1)S(1)} %copy-done.14, bf16[2048,2048]{1,0:T(8,128)(2,1)} %all-gather.5.cloned.1.call-done), kind=kOutput, calls=%fused_computation.174 | convolution fusion | flops 8589934592 | bytes 20971520 | tf_op jit(solution)/shard_map/dot_general | solution.py:356
  704.1 14.7 %reduce-scatter.9.cloned.1.call-done = bf16[256,2048]{1,0:T(8,128)(2,1)} async-done(((bf16[2048,2048]{1,0:T(8,128)(2,1)}), bf16[256,2048]{1,0:T(8,128)(2,1)}) %reduce-scatter.9.cloned.1.call-update) | async-done | bytes 1048592 | tf_op jit(solution)/shard_map/reduce_scatter | solution.py:431
  (382 shorter events, 278.2 us)
Async XLA Ops:
  7.2 99.3 %all-gather.5.cloned.1.call-start = ((), (), s32[]{:S(2)}) async-start(), calls=%async_computation.5 | async-start | bytes 9437184 | tf_op jit(solution)/shard_map/all_gather | solution.py:427
  11.9 168.6 %all-gather.7.cloned.1.call-start = ((), (), s32[]{:S(2)}) async-start(), calls=%async_computation.6 | async-start | bytes 9437184 | tf_op jit(solution)/shard_map/all_gather | solution.py:427
  14.6 274.3 %all-gather.9.cloned.1.call-start = ((), (), s32[]{:S(2)}) async-start(), calls=%async_computation.7 | async-start | bytes 12976128 | tf_op jit(solution)/shard_map/all_gather | solution.py:427
  17.6 332.6 %all-gather.11.cloned.1.call-start = ((), (), s32[]{:S(2)}) async-start(), calls=%async_computation.8 | async-start | bytes 6488064 | tf_op jit(solution)/shard_map/all_gather | solution.py:427
  19.3 26.1 %collective-permute-start.1 = (bf16[256,2048]{1,0:T(8,128)(2,1)S(1)}, bf16[256,2048]{1,0:T(8,128)(2,1)S(1)}, u32[]{:S(2)}, u32[]{:S(2)}) collective-permute-start(bf16[256,2048]{1,0:T(8,128)(2,1)S(1)} %get-tuple-element.146), channel_id=1, source_target_pairs={{0,2},{1,3},{2,0},{3,1},{4,6},{5,7},{6,4},{7,5},{8,10},{9,11},{10,... | collective-permute-start | bytes 3145736 | tf_op jit(solution)/shard_map/ppermute | solution.py:360
  22.2 25.8 %collective-permute-start = (bf16[256,2048]{1,0:T(8,128)(2,1)S(1)}, bf16[256,2048]{1,0:T(8,128)(2,1)S(1)}, u32[]{:S(2)}, u32[]{:S(2)}) collective-permute-start(bf16[256,2048]{1,0:T(8,128)(2,1)S(1)} %get-tuple-element.146), channel_id=1, source_target_pairs={{0,1},{1,0},{2,3},{3,2},{4,5},{5,4},{6,7},{7,6},{8,9},{9,8},{10,11... | collective-permute-start | bytes 3145736 | tf_op jit(solution)/shard_map/ppermute | solution.py:360
  67.9 23.6 %collective-permute-start.5 = (bf16[256,2048]{1,0:T(8,128)(2,1)S(1)}, bf16[256,2048]{1,0:T(8,128)(2,1)S(1)}, u32[]{:S(2)}, u32[]{:S(2)}) collective-permute-start(bf16[256,2048]{1,0:T(8,128)(2,1)S(1)} %copy-done.37), channel_id=1, source_target_pairs={{0,2},{1,3},{2,0},{3,1},{4,6},{5,7},{6,4},{7,5},{8,10},{9,11},{10,... | collective-permute-start | bytes 3145736 | tf_op jit(solution)/shard_map/ppermute | solution.py:360
  69.3 24.4 %collective-permute-start.4 = (bf16[256,2048]{1,0:T(8,128)(2,1)S(1)}, bf16[256,2048]{1,0:T(8,128)(2,1)}, u32[]{:S(2)}, u32[]{:S(2)}) collective-permute-start(bf16[256,2048]{1,0:T(8,128)(2,1)S(1)} %copy-done.37), channel_id=1, source_target_pairs={{0,1},{1,0},{2,3},{3,2},{4,5},{5,4},{6,7},{7,6},{8,9},{9,8},{10,11... | collective-permute-start | bytes 3145736 | tf_op jit(solution)/shard_map/ppermute | solution.py:360
  196.5 25.4 %collective-permute-start.8 = (bf16[512,1024]{1,0:T(8,128)(2,1)S(1)}, bf16[512,1024]{1,0:T(8,128)(2,1)S(1)}, u32[]{:S(2)}, u32[]{:S(2)}) collective-permute-start(bf16[512,1024]{1,0:T(8,128)(2,1)S(1)} %pad_maximum_fusion.11), channel_id=1, source_target_pairs={{0,1},{1,0},{2,3},{3,2},{4,5},{5,4},{6,7},{7,6},{8,9},{9,8},{10,11... | collective-permute-start | bytes 3145736 | tf_op jit(solution)/shard_map/ppermute | solution.py:360
  198.1 25.1 %collective-permute-start.9 = (bf16[512,1024]{1,0:T(8,128)(2,1)S(1)}, bf16[512,1024]{1,0:T(8,128)(2,1)S(1)}, u32[]{:S(2)}, u32[]{:S(2)}) collective-permute-start(bf16[512,1024]{1,0:T(8,128)(2,1)S(1)} %pad_maximum_fusion.12), channel_id=1, source_target_pairs={{0,2},{1,3},{2,0},{3,1},{4,6},{5,7},{6,4},{7,5},{8,10},{9,11},{10,... | collective-permute-start | bytes 3145736 | tf_op jit(solution)/shard_map/ppermute | solution.py:360
  228.3 278.4 %reduce-scatter.5.cloned.1.call-start = ((), (), s32[]{:S(2)}) async-start(), calls=%async_computation.9 | async-start | bytes 6488064 | tf_op jit(solution)/shard_map/reduce_scatter | solution.py:431
  244.3 23.0 %collective-permute-start.13 = (bf16[256,2048]{1,0:T(8,128)(2,1)S(1)}, bf16[256,2048]{1,0:T(8,128)(2,1)S(1)}, u32[]{:S(2)}, u32[]{:S(2)}) collective-permute-start(bf16[256,2048]{1,0:T(8,128)(2,1)S(1)} %get-tuple-element.142), channel_id=1, source_target_pairs={{0,2},{1,3},{2,0},{3,1},{4,6},{5,7},{6,4},{7,5},{8,10},{9,11},{10,... | collective-permute-start | bytes 3145736 | tf_op jit(solution)/shard_map/ppermute | solution.py:360
  244.9 24.1 %collective-permute-start.12 = (bf16[256,2048]{1,0:T(8,128)(2,1)S(1)}, bf16[256,2048]{1,0:T(8,128)(2,1)S(1)}, u32[]{:S(2)}, u32[]{:S(2)}) collective-permute-start(bf16[256,2048]{1,0:T(8,128)(2,1)S(1)} %get-tuple-element.142), channel_id=1, source_target_pairs={{0,1},{1,0},{2,3},{3,2},{4,5},{5,4},{6,7},{7,6},{8,9},{9,8},{10,11... | collective-permute-start | bytes 3145736 | tf_op jit(solution)/shard_map/ppermute | solution.py:360
  322.7 256.8 %reduce-scatter.7.cloned.1.call-start = ((), (), s32[]{:S(2)}) async-start(), calls=%async_computation.10 | async-start | bytes 12976128 | tf_op jit(solution)/shard_map/reduce_scatter | solution.py:431
  386.3 25.5 %collective-permute-start.16 = (bf16[512,1024]{1,0:T(8,128)(2,1)}, bf16[512,1024]{1,0:T(8,128)(2,1)S(1)}, u32[]{:S(2)}, u32[]{:S(2)}) collective-permute-start(bf16[512,1024]{1,0:T(8,128)(2,1)} %pad_maximum_fusion.13), channel_id=1, source_target_pairs={{0,1},{1,0},{2,3},{3,2},{4,5},{5,4},{6,7},{7,6},{8,9},{9,8},{10,11... | collective-permute-start | bytes 3145736 | tf_op jit(solution)/shard_map/ppermute | solution.py:360
  387.7 25.4 %collective-permute-start.17 = (bf16[512,1024]{1,0:T(8,128)(2,1)}, bf16[512,1024]{1,0:T(8,128)(2,1)}, u32[]{:S(2)}, u32[]{:S(2)}) collective-permute-start(bf16[512,1024]{1,0:T(8,128)(2,1)} %concatenate.140), channel_id=1, source_target_pairs={{0,2},{1,3},{2,0},{3,1},{4,6},{5,7},{6,4},{7,5},{8,10},{9,11},{10,... | collective-permute-start | bytes 3145736 | tf_op jit(solution)/shard_map/ppermute | solution.py:360
  413.1 287.3 %reduce-scatter.11.cloned.1.call-start = ((), (), s32[]{:S(2)}) async-start(), calls=%async_computation.12 | async-start | bytes 9437184 | tf_op jit(solution)/shard_map/reduce_scatter | solution.py:431
  434.0 23.1 %collective-permute-start.21 = (bf16[256,2048]{1,0:T(8,128)(2,1)S(1)}, bf16[256,2048]{1,0:T(8,128)(2,1)S(1)}, u32[]{:S(2)}, u32[]{:S(2)}) collective-permute-start(bf16[256,2048]{1,0:T(8,128)(2,1)S(1)} %get-tuple-element.139), channel_id=1, source_target_pairs={{0,2},{1,3},{2,0},{3,1},{4,6},{5,7},{6,4},{7,5},{8,10},{9,11},{10,... | collective-permute-start | bytes 3145736 | tf_op jit(solution)/shard_map/ppermute | solution.py:360
  434.6 23.3 %collective-permute-start.20 = (bf16[256,2048]{1,0:T(8,128)(2,1)S(1)}, bf16[256,2048]{1,0:T(8,128)(2,1)S(1)}, u32[]{:S(2)}, u32[]{:S(2)}) collective-permute-start(bf16[256,2048]{1,0:T(8,128)(2,1)S(1)} %get-tuple-element.139), channel_id=1, source_target_pairs={{0,1},{1,0},{2,3},{3,2},{4,5},{5,4},{6,7},{7,6},{8,9},{9,8},{10,11... | collective-permute-start | bytes 3145736 | tf_op jit(solution)/shard_map/ppermute | solution.py:360
  506.7 212.1 %reduce-scatter.9.cloned.1.call-start = ((), (), s32[]{:S(2)}) async-start(), calls=%async_computation.11 | async-start | bytes 9437184 | tf_op jit(solution)/shard_map/reduce_scatter | solution.py:431
  606.6 50.9 %collective-permute-start.24 = (bf16[512,1024]{1,0:T(8,128)(2,1)}, bf16[512,1024]{1,0:T(8,128)(2,1)S(1)}, u32[]{:S(2)}, u32[]{:S(2)}) collective-permute-start(bf16[512,1024]{1,0:T(8,128)(2,1)} %pad_maximum_fusion.14), channel_id=1, source_target_pairs={{0,1},{1,0},{2,3},{3,2},{4,5},{5,4},{6,7},{7,6},{8,9},{9,8},{10,11... | collective-permute-start | bytes 3145736 | tf_op jit(solution)/shard_map/ppermute | solution.py:360
  607.9 49.8 %collective-permute-start.25 = (bf16[512,1024]{1,0:T(8,128)(2,1)}, bf16[512,1024]{1,0:T(8,128)(2,1)S(1)}, u32[]{:S(2)}, u32[]{:S(2)}) collective-permute-start(bf16[512,1024]{1,0:T(8,128)(2,1)} %concatenate.132), channel_id=1, source_target_pairs={{0,2},{1,3},{2,0},{3,1},{4,6},{5,7},{6,4},{7,5},{8,10},{9,11},{10,... | collective-permute-start | bytes 3145736 | tf_op jit(solution)/shard_map/ppermute | solution.py:360
  626.7 24.3 %collective-permute-start.28 = (bf16[512,1024]{1,0:T(8,128)(2,1)}, bf16[512,1024]{1,0:T(8,128)(2,1)S(1)}, u32[]{:S(2)}, u32[]{:S(2)}) collective-permute-start(bf16[512,1024]{1,0:T(8,128)(2,1)} %pad_maximum_fusion.15), channel_id=1, source_target_pairs={{0,1},{1,0},{2,3},{3,2},{4,5},{5,4},{6,7},{7,6},{8,9},{9,8},{10,11... | collective-permute-start | bytes 3145736 | tf_op jit(solution)/shard_map/ppermute | solution.py:360
  629.2 22.7 %collective-permute-start.29 = (bf16[512,1024]{1,0:T(8,128)(2,1)}, bf16[512,1024]{1,0:T(8,128)(2,1)}, u32[]{:S(2)}, u32[]{:S(2)}) collective-permute-start(bf16[512,1024]{1,0:T(8,128)(2,1)} %pad_maximum_fusion.16), channel_id=1, source_target_pairs={{0,2},{1,3},{2,0},{3,1},{4,6},{5,7},{6,4},{7,5},{8,10},{9,11},{10,... | collective-permute-start | bytes 3145736 | tf_op jit(solution)/shard_map/ppermute | solution.py:360
  (96 other events, 1006.0 us)
Sparse Core Ops, SparseCore 0:
  12.0 85.1 all-gather.4
  99.4 81.0 all-gather.6
  182.7 106.2 all-gather.8
  291.0 59.1 all-gather.10
  352.3 63.0 reduce-scatter.4
  417.5 117.6 reduce-scatter.6
  537.6 87.9 reduce-scatter.10
  627.9 90.9 reduce-scatter.8

commit v3 on v2

--- a/solution.py
+++ b/solution.py
@@ -360,12 +360,16 @@
     return lax.ppermute(piece, "tensor", [(i, i ^ mask) for i in range(4)])
 
 
-def gather_rows(own):
+def gather_rows(own, beside=None):
     if lax.axis_size("tensor") != 4:
-        return lax.all_gather(own, "tensor", axis=0, tiled=True)
+        full = lax.all_gather(own, "tensor", axis=0, tiled=True)
+        return full if beside is None else (full, beside)
     half = own.shape[0] // 2
     first, second = swap(own, 1), swap(own, 2)
-    return jnp.concatenate([own, first, second, swap(second[:half], 1), swap(first[half:], 2)], 0)
+    if beside is not None:
+        first, second, beside = lax.optimization_barrier((first, second, beside))
+    full = jnp.concatenate([own, first, second, swap(second[:half], 1), swap(first[half:], 2)], 0)
+    return full if beside is None else (full, beside)
 
 
 def scatter_rows(part, beside=None):
@@ -427,8 +431,31 @@
     return lax.all_gather(shard.astype(BF16), "dp", axis=axis, tiled=True)
 
 
+def sibling(piece):
+    return lax.ppermute(piece, "dp", [(i, i ^ 1) for i in range(lax.axis_size("dp"))])
+
+
+def split_blocks(full):
+    size = lax.axis_size("dp")
+    width = full.shape[1] // size
+    core = lax.axis_index("dp") % 2
+
+    def pick(c):
+        return jnp.concatenate(
+            [lax.dynamic_slice_in_dim(full, (2 * i + c) * width, width, 1) for i in range(size // 2)], 1
+        )
+
+    return pick(core), pick(1 - core)
+
+
 def scatter_dp(part, axis):
     return lax.psum_scatter(part, "dp", scatter_dimension=axis, tiled=True)
+
+
+def scatter_chips(part, axis):
+    size = lax.axis_size("dp")
+    groups = [list(range(core, size, 2)) for core in range(2)]
+    return lax.psum_scatter(part, "dp", scatter_dimension=axis, tiled=True, axis_index_groups=groups)
 
 
 def local(
@@ -488,7 +515,7 @@
     cot = gather_rows(cot_own)
     pqkv = dot(normed, full_qkv)
     pab = dot(normed, full_narrow, NT)
-    pqkv, cot = hold((pqkv, cot))
+    pqkv, cot, normed_here, normed_there = hold((pqkv, cot, *split_blocks(normed)))
     kept = core_forward(pqkv, pab, taps, rate, bias, keys)
     po = dot(normed, full_outgate)
     po_sig = jax.nn.sigmoid(po)
@@ -506,32 +533,44 @@
     grad_gate_pre = (grad_activ * up_pre * gate_sig * (1.0 + gate_pre * (1.0 - gate_sig))).astype(BF16)
     grad_up_pre = (grad_activ * (gate_pre * gate_sig)).astype(BF16)
     grad_pre = jnp.concatenate([grad_gate_pre, grad_up_pre], 1)
-    grad_ffn_norm, part_pair = scatter_rows(
-        dot(grad_pre, full_pair, NT).astype(BF16), dot(ffn_rows, grad_pre, TN).astype(BF16)
-    )
-    grad_pair = scatter_dp(part_pair, 0)
+    ffn_here, ffn_there = split_blocks(ffn_rows)
+    grad_pre, sent = hold((grad_pre, dot(ffn_there, grad_pre, TN).astype(BF16)))
+    got = sibling(sent)
+    grad_ffn_rows, got = hold((dot(grad_pre, full_pair, NT).astype(BF16), got))
+    part_pair = (dot(ffn_here, grad_pre, TN) + got.astype(F32)).astype(BF16)
+    grad_ffn_norm, part_pair = scatter_rows(grad_ffn_rows, part_pair)
+    grad_pair = scatter_chips(part_pair, 0)
     grad_middle_norm, ffn_gain_part = norm_back(middle, ffn_gain, grad_ffn_norm)
     grad_middle = grad_out.astype(F32) + grad_middle_norm
 
-    mix_cot = reorder(gather_rows(grad_middle.astype(BF16)))
+    activ_late, mix_low = hold((activ, grad_middle.astype(BF16)))
+    mix_cot, out_part = gather_rows(mix_low, dot(activ_late, full_down).astype(BF16))
+    mix_cot = reorder(mix_cot)
+    mix_here, mix_there = split_blocks(mix_cot)
+    mix_cot, sent_output = hold((mix_cot, dot(mix_there, mixed, TN).astype(BF16)))
     grad_mixed = dot(mix_cot, full_output)
     grad_po = grad_mixed * kept[0].astype(F32) * gain * (po_sig * (1.0 + po * (1.0 - po_sig)))
     grad_po = grad_po.astype(BF16)
     grad_n = grad_mixed * gain * (po * po_sig)
-    part_gate_out = jnp.concatenate([dot(normed, grad_po, TN), dot(mix_cot, mixed, TN)], 1).astype(BF16)
-    grad_n, activ_late, grad_w_down, part_gate_out = hold((grad_n, activ, grad_w_down, part_gate_out))
-    grad_gate_out = scatter_dp(part_gate_out, 0)
-    out_part = dot(activ_late, full_down).astype(BF16)
-    grad_n, out_part = hold((grad_n, out_part))
-    hidden_out = (middle + scatter_rows(out_part)).astype(BF16)
+    sent_outgate = dot(normed_there, grad_po, TN).astype(BF16)
+    got_output, got_outgate = sibling(sent_output), sibling(sent_outgate)
+    part_output = (dot(mix_here, mixed, TN) + got_output.astype(F32)).astype(BF16)
+    part_outgate = (dot(normed_here, grad_po, TN) + got_outgate.astype(F32)).astype(BF16)
+    part_gate_out = jnp.concatenate([part_outgate, part_output], 1)
+    grad_n, grad_w_down, part_gate_out = hold((grad_n, grad_w_down, part_gate_out))
+    grad_gate_out = scatter_chips(part_gate_out, 0)
     grad_pqkv, grad_pab, grad_taps, grad_small, grad_gain = core_backward(grad_n, pqkv, pab, kept, taps, rate, bias)
     grad_pqkv, grad_pair = hold((grad_pqkv, grad_pair))
-    grad_pqkv, part_qkv = hold((grad_pqkv, dot(normed, grad_pqkv, TN).astype(BF16)))
+    out_rows, grad_pqkv = scatter_rows(out_part, grad_pqkv)
+    hidden_out = (middle + out_rows).astype(BF16)
+    part_qkv = dot(normed, grad_pqkv, TN).astype(BF16)
+    grad_pqkv, grad_pab, grad_taps, part_qkv = hold((grad_pqkv, grad_pab, grad_taps, part_qkv))
     grad_qkv = scatter_dp(part_qkv, 0)
     low_pab = grad_pab.astype(BF16)
     grad_normed = dot(grad_pqkv, full_qkv, NT) + dot(grad_po, full_outgate, NT) + dot(low_pab, full_narrow)
+    mix_gain_part = jnp.sum(grad_normed * normed.astype(F32), 0) / mix_gain
     grad_mix_norm = scatter_rows(reorder(grad_normed.astype(BF16)))
-    grad_rows, mix_gain_part = norm_back(rows_in, mix_gain, grad_mix_norm)
+    grad_rows, _ = norm_back(rows_in, mix_gain, grad_mix_norm)
     grad_in = (grad_middle + grad_rows).astype(BF16)
 
     grad_narrow = dot(low_pab, normed, TN)

time: 734 us -> 723 us (0.985)
  waiting for transfers between devices: 249 us -> 226 us
    reduce_scatter x4 -> x2, waiting for transfers between devices: 14.7 us -> 0.01 us  [scatter_dp(): return lax.psum_scatter(part, 'dp', scatter_dimension=axis, tiled=True)]
    ppermute x32, waiting for transfers between devices: 169 us -> 156 us  [swap(): return lax.ppermute(piece, 'tensor', [(i, i ^ mask) for i in range(4)])]
    dot_general x18 -> x21, matrix products: 189 us -> 186 us  [dot(): return lax.dot_general(a, b, (dims, ((), ())), preferred_element_type=F32)]
    unnamed x167 -> x180, local copies, waits for them, and re-layouts: 33 us -> 30.9 us
  transfers between devices with their start and end apart: 46 -> 49, of which waited for: 34 -> 31; matrix products, arithmetic and copies ran while one was open for 38% -> 39% of each run, Pallas kernels for 14% -> 14%
where the time goes in v3:
time: 723 us; the launch traced here: 719 us
  waiting for transfers between devices  226 us (31%)
  matrix products  186 us (26%)
  Pallas kernels  101 us (14%)
  other arithmetic  62.9 us (9%)
  local copies, waits for them, and re-layouts  59.5 us (8%)
  starting transfers between devices  53 us (7%)
  between operations  15.8 us (2%)
  blocking collectives  14.3 us (2%)
    dot_general x21, matrix products, dot(): return lax.dot_general(a, b, (dims, ((), ())), preferred_element_type=F32)  186 us
    ppermute x32, waiting for transfers between devices, swap(): return lax.ppermute(piece, 'tensor', [(i, i ^ mask) for i in range(4)])  156 us
    pallas_call x1, Pallas kernels, core_backward(): pl.pallas_call(backward_kernel, grid=(blocks,), in_specs=[tokens(a.shape[...  59.1 us
    all_gather x4, waiting for transfers between devices, gather_dp(): return lax.all_gather(shard.astype(BF16), 'dp', axis=axis, tiled=True)  47.7 us
    pallas_call x1, Pallas kernels, core_forward(): pl.pallas_call(forward_kernel, grid=(blocks,), in_specs=[tokens(a.shape[1...  41.8 us
    ppermute x32, starting transfers between devices, swap(): return lax.ppermute(piece, 'tensor', [(i, i ^ mask) for i in range(4)])  41.5 us
    unnamed x180, local copies, waits for them, and re-layouts  30.9 us
    ppermute x5, waiting for transfers between devices, sum_everywhere(): lax.ppermute(values, axis, [(i, i ^ mask) for i in range(size)])  18.5 us
  transfers between devices with their start and end apart: 49, of which 31 were waited for; matrix products, arithmetic and copies ran while one was open for 39% of the time, Pallas kernels for 14%

profile of v3, /device:TPU:0, one launch (start us, length us, event | category | flops | bytes accessed | tf_op | source)
XLA Modules:
  0.0 719.1 jit_solution(888271083032772895)
XLA Ops:
  23.9 14.3 %all_gather.17 = bf16[8,12,256]{2,1,0:T(8,128)(2,1)S(1)} all-gather(bf16[1,12,256]{2,1,0:T(8,128)(2,1)S(1)} %pad_maximum_fusion.18), channel_id=1, replica_groups=mesh['dp'=8,'tensor'=4] {'dp'}, dimensions={0}, use_global_device_ids=true | all-gather | bytes 55296 | tf_op jit(solution)/shard_map/all_gather | solution.py:496
  73.8 16.3 %collective-permute-done.5 = bf16[256,2048]{1,0:T(8,128)(2,1)S(1)} collective-permute-done((bf16[256,2048]{1,0:T(8,128)(2,1)S(1)}, bf16[256,2048]{1,0:T(8,128)(2,1)S(1)}, u32[]{:S(2)}, u32[]{:S(2)}) %collective-permute-start.5) | collective-permute-done | bytes 1048608 | tf_op jit(solution)/shard_map/ppermute | solution.py:360
  104.3 15.4 %fusion.94.pqkv = f32[1024,2048]{1,0:T(8,128)} fusion(bf16[1024,2048]{1,0:T(8,128)(2,1)} %copy-done.18, bf16[2048,2048]{1,0:T(8,128)(2,1)} %all-gather.5.cloned.1.call-done), kind=kOutput, calls=%fused_computation.230 | convolution fusion | flops 8589934592 | bytes 20971520 | tf_op jit(solution)/shard_map/dot_general | solution.py:356
  119.7 41.8 %core_forward.1 = (bf16[1024,1024]{1,0:T(8,128)(2,1)S(1)}, f32[1024,4]{1,0:T(8,128)S(1)}, f32[1024,2048]{1,0:T(8,128)}, bf16[1024,1024]{1,0:T(8,128)(2,1)S(1)}, ...) custom-call(f32[1024,2048]{1,0:T(8,128)} %fusion.94.pqkv, f32[1024,8]{1,0:T(8,128)S(1)} %fusion.95.pab, ...), custom_call_target="tpu_custom_call" | custom-call | flops 8000000000 | bytes 33554432 | tf_op jit(solution)/shard_map/core_forward/pallas_call | solution.py:162
  166.6 13.9 %all-gather.7.cloned.1.call-done = bf16[2048,2048]{0,1:T(8,128)(2,1)} async-done(((bf16[256,2048]{0,1:T(8,128)(2,1)}), bf16[2048,2048]{0,1:T(8,128)(2,1)}) %all-gather.7.cloned.1.call-update) | async-done | bytes 8388624 | tf_op jit(solution)/shard_map/all_gather | solution.py:431
  180.5 10.8 %fusion.2 = (bf16[1024,1024]{1,0:T(8,128)(2,1)S(1)}, f32[1024,1024]{1,0:T(8,128)}) fusion(bf16[1024,1024]{1,0:T(8,128)(2,1)S(1)} %get-tuple-element.74.n_in, f32[1024]{0:T(1024)S(1)} %bitcast.86, bf16[1024,2048]{1,0:T(8,128)(2,1)} %copy-done.18, bf16[2048,2048]{0,1:T(8,128)(2,1)} %all-gather.7.cloned.1.call-done), kind=kOutput, calls=%fused_computation.15 | convolution fusion | flops 4303355904 | bytes 16781312 | tf_op jit(solution)/shard_map/dot_general | solution.py:356
  199.8 22.3 %collective-permute-done.9 = bf16[512,1024]{1,0:T(8,128)(2,1)S(1)} collective-permute-done((bf16[512,1024]{1,0:T(8,128)(2,1)S(1)}, bf16[512,1024]{1,0:T(8,128)(2,1)S(1)}, u32[]{:S(2)}, u32[]{:S(2)}) %collective-permute-start.9) | collective-permute-done | bytes 1048608 | tf_op jit(solution)/shard_map/ppermute | solution.py:360
  228.3 10.4 %collective-permute-done.10 = bf16[256,1024]{1,0:T(8,128)(2,1)} collective-permute-done((bf16[256,1024]{1,0:T(8,128)(2,1)}, bf16[256,1024]{1,0:T(8,128)(2,1)}, u32[]{:S(2)}, u32[]{:S(2)}) %collective-permute-start.10) | collective-permute-done | bytes 524320 | tf_op jit(solution)/shard_map/ppermute | solution.py:360
  245.2 20.6 %collective-permute-done.13 = bf16[256,2048]{1,0:T(8,128)(2,1)S(1)} collective-permute-done((bf16[256,2048]{1,0:T(8,128)(2,1)S(1)}, bf16[256,2048]{1,0:T(8,128)(2,1)S(1)}, u32[]{:S(2)}, u32[]{:S(2)}) %collective-permute-start.13) | collective-permute-done | bytes 1048608 | tf_op jit(solution)/shard_map/ppermute | solution.py:360
  289.0 17.2 %fusion.96 = f32[1024,2816]{1,0:T(8,128)S(1)} fusion(bf16[1024,2048]{1,0:T(8,128)(2,1)} %copy-done.32, bf16[2048,2816]{1,0:T(8,128)(2,1)} %all-gather.9.cloned.1.call-done), kind=kOutput, calls=%fused_computation.232 | convolution fusion | flops 11811160064 | bytes 27262976 | tf_op jit(solution)/shard_map/dot_general | solution.py:356
  312.0 10.7 %convolution_convert_fusion.1 = bf16[1408,2048]{1,0:T(8,128)(2,1)} fusion(bf16[1024,1408]{1,0:T(8,128)(2,1)S(1)} %multiply_convert_fusion.2, bf16[1024,2048]{1,0:T(8,128)(2,1)} %constant_dynamic-update-slice_fusion.5), kind=kOutput, calls=%fused_computation.4 | convolution fusion | flops 5908463616 | bytes 12845056 | tf_op jit(solution)/shard_map/dot_general | solution.py:356
  322.8 27.4 %all-gather.11.cloned.1.call-done = bf16[1408,2048]{1,0:T(8,128)(2,1)} async-done(((bf16[1408,256]{1,0:T(8,128)(2,1)}), bf16[1408,2048]{1,0:T(8,128)(2,1)}) %all-gather.11.cloned.1.call-update) | async-done | bytes 5767184 | tf_op jit(solution)/shard_map/all_gather | solution.py:431
  350.2 14.2 %multiply_convert_fusion.1 = (bf16[1024,1408]{1,0:T(8,128)(2,1)S(1)}, bf16[1024,1408]{1,0:T(8,128)(2,1)S(1)}) fusion(f32[1024,2816]{1,0:T(8,128)} %copy-done.25, bf16[1024,2048]{1,0:T(8,128)(2,1)} %constant_dynamic-update-slice_fusion.5, bf16[1408,2048]{1,0:T(8,128)(2,1)} %all-gather.11.cloned.1.call-done), kind=kOutput, calls=%fused_computation.7 | convolution fusion | flops 5924323328 | bytes 27262976 | tf_op jit(solution)/shard_map/dot_general | solution.py:356
  374.7 15.0 %convolution_convert_fusion.3 = bf16[1024,2048]{1,0:T(8,128)(2,1)S(1)} fusion(bf16[1024,2816]{1,0:T(8,128)(2,1)S(1)} %pad_maximum_fusion, bf16[2048,2816]{1,0:T(8,128)(2,1)} %all-gather.9.cloned.1.call-done), kind=kOutput, calls=%fused_computation.27 | convolution fusion | flops 11813257216 | bytes 21495808 | tf_op jit(solution)/shard_map/dot_general | solution.py:356
  396.3 10.7 %add_convert_fusion = bf16[1024,2816]{1,0:T(8,128)(2,1)} fusion(bf16[1024,2816]{1,0:T(8,128)(2,1)} %collective-permute-done.16, bf16[1024,2816]{1,0:T(8,128)(2,1)S(1)} %pad_maximum_fusion, bf16[1024,256]{1,0:T(8,128)(2,1)S(1)} %copy-done.48, bf16[1024,256]{1,0:T(8,128)(2,1)S(1)} %copy-done.49, bf16[1024,256]{1,0:T(8,128)(2,1)S(1)} %copy-done.50, ...), kind=kOutput, calls=%fused_computation | convolution fusion | flops 5922619392 | bytes 19398656 | tf_op jit(solution)/shard_map/dot_general | solution.py:356
  407.0 11.9 %collective-permute-done.17 = bf16[512,1024]{1,0:T(8,128)(2,1)S(1)} collective-permute-done((bf16[512,1024]{1,0:T(8,128)(2,1)}, bf16[512,1024]{1,0:T(8,128)(2,1)S(1)}, u32[]{:S(2)}, u32[]{:S(2)}) %collective-permute-start.17) | collective-permute-done | bytes 1048608 | tf_op jit(solution)/shard_map/ppermute | solution.py:360
  428.1 11.1 %collective-permute-done.19 = bf16[256,1024]{1,0:T(8,128)(2,1)} collective-permute-done((bf16[256,1024]{1,0:T(8,128)(2,1)}, bf16[256,1024]{1,0:T(8,128)(2,1)}, u32[]{:S(2)}, u32[]{:S(2)}) %collective-permute-start.19) | collective-permute-done | bytes 524320 | tf_op jit(solution)/shard_map/ppermute | solution.py:360
  455.7 13.4 %collective-permute-done.21 = bf16[256,2048]{1,0:T(8,128)(2,1)S(1)} collective-permute-done((bf16[256,2048]{1,0:T(8,128)(2,1)S(1)}, bf16[256,2048]{1,0:T(8,128)(2,1)S(1)}, u32[]{:S(2)}, u32[]{:S(2)}) %collective-permute-start.21) | collective-permute-done | bytes 1048608 | tf_op jit(solution)/shard_map/ppermute | solution.py:360
  487.5 10.1 %fusion.5 = (bf16[1024,1024]{1,0:T(8,128)(2,1)}, f32[1024,1024]{1,0:T(8,128)}) fusion(bf16[1024,1024]{1,0:T(8,128)(2,1)S(1)} %copy-done.10, f32[1024,1024]{1,0:T(8,128)} %get-tuple-element.257, f32[1024]{0:T(1024)S(1)} %bitcast.87, bf16[1024,2048]{1,0:T(8,128)(2,1)S(1)} %pad_maximum_fusion.2, bf16[2048,2048]{0,1:T(8,128)(2,1)S(1)} %bitcast.89), kind=kOutput, calls=%fused_computation.18 | convolution fusion | flops 4310695936 | bytes 20975616 | tf_op jit(solution)/shard_map/dot_general | solution.py:356
  520.1 59.1 %core_backward.1 = (bf16[1024,2048]{1,0:T(8,128)(2,1)S(1)}, f32[1024,8]{1,0:T(8,128)S(1)}, f32[4,2048]{1,0:T(4,128)S(1)}, f32[1,8]{1,0:T(1,128)S(1)}, f32[1,256]{1,0:T(1,128)S(1)}) custom-call(f32[1024,1024]{1,0:T(8,128)} %get-tuple-element.97.dn_in, f32[1024,2048]{1,0:T(8,128)} %fusion.94.pqkv, f32[1024,8]{1,0:T(8,128)S(1)} %copy-done.7, ...), custom_call_target="tpu_custom_call" | custom-call | flops 20000000000 | bytes 50331648 | tf_op jit(solution)/shard_map/core_backward/pallas_call | solution.py:331
  581.1 14.2 %convolution_convert_fusion = bf16[2048,2048]{1,0:T(8,128)(2,1)} fusion(bf16[1024,2048]{1,0:T(8,128)(2,1)} %copy-done.18, bf16[1024,2048]{1,0:T(8,128)(2,1)} %copy-done.15), kind=kOutput, calls=%fused_computation.3 | convolution fusion | flops 8594128896 | bytes 16777216 | tf_op jit(solution)/shard_map/dot_general | solution.py:356
  595.3 10.8 %fusion.10 = f32[1024,2048]{1,0:T(8,128)} fusion(bf16[1024,1024]{1,0:T(8,128)(2,1)} %get-tuple-element.176, bf16[2048,2048]{0,1:T(8,128)(2,1)} %all-gather.7.cloned.1.call-done), kind=kOutput, calls=%fused_computation.33 | convolution fusion | flops 4294967296 | bytes 14680064 | tf_op jit(solution)/shard_map/dot_general | solution.py:356
  615.0 13.5 %fusion.97 = f32[1024,2048]{1,0:T(8,128)S(1)} fusion(bf16[1024,2048]{1,0:T(8,128)(2,1)} %copy-done.15, bf16[2048,2048]{1,0:T(8,128)(2,1)} %all-gather.5.cloned.1.call-done), kind=kOutput, calls=%fused_computation.233 | convolution fusion | flops 8589934592 | bytes 20971520 | tf_op jit(solution)/shard_map/dot_general | solution.py:356
  655.4 16.3 %collective-permute-done.38 = f32[4384]{0:T(1024)S(1)} collective-permute-done((f32[4384]{0:T(1024)S(1)}, f32[4384]{0:T(1024)S(1)}, u32[]{:S(2)}, u32[]{:S(2)}) %collective-permute-start.38) | collective-permute-done | bytes 17568 | tf_op jit(solution)/shard_map/ppermute | solution.py:407
  (412 shorter events, 282.2 us)
Async XLA Ops:
  7.2 97.1 %all-gather.5.cloned.1.call-start = ((), (), s32[]{:S(2)}) async-start(), calls=%async_computation.5 | async-start | bytes 9437184 | tf_op jit(solution)/shard_map/all_gather | solution.py:431
  11.9 168.6 %all-gather.7.cloned.1.call-start = ((), (), s32[]{:S(2)}) async-start(), calls=%async_computation.6 | async-start | bytes 9437184 | tf_op jit(solution)/shard_map/all_gather | solution.py:431
  14.6 274.3 %all-gather.9.cloned.1.call-start = ((), (), s32[]{:S(2)}) async-start(), calls=%async_computation.7 | async-start | bytes 12976128 | tf_op jit(solution)/shard_map/all_gather | solution.py:431
  17.6 332.6 %all-gather.11.cloned.1.call-start = ((), (), s32[]{:S(2)}) async-start(), calls=%async_computation.8 | async-start | bytes 6488064 | tf_op jit(solution)/shard_map/all_gather | solution.py:431
  19.3 26.1 %collective-permute-start.1 = (bf16[256,2048]{1,0:T(8,128)(2,1)S(1)}, bf16[256,2048]{1,0:T(8,128)(2,1)S(1)}, u32[]{:S(2)}, u32[]{:S(2)}) collective-permute-start(bf16[256,2048]{1,0:T(8,128)(2,1)S(1)} %get-tuple-element.173), channel_id=1, source_target_pairs={{0,2},{1,3},{2,0},{3,1},{4,6},{5,7},{6,4},{7,5},{8,10},{9,11},{10,... | collective-permute-start | bytes 3145736 | tf_op jit(solution)/shard_map/ppermute | solution.py:360
  22.2 25.8 %collective-permute-start = (bf16[256,2048]{1,0:T(8,128)(2,1)S(1)}, bf16[256,2048]{1,0:T(8,128)(2,1)S(1)}, u32[]{:S(2)}, u32[]{:S(2)}) collective-permute-start(bf16[256,2048]{1,0:T(8,128)(2,1)S(1)} %get-tuple-element.173), channel_id=1, source_target_pairs={{0,1},{1,0},{2,3},{3,2},{4,5},{5,4},{6,7},{7,6},{8,9},{9,8},{10,11... | collective-permute-start | bytes 3145736 | tf_op jit(solution)/shard_map/ppermute | solution.py:360
  66.5 23.5 %collective-permute-start.5 = (bf16[256,2048]{1,0:T(8,128)(2,1)S(1)}, bf16[256,2048]{1,0:T(8,128)(2,1)S(1)}, u32[]{:S(2)}, u32[]{:S(2)}) collective-permute-start(bf16[256,2048]{1,0:T(8,128)(2,1)S(1)} %copy-done.37), channel_id=1, source_target_pairs={{0,2},{1,3},{2,0},{3,1},{4,6},{5,7},{6,4},{7,5},{8,10},{9,11},{10,... | collective-permute-start | bytes 3145736 | tf_op jit(solution)/shard_map/ppermute | solution.py:360
  68.1 24.4 %collective-permute-start.4 = (bf16[256,2048]{1,0:T(8,128)(2,1)S(1)}, bf16[256,2048]{1,0:T(8,128)(2,1)S(1)}, u32[]{:S(2)}, u32[]{:S(2)}) collective-permute-start(bf16[256,2048]{1,0:T(8,128)(2,1)S(1)} %copy-done.37), channel_id=1, source_target_pairs={{0,1},{1,0},{2,3},{3,2},{4,5},{5,4},{6,7},{7,6},{8,9},{9,8},{10,11... | collective-permute-start | bytes 3145736 | tf_op jit(solution)/shard_map/ppermute | solution.py:360
  196.7 25.3 %collective-permute-start.9 = (bf16[512,1024]{1,0:T(8,128)(2,1)S(1)}, bf16[512,1024]{1,0:T(8,128)(2,1)S(1)}, u32[]{:S(2)}, u32[]{:S(2)}) collective-permute-start(bf16[512,1024]{1,0:T(8,128)(2,1)S(1)} %pad_maximum_fusion.11), channel_id=1, source_target_pairs={{0,2},{1,3},{2,0},{3,1},{4,6},{5,7},{6,4},{7,5},{8,10},{9,11},{10,... | collective-permute-start | bytes 3145736 | tf_op jit(solution)/shard_map/ppermute | solution.py:360
  198.2 25.1 %collective-permute-start.8 = (bf16[512,1024]{1,0:T(8,128)(2,1)S(1)}, bf16[512,1024]{1,0:T(8,128)(2,1)S(1)}, u32[]{:S(2)}, u32[]{:S(2)}) collective-permute-start(bf16[512,1024]{1,0:T(8,128)(2,1)S(1)} %pad_maximum_fusion.10), channel_id=1, source_target_pairs={{0,1},{1,0},{2,3},{3,2},{4,5},{5,4},{6,7},{7,6},{8,9},{9,8},{10,11... | collective-permute-start | bytes 3145736 | tf_op jit(solution)/shard_map/ppermute | solution.py:360
  228.3 285.6 %reduce-scatter.5.cloned.1.call-start = ((), (), s32[]{:S(2)}) async-start(), calls=%async_computation.9 | async-start | bytes 6488064 | tf_op jit(solution)/shard_map/reduce_scatter | solution.py:452
  243.8 23.7 %collective-permute-start.12 = (bf16[256,2048]{1,0:T(8,128)(2,1)S(1)}, bf16[256,2048]{1,0:T(8,128)(2,1)S(1)}, u32[]{:S(2)}, u32[]{:S(2)}) collective-permute-start(bf16[256,2048]{1,0:T(8,128)(2,1)S(1)} %get-tuple-element.169), channel_id=1, source_target_pairs={{0,1},{1,0},{2,3},{3,2},{4,5},{5,4},{6,7},{7,6},{8,9},{9,8},{10,11... | collective-permute-start | bytes 3145736 | tf_op jit(solution)/shard_map/ppermute | solution.py:360
  322.7 258.4 %reduce-scatter.7.cloned.1.call-start = ((), (), s32[]{:S(2)}) async-start(), calls=%async_computation.10 | async-start | bytes 7208960 | tf_op jit(solution)/shard_map/reduce_scatter | solution.py:458
  393.3 25.5 %collective-permute-start.17 = (bf16[512,1024]{1,0:T(8,128)(2,1)}, bf16[512,1024]{1,0:T(8,128)(2,1)S(1)}, u32[]{:S(2)}, u32[]{:S(2)}) collective-permute-start(bf16[512,1024]{1,0:T(8,128)(2,1)} %pad_maximum_fusion.12), channel_id=1, source_target_pairs={{0,1},{1,0},{2,3},{3,2},{4,5},{5,4},{6,7},{7,6},{8,9},{9,8},{10,11... | collective-permute-start | bytes 3145736 | tf_op jit(solution)/shard_map/ppermute | solution.py:360
  394.8 25.3 %collective-permute-start.18 = (bf16[512,1024]{1,0:T(8,128)(2,1)}, bf16[512,1024]{1,0:T(8,128)(2,1)}, u32[]{:S(2)}, u32[]{:S(2)}) collective-permute-start(bf16[512,1024]{1,0:T(8,128)(2,1)} %concatenate.146), channel_id=1, source_target_pairs={{0,2},{1,3},{2,0},{3,1},{4,6},{5,7},{6,4},{7,5},{8,10},{9,11},{10,... | collective-permute-start | bytes 3145736 | tf_op jit(solution)/shard_map/ppermute | solution.py:360
  428.1 265.5 %reduce-scatter.11.cloned.1.call-start = ((), (), s32[]{:S(2)}) async-start(), calls=%async_computation.12 | async-start | bytes 5242880 | tf_op jit(solution)/shard_map/reduce_scatter | solution.py:458
  513.9 193.9 %reduce-scatter.9.cloned.1.call-start = ((), (), s32[]{:S(2)}) async-start(), calls=%async_computation.11 | async-start | bytes 9437184 | tf_op jit(solution)/shard_map/reduce_scatter | solution.py:452
  518.7 62.4 %collective-permute-start.23 = (bf16[512,1024]{1,0:T(8,128)(2,1)}, bf16[512,1024]{1,0:T(8,128)(2,1)}, u32[]{:S(2)}, u32[]{:S(2)}) collective-permute-start(bf16[512,1024]{1,0:T(8,128)(2,1)} %pad_maximum_fusion.13), channel_id=1, source_target_pairs={{0,1},{1,0},{2,3},{3,2},{4,5},{5,4},{6,7},{7,6},{8,9},{9,8},{10,11... | collective-permute-start | bytes 3145736 | tf_op jit(solution)/shard_map/ppermute | solution.py:360
  519.4 61.7 %collective-permute-start.24 = (bf16[512,1024]{1,0:T(8,128)(2,1)}, bf16[512,1024]{1,0:T(8,128)(2,1)}, u32[]{:S(2)}, u32[]{:S(2)}) collective-permute-start(bf16[512,1024]{1,0:T(8,128)(2,1)} %concatenate.150), channel_id=1, source_target_pairs={{0,2},{1,3},{2,0},{3,1},{4,6},{5,7},{6,4},{7,5},{8,10},{9,11},{10,... | collective-permute-start | bytes 3145736 | tf_op jit(solution)/shard_map/ppermute | solution.py:360
  611.4 67.0 %all-to-all-start = ((f32[8,12,256]{2,1,0:T(8,128)}), f32[8,12,256]{2,1,0:T(8,128)S(1)}, u32[]{:S(2)}, u32[]{:S(2)}) async-start(f32[8,12,256]{2,1,0:T(8,128)} %pad_maximum_fusion.16), calls=%async_computation.3 | async-start | bytes 262144 | tf_op jit(solution)/shard_map/all_to_all | solution.py:583
  639.6 44.2 %collective-permute-start.32 = (bf16[512,1024]{1,0:T(8,128)(2,1)}, bf16[512,1024]{1,0:T(8,128)(2,1)S(1)}, u32[]{:S(2)}, u32[]{:S(2)}) collective-permute-start(bf16[512,1024]{1,0:T(8,128)(2,1)} %pad_maximum_fusion.15), channel_id=1, source_target_pairs={{0,2},{1,3},{2,0},{3,1},{4,6},{5,7},{6,4},{7,5},{8,10},{9,11},{10,... | collective-permute-start | bytes 3145736 | tf_op jit(solution)/shard_map/ppermute | solution.py:360
  644.9 39.1 %collective-permute-start.31 = (bf16[512,1024]{1,0:T(8,128)(2,1)}, bf16[512,1024]{1,0:T(8,128)(2,1)}, u32[]{:S(2)}, u32[]{:S(2)}) collective-permute-start(bf16[512,1024]{1,0:T(8,128)(2,1)} %pad_maximum_fusion.14), channel_id=1, source_target_pairs={{0,1},{1,0},{2,3},{3,2},{4,5},{5,4},{6,7},{7,6},{8,9},{9,8},{10,11... | collective-permute-start | bytes 3145736 | tf_op jit(solution)/shard_map/ppermute | solution.py:360
  652.7 27.6 %collective-permute-start.29 = (bf16[256,1024]{1,0:T(8,128)(2,1)}, bf16[256,1024]{1,0:T(8,128)(2,1)}, u32[]{:S(2)}, u32[]{:S(2)}) collective-permute-start(bf16[256,1024]{1,0:T(8,128)(2,1)} %get-tuple-element.108), channel_id=1, source_target_pairs={{0,2},{1,3},{2,0},{3,1},{4,6},{5,7},{6,4},{7,5},{8,10},{9,11},{10,... | collective-permute-start | bytes 1572872 | tf_op jit(solution)/shard_map/ppermute | solution.py:360
  654.1 27.4 %collective-permute-start.30 = (bf16[256,1024]{1,0:T(8,128)(2,1)}, bf16[256,1024]{1,0:T(8,128)(2,1)}, u32[]{:S(2)}, u32[]{:S(2)}) collective-permute-start(bf16[256,1024]{1,0:T(8,128)(2,1)} %get-tuple-element.109), channel_id=1, source_target_pairs={{0,1},{1,0},{2,3},{3,2},{4,5},{5,4},{6,7},{7,6},{8,9},{9,8},{10,11... | collective-permute-start | bytes 1572872 | tf_op jit(solution)/shard_map/ppermute | solution.py:360
  (105 other events, 1396.4 us)
Sparse Core Ops, SparseCore 0:
  12.0 85.1 all-gather.4
  99.4 81.0 all-gather.6
  182.7 106.2 all-gather.8
  291.0 59.1 all-gather.10
  352.3 63.0 reduce-scatter.4
  428.2 99.5 reduce-scatter.6
  530.0 77.2 reduce-scatter.10
  609.7 93.1 reduce-scatter.8

commit v4 on v3

--- a/solution.py
+++ b/solution.py
@@ -348,6 +348,42 @@
     )(dn, pqkv, pab, n_in, norm_in, conved, u_in, s_in, t_in, taps, rate, bias)
 
 
+def projections_kernel(dqkv, dpo, dab, w_qkv, w_out, w_ab, normed, out, sums):
+    grad = (
+        mm(dqkv[...], w_qkv[...], NT)
+        + mm(dpo[...], w_out[...], NT)
+        + mm(dab[...], w_ab[...])
+    )
+    out[...] = grad.astype(out.dtype)
+    sums[...] = jnp.sum(grad * normed[...].astype(F32), 0, keepdims=True)
+
+
+def projections_back(dqkv, dpo, dab, w_qkv, w_out, w_ab, normed):
+    rows, model = normed.shape
+    tile = 256
+    whole = lambda a: pl.BlockSpec(a.shape, lambda n: (0, 0), pipeline_mode=pl.Buffered(1))
+    return pl.pallas_call(
+        projections_kernel,
+        grid=(model // tile,),
+        in_specs=[
+            whole(dqkv),
+            whole(dpo),
+            whole(dab),
+            pl.BlockSpec((tile, dqkv.shape[1]), lambda n: (n, 0)),
+            pl.BlockSpec((tile, dpo.shape[1]), lambda n: (n, 0)),
+            pl.BlockSpec((dab.shape[1], tile), lambda n: (0, n)),
+            pl.BlockSpec((rows, tile), lambda n: (0, n)),
+        ],
+        out_specs=[pl.BlockSpec((rows, tile), lambda n: (0, n)), pl.BlockSpec((1, tile), lambda n: (0, n))],
+        out_shape=[jax.ShapeDtypeStruct((rows, model), BF16), jax.ShapeDtypeStruct((1, model), F32)],
+        compiler_params=pltpu.CompilerParams(dimension_semantics=("arbitrary",), vmem_limit_bytes=40 * 2**20),
+        cost_estimate=pl.CostEstimate(
+            flops=2 * rows * model * (dqkv.shape[1] + dpo.shape[1]), bytes_accessed=32 * 2**20, transcendentals=0
+        ),
+        name="projections_back",
+    )(dqkv, dpo, dab, w_qkv, w_out, w_ab, normed)
+
+
 def rms_norm(values, gain_vec):
     return values * lax.rsqrt(jnp.mean(values * values, -1, keepdims=True) + 1e-05) * gain_vec
 
@@ -396,16 +432,22 @@
     return total if beside is None else (total, beside)
 
 
-def sum_everywhere(values):
-    for axis in ("dp", "tensor"):
-        size = lax.axis_size(axis)
-        if size & (size - 1):
-            values = lax.psum(values, axis)
-            continue
-        mask = 1
-        while mask < size:
-            values = values + lax.ppermute(values, axis, [(i, i ^ mask) for i in range(size)])
-            mask *= 2
+def scatter_direct(part, beside):
+    if lax.axis_size("tensor") != 4:
+        return lax.psum_scatter(part, "tensor", scatter_dimension=0, tiled=True).astype(F32), beside
+    chunks = jnp.split(part, 4)
+    arrived, beside = lax.optimization_barrier(([swap(chunks[k], k) for k in range(1, 4)], beside))
+    return sum((piece.astype(F32) for piece in arrived), chunks[0].astype(F32)), beside
+
+
+def sum_along(values, axis):
+    size = lax.axis_size(axis)
+    if size & (size - 1):
+        return lax.psum(values, axis)
+    mask = 1
+    while mask < size:
+        values = values + lax.ppermute(values, axis, [(i, i ^ mask) for i in range(size)])
+        mask *= 2
     return values
 
 
@@ -561,18 +603,15 @@
     grad_gate_out = scatter_chips(part_gate_out, 0)
     grad_pqkv, grad_pab, grad_taps, grad_small, grad_gain = core_backward(grad_n, pqkv, pab, kept, taps, rate, bias)
     grad_pqkv, grad_pair = hold((grad_pqkv, grad_pair))
-    out_rows, grad_pqkv = scatter_rows(out_part, grad_pqkv)
-    hidden_out = (middle + out_rows).astype(BF16)
-    part_qkv = dot(normed, grad_pqkv, TN).astype(BF16)
+    out_rows, grad_pqkv = scatter_direct(out_part, grad_pqkv)
+    grad_pqkv, sent = hold((grad_pqkv, dot(normed_there, grad_pqkv, TN).astype(BF16)))
+    got = sibling(sent)
+    part_qkv = (dot(normed_here, grad_pqkv, TN) + got.astype(F32)).astype(BF16)
     grad_pqkv, grad_pab, grad_taps, part_qkv = hold((grad_pqkv, grad_pab, grad_taps, part_qkv))
-    grad_qkv = scatter_dp(part_qkv, 0)
+    grad_qkv = scatter_chips(part_qkv, 0)
     low_pab = grad_pab.astype(BF16)
-    grad_normed = dot(grad_pqkv, full_qkv, NT) + dot(grad_po, full_outgate, NT) + dot(low_pab, full_narrow)
-    mix_gain_part = jnp.sum(grad_normed * normed.astype(F32), 0) / mix_gain
-    grad_mix_norm = scatter_rows(reorder(grad_normed.astype(BF16)))
-    grad_rows, _ = norm_back(rows_in, mix_gain, grad_mix_norm)
-    grad_in = (grad_middle + grad_rows).astype(BF16)
-
+    grad_normed, gain_sum = projections_back(grad_pqkv, grad_po, low_pab, full_qkv, full_gate_out, full_narrow, normed)
+    mix_gain_part = gain_sum[0] / mix_gain
     grad_narrow = dot(low_pab, normed, TN)
     roll = lambda a: jnp.swapaxes(a.reshape(a.shape[0], dp, -1), 0, 1)
     grad_kernels = jnp.concatenate(
@@ -585,17 +624,23 @@
     grad_kernels = few_grads[2 * heads :, : kernels.shape[1]]
 
     place = lambda a: lax.dynamic_update_slice_in_dim(jnp.zeros_like(log_rate), a, first_head, 0)
-    sums = sum_everywhere(
-        jnp.concatenate(
-            [
-                mix_gain_part,
-                ffn_gain_part,
-                grad_gain[0] / head_gain,
-                place(grad_small[0, :heads]),
-                place(grad_small[0, heads:]),
-            ]
-        )
-    )
+    gains = jnp.concatenate(
+        [
+            mix_gain_part,
+            ffn_gain_part,
+            grad_gain[0] / head_gain,
+            place(grad_small[0, :heads]),
+            place(grad_small[0, heads:]),
+        ]
+    )
+    grad_normed, grad_pair, grad_w_down, grad_gate_out, out_rows, gains = hold(
+        (grad_normed, grad_pair, grad_w_down, grad_gate_out, out_rows, gains)
+    )
+    hidden_out = (middle + out_rows).astype(BF16)
+    grad_mix_norm, gains = scatter_rows(reorder(grad_normed), sum_along(gains, "dp"))
+    sums = sum_along(gains, "tensor")
+    grad_rows, _ = norm_back(rows_in, mix_gain, grad_mix_norm)
+    grad_in = (grad_middle + grad_rows).astype(BF16)
     ends = [model, 2 * model, 2 * model + head_gain.shape[0], 2 * model + head_gain.shape[0] + log_rate.shape[0]]
     grad_mix_gain, grad_ffn_gain, grad_head_gain, grad_log_rate, grad_decay_bias = jnp.split(sums, ends)
     grad_qkv, grad_gate_out, grad_pair = grad_qkv.astype(F32), grad_gate_out.astype(F32), grad_pair.astype(F32)

time: 723 us -> 705 us (0.975)
  matrix products: 186 us -> 152 us
  Pallas kernels: 101 us -> 119 us
  other arithmetic: 62.9 us -> 52.9 us
    dot_general x21 -> x19, matrix products: 186 us -> 152 us  [dot(): return lax.dot_general(a, b, (dims, ((), ())), preferred_element_type=F32)]
    pallas_call x0 -> x1, Pallas kernels: none -> 18.2 us  [projections_back(): pl.pallas_call(projections_kernel, grid=(model // tile,), in_specs=[whole...]
    ppermute x5, waiting for transfers between devices: 18.5 us -> 9.36 us  [sum_along(): lax.ppermute(values, axis, [(i, i ^ mask) for i in range(size)])]
    unnamed x180 -> x172, local copies, waits for them, and re-layouts: 30.9 us -> 36.2 us
    ppermute x32 -> x31, waiting for transfers between devices: 156 us -> 161 us  [swap(): return lax.ppermute(piece, 'tensor', [(i, i ^ mask) for i in range(4)])]
    ppermute x32 -> x31, starting transfers between devices: 41.5 us -> 39.3 us  [swap(): return lax.ppermute(piece, 'tensor', [(i, i ^ mask) for i in range(4)])]
  transfers between devices with their start and end apart: 49 -> 49, of which waited for: 31 -> 31; matrix products, arithmetic and copies ran while one was open for 39% -> 34% of each run, Pallas kernels for 14% -> 17%
where the time goes in v4:
time: 705 us; the launch traced here: 700 us
  waiting for transfers between devices  231 us (33%)
  matrix products  152 us (22%)
  Pallas kernels  119 us (17%)
  local copies, waits for them, and re-layouts  64.1 us (9%)
  other arithmetic  52.9 us (8%)
  starting transfers between devices  50.7 us (7%)
  between operations  15.7 us (2%)
  blocking collectives  14.6 us (2%)
    ppermute x31, waiting for transfers between devices, swap(): return lax.ppermute(piece, 'tensor', [(i, i ^ mask) for i in range(4)])  161 us
    dot_general x19, matrix products, dot(): return lax.dot_general(a, b, (dims, ((), ())), preferred_element_type=F32)  152 us
    pallas_call x1, Pallas kernels, core_backward(): pl.pallas_call(backward_kernel, grid=(blocks,), in_specs=[tokens(a.shape[...  58.9 us
    all_gather x4, waiting for transfers between devices, gather_dp(): return lax.all_gather(shard.astype(BF16), 'dp', axis=axis, tiled=True)  46.5 us
    pallas_call x1, Pallas kernels, core_forward(): pl.pallas_call(forward_kernel, grid=(blocks,), in_specs=[tokens(a.shape[1...  41.8 us
    ppermute x31, starting transfers between devices, swap(): return lax.ppermute(piece, 'tensor', [(i, i ^ mask) for i in range(4)])  39.3 us
    unnamed x172, local copies, waits for them, and re-layouts  36.2 us
    pallas_call x1, Pallas kernels, projections_back(): pl.pallas_call(projections_kernel, grid=(model // tile,), in_specs=[whole...  18.2 us
  transfers between devices with their start and end apart: 49, of which 31 were waited for; matrix products, arithmetic and copies ran while one was open for 34% of the time, Pallas kernels for 17%

profile of v4, /device:TPU:0, one launch (start us, length us, event | category | flops | bytes accessed | tf_op | source)
XLA Modules:
  0.0 700.3 jit_solution(16251325660735181587)
XLA Ops:
  25.1 14.6 %all_gather.17 = bf16[8,12,256]{2,1,0:T(8,128)(2,1)S(1)} all-gather(bf16[1,12,256]{2,1,0:T(8,128)(2,1)S(1)} %pad_maximum_fusion.17), channel_id=1, replica_groups=mesh['dp'=8,'tensor'=4] {'dp'}, dimensions={0}, use_global_device_ids=true | all-gather | bytes 55296 | tf_op jit(solution)/shard_map/all_gather | solution.py:538
  74.9 16.3 %collective-permute-done.5 = bf16[256,2048]{1,0:T(8,128)(2,1)S(1)} collective-permute-done((bf16[256,2048]{1,0:T(8,128)(2,1)S(1)}, bf16[256,2048]{1,0:T(8,128)(2,1)S(1)}, u32[]{:S(2)}, u32[]{:S(2)}) %collective-permute-start.5) | collective-permute-done | bytes 1048608 | tf_op jit(solution)/shard_map/ppermute | solution.py:396
  105.4 15.4 %fusion.85.pqkv = f32[1024,2048]{1,0:T(8,128)} fusion(bf16[1024,2048]{1,0:T(8,128)(2,1)} %copy-done.21, bf16[2048,2048]{1,0:T(8,128)(2,1)} %all-gather.5.cloned.1.call-done.w_qkv), kind=kOutput, calls=%fused_computation.216 | convolution fusion | flops 8589934592 | bytes 20971520 | tf_op jit(solution)/shard_map/dot_general | solution.py:392
  120.8 41.8 %core_forward.1 = (bf16[1024,1024]{1,0:T(8,128)(2,1)S(1)}, f32[1024,4]{1,0:T(8,128)S(1)}, f32[1024,2048]{1,0:T(8,128)}, bf16[1024,1024]{1,0:T(8,128)(2,1)S(1)}, ...) custom-call(f32[1024,2048]{1,0:T(8,128)} %fusion.85.pqkv, f32[1024,8]{1,0:T(8,128)S(1)} %fusion.86.pab, ...), custom_call_target="tpu_custom_call" | custom-call | flops 8000000000 | bytes 33554432 | tf_op jit(solution)/shard_map/core_forward/pallas_call | solution.py:162
  167.7 12.3 %all-gather.7.cloned.1.call-done.w_out = bf16[2048,2048]{1,0:T(8,128)(2,1)} async-done(((bf16[256,2048]{1,0:T(8,128)(2,1)}), bf16[2048,2048]{1,0:T(8,128)(2,1)}) %all-gather.7.cloned.1.call-update) | async-done | bytes 8388624 | tf_op jit(solution)/shard_map/all_gather | solution.py:473
  180.0 10.7 %fusion.2 = (bf16[1024,1024]{1,0:T(8,128)(2,1)S(1)}, f32[1024,1024]{1,0:T(8,128)}) fusion(bf16[1024,1024]{1,0:T(8,128)(2,1)S(1)} %get-tuple-element.86.n_in, f32[1024]{0:T(1024)S(1)} %bitcast.89, bf16[1024,2048]{1,0:T(8,128)(2,1)} %copy-done.21, bf16[2048,2048]{1,0:T(8,128)(2,1)} %all-gather.7.cloned.1.call-done.w_out), kind=kOutput, calls=%fused_computation.13 | convolution fusion | flops 4303355904 | bytes 16781312 | tf_op jit(solution)/shard_map/dot_general | solution.py:392
  199.4 22.2 %collective-permute-done.9 = bf16[512,1024]{1,0:T(8,128)(2,1)S(1)} collective-permute-done((bf16[512,1024]{1,0:T(8,128)(2,1)S(1)}, bf16[512,1024]{1,0:T(8,128)(2,1)S(1)}, u32[]{:S(2)}, u32[]{:S(2)}) %collective-permute-start.9) | collective-permute-done | bytes 1048608 | tf_op jit(solution)/shard_map/ppermute | solution.py:396
  228.0 10.4 %collective-permute-done.10 = bf16[256,1024]{1,0:T(8,128)(2,1)} collective-permute-done((bf16[256,1024]{1,0:T(8,128)(2,1)}, bf16[256,1024]{1,0:T(8,128)(2,1)}, u32[]{:S(2)}, u32[]{:S(2)}) %collective-permute-start.10) | collective-permute-done | bytes 524320 | tf_op jit(solution)/shard_map/ppermute | solution.py:396
  244.8 20.8 %collective-permute-done.13 = bf16[256,2048]{1,0:T(8,128)(2,1)S(1)} collective-permute-done((bf16[256,2048]{1,0:T(8,128)(2,1)S(1)}, bf16[256,2048]{1,0:T(8,128)(2,1)S(1)}, u32[]{:S(2)}, u32[]{:S(2)}) %collective-permute-start.13) | collective-permute-done | bytes 1048608 | tf_op jit(solution)/shard_map/ppermute | solution.py:396
  268.4 9.1 %collective-permute-done.14 = bf16[128,2048]{1,0:T(8,128)(2,1)S(1)} collective-permute-done((bf16[128,2048]{1,0:T(8,128)(2,1)S(1)}, bf16[128,2048]{1,0:T(8,128)(2,1)S(1)}, u32[]{:S(2)}, u32[]{:S(2)}) %collective-permute-start.14) | collective-permute-done | bytes 524320 | tf_op jit(solution)/shard_map/ppermute | solution.py:396
  288.9 17.2 %fusion.87 = f32[1024,2816]{1,0:T(8,128)S(1)} fusion(bf16[1024,2048]{1,0:T(8,128)(2,1)} %copy-done.31, bf16[2048,2816]{1,0:T(8,128)(2,1)} %all-gather.9.cloned.1.call-done), kind=kOutput, calls=%fused_computation.218 | convolution fusion | flops 11811160064 | bytes 27262976 | tf_op jit(solution)/shard_map/dot_general | solution.py:392
  311.9 10.7 %convolution_convert_fusion = bf16[1408,2048]{1,0:T(8,128)(2,1)} fusion(bf16[1024,1408]{1,0:T(8,128)(2,1)S(1)} %multiply_convert_fusion.2, bf16[1024,2048]{1,0:T(8,128)(2,1)} %constant_dynamic-update-slice_fusion.5), kind=kOutput, calls=%fused_computation.2 | convolution fusion | flops 5908463616 | bytes 12845056 | tf_op jit(solution)/shard_map/dot_general | solution.py:392
  322.7 27.4 %all-gather.11.cloned.1.call-done = bf16[1408,2048]{1,0:T(8,128)(2,1)} async-done(((bf16[1408,256]{1,0:T(8,128)(2,1)}), bf16[1408,2048]{1,0:T(8,128)(2,1)}) %all-gather.11.cloned.1.call-update) | async-done | bytes 5767184 | tf_op jit(solution)/shard_map/all_gather | solution.py:473
  350.0 14.2 %multiply_convert_fusion.1 = (bf16[1024,1408]{1,0:T(8,128)(2,1)S(1)}, bf16[1024,1408]{1,0:T(8,128)(2,1)S(1)}) fusion(f32[1024,2816]{1,0:T(8,128)} %copy-done.25, bf16[1024,2048]{1,0:T(8,128)(2,1)} %constant_dynamic-update-slice_fusion.5, bf16[1408,2048]{1,0:T(8,128)(2,1)} %all-gather.11.cloned.1.call-done), kind=kOutput, calls=%fused_computation.5 | convolution fusion | flops 5924323328 | bytes 27262976 | tf_op jit(solution)/shard_map/dot_general | solution.py:392
  365.5 8.8 %convolution_convert_fusion.1 = bf16[1024,2816]{1,0:T(8,128)(2,1)} fusion(bf16[1024,256]{1,0:T(8,128)(2,1)S(1)} %get-tuple-element.233, bf16[1024,256]{1,0:T(8,128)(2,1)S(1)} %get-tuple-element.234, bf16[1024,256]{1,0:T(8,128)(2,1)S(1)} %copy-done.49, bf16[1024,256]{1,0:T(8,128)(2,1)S(1)} %copy-done.50, bf16[1024,1408]{1,0:T(8,128)(2,1)S(1)} %get-tuple-element.199, ...), kind=kOutput, calls=%fused_computation.9 | convolution fusion | flops 5928386560 | bytes 13631488 | tf_op jit(solution)/shard_map/dot_general | solution.py:392
  374.6 15.0 %convolution_convert_fusion.2 = bf16[1024,2048]{1,0:T(8,128)(2,1)S(1)} fusion(bf16[1024,2816]{1,0:T(8,128)(2,1)S(1)} %pad_maximum_fusion, bf16[2048,2816]{1,0:T(8,128)(2,1)} %all-gather.9.cloned.1.call-done), kind=kOutput, calls=%fused_computation.27 | convolution fusion | flops 11813257216 | bytes 21495808 | tf_op jit(solution)/shard_map/dot_general | solution.py:392
  396.2 10.7 %add_convert_fusion = bf16[1024,2816]{1,0:T(8,128)(2,1)} fusion(bf16[1024,2816]{1,0:T(8,128)(2,1)} %collective-permute-done.16, bf16[1024,2816]{1,0:T(8,128)(2,1)S(1)} %pad_maximum_fusion, bf16[1024,256]{1,0:T(8,128)(2,1)S(1)} %copy-done.46, bf16[1024,256]{1,0:T(8,128)(2,1)S(1)} %copy-done.47, bf16[1024,256]{1,0:T(8,128)(2,1)S(1)} %copy-done.48, ...), kind=kOutput, calls=%fused_computation | convolution fusion | flops 5922619392 | bytes 19398656 | tf_op jit(solution)/shard_map/dot_general | solution.py:392
  406.8 11.9 %collective-permute-done.17 = bf16[512,1024]{1,0:T(8,128)(2,1)S(1)} collective-permute-done((bf16[512,1024]{1,0:T(8,128)(2,1)}, bf16[512,1024]{1,0:T(8,128)(2,1)S(1)}, u32[]{:S(2)}, u32[]{:S(2)}) %collective-permute-start.17) | collective-permute-done | bytes 1048608 | tf_op jit(solution)/shard_map/ppermute | solution.py:396
  428.0 11.1 %collective-permute-done.19 = bf16[256,1024]{1,0:T(8,128)(2,1)} collective-permute-done((bf16[256,1024]{1,0:T(8,128)(2,1)}, bf16[256,1024]{1,0:T(8,128)(2,1)}, u32[]{:S(2)}, u32[]{:S(2)}) %collective-permute-start.19) | collective-permute-done | bytes 524320 | tf_op jit(solution)/shard_map/ppermute | solution.py:396
  447.1 8.5 %convolution_convert_fusion.3 = bf16[1024,2048]{1,0:T(8,128)(2,1)} fusion(bf16[1024,1408]{1,0:T(8,128)(2,1)S(1)} %copy-done.39, bf16[1408,2048]{1,0:T(8,128)(2,1)S(1)} %bitcast.94), kind=kOutput, calls=%fused_computation.28 | convolution fusion | flops 5907677184 | bytes 12845056 | tf_op jit(solution)/shard_map/dot_general | solution.py:392
  455.6 13.3 %collective-permute-done.21 = bf16[256,2048]{1,0:T(8,128)(2,1)S(1)} collective-permute-done((bf16[256,2048]{1,0:T(8,128)(2,1)S(1)}, bf16[256,2048]{1,0:T(8,128)(2,1)S(1)}, u32[]{:S(2)}, u32[]{:S(2)}) %collective-permute-start.21) | collective-permute-done | bytes 1048608 | tf_op jit(solution)/shard_map/ppermute | solution.py:396
  519.0 58.9 %core_backward.1 = (bf16[1024,2048]{1,0:T(8,128)(2,1)S(1)}, f32[1024,8]{1,0:T(8,128)S(1)}, f32[4,2048]{1,0:T(4,128)S(1)}, f32[1,8]{1,0:T(1,128)S(1)}, f32[1,256]{1,0:T(1,128)S(1)}) custom-call(f32[1024,1024]{1,0:T(8,128)} %get-tuple-element.109.dn_in, f32[1024,2048]{1,0:T(8,128)} %fusion.85.pqkv, f32[1024,8]{1,0:T(8,128)S(1)} %copy-done.5, ...), custom_call_target="tpu_custom_call" | custom-call | flops 20000000000 | bytes 50331648 | tf_op jit(solution)/shard_map/core_backward/pallas_call | solution.py:331
  616.2 18.2 %projections_back.1 = (bf16[1024,2048]{1,0:T(8,128)(2,1)S(1)}, f32[1,2048]{1,0:T(1,128)S(1)}) custom-call(bf16[1024,2048]{1,0:T(8,128)(2,1)S(1)} %copy-done.8, bf16[1024,1024]{1,0:T(8,128)(2,1)S(1)} %get-tuple-element.200.dpo, bf16[1024,8]{1,0:T(8,128)(2,1)S(1)} %convert_element_type.271.dab, bf16[2048,2048]{1,0:T(8,128)(2,1)} %all-gather.5.cloned.1.call-done.w_qkv, ...), custom_call_target="tpu_custom_call" | custom-call | flops 12884901888 | bytes 33554432 | tf_op jit(solution)/shard_map/projections_back/pallas_call | solution.py:365
  656.2 9.1 %collective-permute-done.32 = bf16[512,1024]{1,0:T(8,128)(2,1)S(1)} collective-permute-done((bf16[512,1024]{1,0:T(8,128)(2,1)}, bf16[512,1024]{1,0:T(8,128)(2,1)S(1)}, u32[]{:S(2)}, u32[]{:S(2)}) %collective-permute-start.32) | collective-permute-done | bytes 1048608 | tf_op jit(solution)/shard_map/ppermute | solution.py:396
  (399 shorter events, 276.0 us)
Async XLA Ops:
  7.2 98.2 %all-gather.5.cloned.1.call-start = ((), (), s32[]{:S(2)}) async-start(), calls=%async_computation.5 | async-start | bytes 9437184 | tf_op jit(solution)/shard_map/all_gather | solution.py:473
  11.8 168.2 %all-gather.7.cloned.1.call-start = ((), (), s32[]{:S(2)}) async-start(), calls=%async_computation.6 | async-start | bytes 9437184 | tf_op jit(solution)/shard_map/all_gather | solution.py:473
  15.8 273.1 %all-gather.9.cloned.1.call-start = ((), (), s32[]{:S(2)}) async-start(), calls=%async_computation.7 | async-start | bytes 12976128 | tf_op jit(solution)/shard_map/all_gather | solution.py:473
  18.7 331.3 %all-gather.11.cloned.1.call-start = ((), (), s32[]{:S(2)}) async-start(), calls=%async_computation.8 | async-start | bytes 6488064 | tf_op jit(solution)/shard_map/all_gather | solution.py:473
  20.4 26.1 %collective-permute-start.1 = (bf16[256,2048]{1,0:T(8,128)(2,1)S(1)}, bf16[256,2048]{1,0:T(8,128)(2,1)S(1)}, u32[]{:S(2)}, u32[]{:S(2)}) collective-permute-start(bf16[256,2048]{1,0:T(8,128)(2,1)S(1)} %get-tuple-element.197), channel_id=1, source_target_pairs={{0,2},{1,3},{2,0},{3,1},{4,6},{5,7},{6,4},{7,5},{8,10},{9,11},{10,... | collective-permute-start | bytes 3145736 | tf_op jit(solution)/shard_map/ppermute | solution.py:396
  23.4 25.8 %collective-permute-start = (bf16[256,2048]{1,0:T(8,128)(2,1)S(1)}, bf16[256,2048]{1,0:T(8,128)(2,1)S(1)}, u32[]{:S(2)}, u32[]{:S(2)}) collective-permute-start(bf16[256,2048]{1,0:T(8,128)(2,1)S(1)} %get-tuple-element.197), channel_id=1, source_target_pairs={{0,1},{1,0},{2,3},{3,2},{4,5},{5,4},{6,7},{7,6},{8,9},{9,8},{10,11... | collective-permute-start | bytes 3145736 | tf_op jit(solution)/shard_map/ppermute | solution.py:396
  67.7 23.5 %collective-permute-start.5 = (bf16[256,2048]{1,0:T(8,128)(2,1)S(1)}, bf16[256,2048]{1,0:T(8,128)(2,1)S(1)}, u32[]{:S(2)}, u32[]{:S(2)}) collective-permute-start(bf16[256,2048]{1,0:T(8,128)(2,1)S(1)} %copy-done.36), channel_id=1, source_target_pairs={{0,2},{1,3},{2,0},{3,1},{4,6},{5,7},{6,4},{7,5},{8,10},{9,11},{10,... | collective-permute-start | bytes 3145736 | tf_op jit(solution)/shard_map/ppermute | solution.py:396
  69.2 24.3 %collective-permute-start.4 = (bf16[256,2048]{1,0:T(8,128)(2,1)S(1)}, bf16[256,2048]{1,0:T(8,128)(2,1)S(1)}, u32[]{:S(2)}, u32[]{:S(2)}) collective-permute-start(bf16[256,2048]{1,0:T(8,128)(2,1)S(1)} %copy-done.36), channel_id=1, source_target_pairs={{0,1},{1,0},{2,3},{3,2},{4,5},{5,4},{6,7},{7,6},{8,9},{9,8},{10,11... | collective-permute-start | bytes 3145736 | tf_op jit(solution)/shard_map/ppermute | solution.py:396
  196.3 25.3 %collective-permute-start.9 = (bf16[512,1024]{1,0:T(8,128)(2,1)S(1)}, bf16[512,1024]{1,0:T(8,128)(2,1)S(1)}, u32[]{:S(2)}, u32[]{:S(2)}) collective-permute-start(bf16[512,1024]{1,0:T(8,128)(2,1)S(1)} %pad_maximum_fusion.11), channel_id=1, source_target_pairs={{0,2},{1,3},{2,0},{3,1},{4,6},{5,7},{6,4},{7,5},{8,10},{9,11},{10,... | collective-permute-start | bytes 3145736 | tf_op jit(solution)/shard_map/ppermute | solution.py:396
  197.9 25.1 %collective-permute-start.8 = (bf16[512,1024]{1,0:T(8,128)(2,1)S(1)}, bf16[512,1024]{1,0:T(8,128)(2,1)S(1)}, u32[]{:S(2)}, u32[]{:S(2)}) collective-permute-start(bf16[512,1024]{1,0:T(8,128)(2,1)S(1)} %pad_maximum_fusion.10), channel_id=1, source_target_pairs={{0,1},{1,0},{2,3},{3,2},{4,5},{5,4},{6,7},{7,6},{8,9},{9,8},{10,11... | collective-permute-start | bytes 3145736 | tf_op jit(solution)/shard_map/ppermute | solution.py:396
  227.9 283.6 %reduce-scatter.5.cloned.1.call-start = ((), (), s32[]{:S(2)}) async-start(), calls=%async_computation.9 | async-start | bytes 6488064 | tf_op jit(solution)/shard_map/reduce_scatter | solution.py:494
  242.2 23.5 %collective-permute-start.13 = (bf16[256,2048]{1,0:T(8,128)(2,1)S(1)}, bf16[256,2048]{1,0:T(8,128)(2,1)S(1)}, u32[]{:S(2)}, u32[]{:S(2)}) collective-permute-start(bf16[256,2048]{1,0:T(8,128)(2,1)S(1)} %get-tuple-element.193), channel_id=1, source_target_pairs={{0,2},{1,3},{2,0},{3,1},{4,6},{5,7},{6,4},{7,5},{8,10},{9,11},{10,... | collective-permute-start | bytes 3145736 | tf_op jit(solution)/shard_map/ppermute | solution.py:396
  243.5 23.6 %collective-permute-start.12 = (bf16[256,2048]{1,0:T(8,128)(2,1)S(1)}, bf16[256,2048]{1,0:T(8,128)(2,1)S(1)}, u32[]{:S(2)}, u32[]{:S(2)}) collective-permute-start(bf16[256,2048]{1,0:T(8,128)(2,1)S(1)} %get-tuple-element.193), channel_id=1, source_target_pairs={{0,1},{1,0},{2,3},{3,2},{4,5},{5,4},{6,7},{7,6},{8,9},{9,8},{10,11... | collective-permute-start | bytes 3145736 | tf_op jit(solution)/shard_map/ppermute | solution.py:396
  322.6 257.3 %reduce-scatter.7.cloned.1.call-start = ((), (), s32[]{:S(2)}) async-start(), calls=%async_computation.10 | async-start | bytes 7208960 | tf_op jit(solution)/shard_map/reduce_scatter | solution.py:500
  393.2 25.5 %collective-permute-start.17 = (bf16[512,1024]{1,0:T(8,128)(2,1)}, bf16[512,1024]{1,0:T(8,128)(2,1)S(1)}, u32[]{:S(2)}, u32[]{:S(2)}) collective-permute-start(bf16[512,1024]{1,0:T(8,128)(2,1)} %pad_maximum_fusion.12), channel_id=1, source_target_pairs={{0,1},{1,0},{2,3},{3,2},{4,5},{5,4},{6,7},{7,6},{8,9},{9,8},{10,11... | collective-permute-start | bytes 3145736 | tf_op jit(solution)/shard_map/ppermute | solution.py:396
  394.7 25.3 %collective-permute-start.18 = (bf16[512,1024]{1,0:T(8,128)(2,1)}, bf16[512,1024]{1,0:T(8,128)(2,1)}, u32[]{:S(2)}, u32[]{:S(2)}) collective-permute-start(bf16[512,1024]{1,0:T(8,128)(2,1)} %concatenate.137), channel_id=1, source_target_pairs={{0,2},{1,3},{2,0},{3,1},{4,6},{5,7},{6,4},{7,5},{8,10},{9,11},{10,... | collective-permute-start | bytes 3145736 | tf_op jit(solution)/shard_map/ppermute | solution.py:396
  428.0 208.6 %reduce-scatter.9.cloned.1.call-start = ((), (), s32[]{:S(2)}) async-start(), calls=%async_computation.11 | async-start | bytes 5242880 | tf_op jit(solution)/shard_map/reduce_scatter | solution.py:500
  511.5 177.5 %reduce-scatter.11.cloned.1.call-start = ((), (), s32[]{:S(2)}) async-start(), calls=%async_computation.12 | async-start | bytes 5242880 | tf_op jit(solution)/shard_map/reduce_scatter | solution.py:500
  515.5 64.4 %collective-permute-start.23 = (bf16[256,2048]{1,0:T(8,128)(2,1)}, bf16[256,2048]{1,0:T(8,128)(2,1)}, u32[]{:S(2)}, u32[]{:S(2)}) collective-permute-start(bf16[256,2048]{1,0:T(8,128)(2,1)} %get-tuple-element.224), channel_id=1, source_target_pairs={{0,1},{1,0},{2,3},{3,2},{4,5},{5,4},{6,7},{7,6},{8,9},{9,8},{10,11... | collective-permute-start | bytes 3145736 | tf_op jit(solution)/shard_map/ppermute | solution.py:396
  516.2 63.7 %collective-permute-start.24 = (bf16[256,2048]{1,0:T(8,128)(2,1)}, bf16[256,2048]{1,0:T(8,128)(2,1)}, u32[]{:S(2)}, u32[]{:S(2)}) collective-permute-start(bf16[256,2048]{1,0:T(8,128)(2,1)} %get-tuple-element.223), channel_id=1, source_target_pairs={{0,2},{1,3},{2,0},{3,1},{4,6},{5,7},{6,4},{7,5},{8,10},{9,11},{10,... | collective-permute-start | bytes 3145736 | tf_op jit(solution)/shard_map/ppermute | solution.py:396
  516.6 63.3 %collective-permute-start.25 = (bf16[256,2048]{1,0:T(8,128)(2,1)}, bf16[256,2048]{1,0:T(8,128)(2,1)}, u32[]{:S(2)}, u32[]{:S(2)}) collective-permute-start(bf16[256,2048]{1,0:T(8,128)(2,1)} %get-tuple-element.222), channel_id=1, source_target_pairs={{0,3},{1,2},{2,1},{3,0},{4,7},{5,6},{6,5},{7,4},{8,11},{9,10},{10,... | collective-permute-start | bytes 3145736 | tf_op jit(solution)/shard_map/ppermute | solution.py:396
  610.3 45.2 %all-to-all-start = ((f32[8,12,256]{2,1,0:T(8,128)}), f32[8,12,256]{2,1,0:T(8,128)S(1)}, u32[]{:S(2)}, u32[]{:S(2)}) async-start(f32[8,12,256]{2,1,0:T(8,128)} %pad_maximum_fusion.15), calls=%async_computation.4 | async-start | bytes 262144 | tf_op jit(solution)/shard_map/all_to_all | solution.py:622
  639.9 25.4 %collective-permute-start.32 = (bf16[512,1024]{1,0:T(8,128)(2,1)}, bf16[512,1024]{1,0:T(8,128)(2,1)S(1)}, u32[]{:S(2)}, u32[]{:S(2)}) collective-permute-start(bf16[512,1024]{1,0:T(8,128)(2,1)} %pad_maximum_fusion.14), channel_id=1, source_target_pairs={{0,2},{1,3},{2,0},{3,1},{4,6},{5,7},{6,4},{7,5},{8,10},{9,11},{10,... | collective-permute-start | bytes 3145736 | tf_op jit(solution)/shard_map/ppermute | solution.py:396
  641.6 25.1 %collective-permute-start.31 = (bf16[512,1024]{1,0:T(8,128)(2,1)}, bf16[512,1024]{1,0:T(8,128)(2,1)S(1)}, u32[]{:S(2)}, u32[]{:S(2)}) collective-permute-start(bf16[512,1024]{1,0:T(8,128)(2,1)} %pad_maximum_fusion.13), channel_id=1, source_target_pairs={{0,1},{1,0},{2,3},{3,2},{4,5},{5,4},{6,7},{7,6},{8,9},{9,8},{10,11... | collective-permute-start | bytes 3145736 | tf_op jit(solution)/shard_map/ppermute | solution.py:396
  (101 other events, 1165.3 us)
Sparse Core Ops, SparseCore 0:
  11.9 85.1 all-gather.4
  99.3 80.6 all-gather.6
  182.2 106.5 all-gather.8
  290.9 59.1 all-gather.10
  352.2 63.0 reduce-scatter.4
  428.1 99.5 reduce-scatter.6
  529.9 77.2 reduce-scatter.8
  609.6 79.3 reduce-scatter.10

commit v5 on v4

--- a/solution.py
+++ b/solution.py
@@ -30,10 +30,10 @@
     return high, (a - high.astype(F32)).astype(BF16)
 
 
-def mm_split(a, b):
+def mm_split(a, b, dims=NN):
     a_high, a_low = halves(a)
     b_high, b_low = halves(b)
-    return mm(a_high, b_high) + (mm(a_high, b_low) + mm(a_low, b_high))
+    return mm(a_high, b_high, dims) + (mm(a_high, b_low, dims) + mm(a_low, b_high, dims))
 
 
 def sigmoid(x):
@@ -122,29 +122,29 @@
         vs.append(uv * sigmoid(uv))
         bs.append(beta[:, h : h + 1])
     for h in range(heads):
-        prods.append(mm(jnp.concatenate([ks[h], qs[h]], 0), ks[h], NT))
+        prods.append(mm_split(jnp.concatenate([ks[h], qs[h]], 0), ks[h], NT))
     for h in range(heads):
         differ = jnp.minimum(c_col[:, h : h + 1] - c_row[h : h + 1, :], 0.0)
         relatives.append(jnp.where(row >= col, jnp.exp(differ), 0.0))
         lowers.append(jnp.where(row > col, bs[h] * relatives[h] * prods[h][:GROUP], 0.0))
-    invs = [inverse.astype(BF16) for inverse in unit_lower_inverses(lowers, row, col)]
+    invs = [inverse for inverse in unit_lower_inverses(lowers, row, col)]
     states = [state[h] for h in range(heads)]
-    lows = [s.astype(BF16) for s in states]
+    lows = states
     reads = []
     for h in range(heads):
         e = start_decay[:, h : h + 1]
-        reads.append(mm(jnp.concatenate([ks[h] * e, qs[h] * e], 0), lows[h]))
-    us = [mm(invs[h], bs[h] * (vs[h] - reads[h][:GROUP])).astype(BF16) for h in range(heads)]
-    outs = [reads[h][GROUP:] + mm(relatives[h] * prods[h][GROUP:], us[h]) for h in range(heads)]
+        reads.append(mm_split(jnp.concatenate([ks[h] * e, qs[h] * e], 0), lows[h]))
+    us = [mm_split(invs[h], bs[h] * (vs[h] - reads[h][:GROUP])) for h in range(heads)]
+    outs = [reads[h][GROUP:] + mm_split(relatives[h] * prods[h][GROUP:], us[h]) for h in range(heads)]
     nexts = [
-        last_decay[:, h : h + 1] * states[h] + mm(ks[h] * end_decay[:, h : h + 1], us[h], TN) for h in range(heads)
+        last_decay[:, h : h + 1] * states[h] + mm_split(ks[h] * end_decay[:, h : h + 1], us[h], TN) for h in range(heads)
     ]
     for h in range(heads):
         cols = slice(h * dv, (h + 1) * dv)
         state[h] = nexts[h]
-        t_out[0, h] = invs[h]
-        s_out[0, h] = lows[h]
-        u_out[:, cols] = us[h]
+        t_out[0, h] = invs[h].astype(t_out.dtype)
+        s_out[0, h] = lows[h].astype(s_out.dtype)
+        u_out[:, cols] = us[h].astype(u_out.dtype)
         o = outs[h]
         norm = lax.rsqrt(jnp.mean(o * o, -1, keepdims=True) + 1e-5)
         n_out[:, cols] = (o * norm).astype(n_out.dtype)
@@ -260,14 +260,16 @@
         ds_low = ds.astype(BF16)
         dob = do.astype(BF16)
         ke, qe, kd = k * e, qs * e, k * f
-        du = mm(mix, dob, TN) + mm(kd, ds_low)
-        dr = mm(inv, du, TN)
+        du = mm_split(mix, do, TN) + mm_split(kd, ds)
+        du_hi, du_lo = halves(du)
+        dr = mm(inv, du_hi, TN) + mm(inv, du_lo, TN)
         pair = jnp.concatenate([dob, dr.astype(BF16)], 0)
         dstate[h] = last_decay[:, h : h + 1] * ds + mm(jnp.concatenate([qe, -(b * ke)], 0), pair, TN)
-        cross = mm(pair, u, NT)
+        rest = jnp.concatenate([halves(do)[1], halves(dr)[1]], 0)
+        cross = mm(pair, u, NT) + mm(rest, u, NT)
         dmix = jnp.where(row >= col, cross[:GROUP], 0.0)
         dlow = jnp.where(row > col, -cross[GROUP:], 0.0)
-        back = mm(pair, s_prev, NT)
+        back = mm(pair, s_prev, NT) + mm(rest, s_prev, NT)
         dqe, x = back[:GROUP], back[GROUP:]
         dkd = mm(u, ds_low, NT)
         dke = -(b * x)
@@ -384,6 +386,50 @@
     )(dqkv, dpo, dab, w_qkv, w_out, w_ab, normed)
 
 
+def side_by_side_kernel(*refs):
+    *parts, out = refs
+    at = 0
+    for part in parts:
+        out[:, at : at + part.shape[1]] = part[...].astype(out.dtype)
+        at += part.shape[1]
+
+
+def side_by_side(*parts):
+    rows = parts[0].shape[0]
+    step = rows // 4
+    width = sum(a.shape[1] for a in parts)
+    band = lambda columns: pl.BlockSpec((step, columns), lambda n: (n, 0))
+    return pl.pallas_call(
+        side_by_side_kernel,
+        grid=(4,),
+        in_specs=[band(a.shape[1]) for a in parts],
+        out_specs=band(width),
+        out_shape=jax.ShapeDtypeStruct((rows, width), BF16),
+        name="side_by_side",
+    )(*parts)
+
+
+def apart_kernel(whole, *outs):
+    at = 0
+    for out in outs:
+        out[...] = whole[:, at : at + out.shape[1]].astype(out.dtype)
+        at += out.shape[1]
+
+
+def apart(whole, *widths):
+    rows = whole.shape[0]
+    step = rows // 4
+    band = lambda columns: pl.BlockSpec((step, columns), lambda n: (n, 0))
+    return pl.pallas_call(
+        apart_kernel,
+        grid=(4,),
+        in_specs=[band(whole.shape[1])],
+        out_specs=[band(width) for width in widths],
+        out_shape=[jax.ShapeDtypeStruct((rows, width), F32) for width in widths],
+        name="apart",
+    )(whole)
+
+
 def rms_norm(values, gain_vec):
     return values * lax.rsqrt(jnp.mean(values * values, -1, keepdims=True) + 1e-05) * gain_vec
 
@@ -488,10 +534,6 @@
         )
 
     return pick(core), pick(1 - core)
-
-
-def scatter_dp(part, axis):
-    return lax.psum_scatter(part, "dp", scatter_dimension=axis, tiled=True)
 
 
 def scatter_chips(part, axis):
@@ -544,7 +586,7 @@
         [unroll(pieces[:, :, : cut[0]]), unroll(pieces[:, :, cut[0] : cut[1]]), unroll(pieces[:, :, cut[1] :])], 1
     ).astype(F32)
 
-    full_qkv = gather_dp(jnp.concatenate([w_query, w_key, w_value], 1), 0)
+    full_qkv = gather_dp(side_by_side(w_query, w_key, w_value), 0)
     full_gate_out = gather_dp(jnp.concatenate([w_outgate, w_output.T], 1), 0)
     full_outgate, full_output = full_gate_out[:, :vals], full_gate_out[:, vals:]
     full_pair = gather_dp(jnp.concatenate([w_gate, w_up], 1), 0)
@@ -570,7 +612,7 @@
     gate_sig = jax.nn.sigmoid(gate_pre)
     activ = (gate_pre * gate_sig * up_pre).astype(BF16)
     cot, part_down = hold((cot, dot(activ, cot, TN).astype(BF16)))
-    grad_w_down = scatter_dp(part_down, 1)
+    grad_w_down = lax.psum_scatter(part_down, "dp", scatter_dimension=1, tiled=True)
     grad_activ = dot(cot, full_down, NT)
     grad_gate_pre = (grad_activ * up_pre * gate_sig * (1.0 + gate_pre * (1.0 - gate_sig))).astype(BF16)
     grad_up_pre = (grad_activ * (gate_pre * gate_sig)).astype(BF16)
@@ -643,14 +685,15 @@
     grad_in = (grad_middle + grad_rows).astype(BF16)
     ends = [model, 2 * model, 2 * model + head_gain.shape[0], 2 * model + head_gain.shape[0] + log_rate.shape[0]]
     grad_mix_gain, grad_ffn_gain, grad_head_gain, grad_log_rate, grad_decay_bias = jnp.split(sums, ends)
-    grad_qkv, grad_gate_out, grad_pair = grad_qkv.astype(F32), grad_gate_out.astype(F32), grad_pair.astype(F32)
+    grad_w_query, grad_w_key, grad_w_value = apart(grad_qkv, keys, keys, vals)
+    grad_gate_out, grad_pair = grad_gate_out.astype(F32), grad_pair.astype(F32)
     return (
         hidden_out,
         grad_in,
         grad_mix_gain,
-        grad_qkv[:, :keys],
-        grad_qkv[:, keys : 2 * keys],
-        grad_qkv[:, 2 * keys :],
+        grad_w_query,
+        grad_w_key,
+        grad_w_value,
         grad_kernels[:, : cut[0]],
         grad_kernels[:, cut[0] : cut[1]],
         grad_kernels[:, cut[1] :],

time: 705 us -> 704 us (level)
  Pallas kernels: 119 us -> 136 us
    pallas_call x0 -> x2, Pallas kernels: none -> 7.17 us  [the longest x1 3.63 us: side_by_side(): pl.pallas_call(side_by_side_kernel, grid=(4,), in_specs=[band(a.shape[1])...]
  transfers between devices with their start and end apart: 49 -> 49, of which waited for: 31 -> 31; matrix products, arithmetic and copies ran while one was open for 34% -> 34% of each run, Pallas kernels for 17% -> 18%
where the time goes in v5:
time: 704 us; the launch traced here: 700 us
  waiting for transfers between devices  224 us (32%)
  matrix products  152 us (22%)
  Pallas kernels  136 us (19%)
  local copies, waits for them, and re-layouts  59.6 us (8%)
  starting transfers between devices  49.6 us (7%)
  other arithmetic  48.4 us (7%)
  between operations  15.7 us (2%)
  blocking collectives  14.6 us (2%)
    ppermute x31, waiting for transfers between devices, swap(): return lax.ppermute(piece, 'tensor', [(i, i ^ mask) for i in range(4)])  160 us
    dot_general x19, matrix products, dot(): return lax.dot_general(a, b, (dims, ((), ())), preferred_element_type=F32)  152 us
    pallas_call x1, Pallas kernels, core_backward(): pl.pallas_call(backward_kernel, grid=(blocks,), in_specs=[tokens(a.shape[...  63.2 us
    pallas_call x1, Pallas kernels, core_forward(): pl.pallas_call(forward_kernel, grid=(blocks,), in_specs=[tokens(a.shape[1...  47.7 us
    all_gather x4, waiting for transfers between devices, gather_dp(): return lax.all_gather(shard.astype(BF16), 'dp', axis=axis, tiled=True)  40.5 us
    ppermute x31, starting transfers between devices, swap(): return lax.ppermute(piece, 'tensor', [(i, i ^ mask) for i in range(4)])  39.6 us
    unnamed x172, local copies, waits for them, and re-layouts  36.1 us
    pallas_call x1, Pallas kernels, projections_back(): pl.pallas_call(projections_kernel, grid=(model // tile,), in_specs=[whole...  18 us
  transfers between devices with their start and end apart: 49, of which 31 were waited for; matrix products, arithmetic and copies ran while one was open for 34% of the time, Pallas kernels for 18%

profile of v5, /device:TPU:0, one launch (start us, length us, event | category | flops | bytes accessed | tf_op | source)
XLA Modules:
  0.0 700.2 jit_solution(11545647366795122001)
XLA Ops:
  24.2 14.6 %all_gather.17 = bf16[8,12,256]{2,1,0:T(8,128)(2,1)S(1)} all-gather(bf16[1,12,256]{2,1,0:T(8,128)(2,1)S(1)} %pad_maximum_fusion.16), channel_id=1, replica_groups=mesh['dp'=8,'tensor'=4] {'dp'}, dimensions={0}, use_global_device_ids=true | all-gather | bytes 55296 | tf_op jit(solution)/shard_map/all_gather | solution.py:580
  74.0 16.3 %collective-permute-done.5 = bf16[256,2048]{1,0:T(8,128)(2,1)S(1)} collective-permute-done((bf16[256,2048]{1,0:T(8,128)(2,1)S(1)}, bf16[256,2048]{1,0:T(8,128)(2,1)S(1)}, u32[]{:S(2)}, u32[]{:S(2)}) %collective-permute-start.5) | collective-permute-done | bytes 1048608 | tf_op jit(solution)/shard_map/ppermute | solution.py:442
  104.5 15.4 %fusion.84.pqkv = f32[1024,2048]{1,0:T(8,128)} fusion(bf16[1024,2048]{1,0:T(8,128)(2,1)} %copy-done.21, bf16[2048,2048]{1,0:T(8,128)(2,1)} %all-gather.5.cloned.1.call-done.w_qkv), kind=kOutput, calls=%fused_computation.214 | convolution fusion | flops 8589934592 | bytes 20971520 | tf_op jit(solution)/shard_map/dot_general | solution.py:438
  119.9 47.7 %core_forward.1 = (bf16[1024,1024]{1,0:T(8,128)(2,1)S(1)}, f32[1024,4]{1,0:T(8,128)S(1)}, f32[1024,2048]{1,0:T(8,128)}, bf16[1024,1024]{1,0:T(8,128)(2,1)S(1)}, ...) custom-call(f32[1024,2048]{1,0:T(8,128)} %fusion.84.pqkv, f32[1024,8]{1,0:T(8,128)S(1)} %fusion.85.pab, ...), custom_call_target="tpu_custom_call" | custom-call | flops 8000000000 | bytes 33554432 | tf_op jit(solution)/shard_map/core_forward/pallas_call | solution.py:162
  179.1 10.7 %fusion.2 = (bf16[1024,1024]{1,0:T(8,128)(2,1)S(1)}, f32[1024,1024]{1,0:T(8,128)}) fusion(bf16[1024,1024]{1,0:T(8,128)(2,1)S(1)} %get-tuple-element.89.n_in, f32[1024]{0:T(1024)S(1)} %bitcast.89, bf16[1024,2048]{1,0:T(8,128)(2,1)} %copy-done.21, bf16[2048,2048]{1,0:T(8,128)(2,1)} %all-gather.7.cloned.1.call-done.w_out), kind=kOutput, calls=%fused_computation.13 | convolution fusion | flops 4303355904 | bytes 16781312 | tf_op jit(solution)/shard_map/dot_general | solution.py:438
  198.5 22.2 %collective-permute-done.9 = bf16[512,1024]{1,0:T(8,128)(2,1)S(1)} collective-permute-done((bf16[512,1024]{1,0:T(8,128)(2,1)S(1)}, bf16[512,1024]{1,0:T(8,128)(2,1)S(1)}, u32[]{:S(2)}, u32[]{:S(2)}) %collective-permute-start.9) | collective-permute-done | bytes 1048608 | tf_op jit(solution)/shard_map/ppermute | solution.py:442
  227.0 10.4 %collective-permute-done.10 = bf16[256,1024]{1,0:T(8,128)(2,1)} collective-permute-done((bf16[256,1024]{1,0:T(8,128)(2,1)}, bf16[256,1024]{1,0:T(8,128)(2,1)}, u32[]{:S(2)}, u32[]{:S(2)}) %collective-permute-start.10) | collective-permute-done | bytes 524320 | tf_op jit(solution)/shard_map/ppermute | solution.py:442
  243.9 20.7 %collective-permute-done.13 = bf16[256,2048]{1,0:T(8,128)(2,1)S(1)} collective-permute-done((bf16[256,2048]{1,0:T(8,128)(2,1)S(1)}, bf16[256,2048]{1,0:T(8,128)(2,1)S(1)}, u32[]{:S(2)}, u32[]{:S(2)}) %collective-permute-start.13) | collective-permute-done | bytes 1048608 | tf_op jit(solution)/shard_map/ppermute | solution.py:442
  267.5 9.1 %collective-permute-done.14 = bf16[128,2048]{1,0:T(8,128)(2,1)S(1)} collective-permute-done((bf16[128,2048]{1,0:T(8,128)(2,1)S(1)}, bf16[128,2048]{1,0:T(8,128)(2,1)S(1)}, u32[]{:S(2)}, u32[]{:S(2)}) %collective-permute-start.14) | collective-permute-done | bytes 524320 | tf_op jit(solution)/shard_map/ppermute | solution.py:442
  287.9 17.2 %fusion.86 = f32[1024,2816]{1,0:T(8,128)S(1)} fusion(bf16[1024,2048]{1,0:T(8,128)(2,1)} %copy-done.31, bf16[2048,2816]{1,0:T(8,128)(2,1)} %all-gather.9.cloned.1.call-done), kind=kOutput, calls=%fused_computation.216 | convolution fusion | flops 11811160064 | bytes 27262976 | tf_op jit(solution)/shard_map/dot_general | solution.py:438
  310.9 10.7 %convolution_convert_fusion = bf16[1408,2048]{1,0:T(8,128)(2,1)} fusion(bf16[1024,1408]{1,0:T(8,128)(2,1)S(1)} %multiply_convert_fusion.2, bf16[1024,2048]{1,0:T(8,128)(2,1)} %constant_dynamic-update-slice_fusion.5), kind=kOutput, calls=%fused_computation.2 | convolution fusion | flops 5908463616 | bytes 12845056 | tf_op jit(solution)/shard_map/dot_general | solution.py:438
  321.8 27.4 %all-gather.11.cloned.1.call-done = bf16[1408,2048]{1,0:T(8,128)(2,1)} async-done(((bf16[1408,256]{1,0:T(8,128)(2,1)}), bf16[1408,2048]{1,0:T(8,128)(2,1)}) %all-gather.11.cloned.1.call-update) | async-done | bytes 5767184 | tf_op jit(solution)/shard_map/all_gather | solution.py:519
  349.1 14.2 %multiply_convert_fusion.1 = (bf16[1024,1408]{1,0:T(8,128)(2,1)S(1)}, bf16[1024,1408]{1,0:T(8,128)(2,1)S(1)}) fusion(f32[1024,2816]{1,0:T(8,128)} %copy-done.25, bf16[1024,2048]{1,0:T(8,128)(2,1)} %constant_dynamic-update-slice_fusion.5, bf16[1408,2048]{1,0:T(8,128)(2,1)} %all-gather.11.cloned.1.call-done), kind=kOutput, calls=%fused_computation.5 | convolution fusion | flops 5924323328 | bytes 27262976 | tf_op jit(solution)/shard_map/dot_general | solution.py:438
  364.6 8.8 %convolution_convert_fusion.1 = bf16[1024,2816]{1,0:T(8,128)(2,1)} fusion(bf16[1024,256]{1,0:T(8,128)(2,1)S(1)} %get-tuple-element.239, bf16[1024,256]{1,0:T(8,128)(2,1)S(1)} %get-tuple-element.240, bf16[1024,256]{1,0:T(8,128)(2,1)S(1)} %copy-done.49, bf16[1024,256]{1,0:T(8,128)(2,1)S(1)} %copy-done.50, bf16[1024,1408]{1,0:T(8,128)(2,1)S(1)} %get-tuple-element.205, ...), kind=kOutput, calls=%fused_computation.9 | convolution fusion | flops 5928386560 | bytes 13631488 | tf_op jit(solution)/shard_map/dot_general | solution.py:438
  373.7 15.0 %convolution_convert_fusion.2 = bf16[1024,2048]{1,0:T(8,128)(2,1)S(1)} fusion(bf16[1024,2816]{1,0:T(8,128)(2,1)S(1)} %pad_maximum_fusion, bf16[2048,2816]{1,0:T(8,128)(2,1)} %all-gather.9.cloned.1.call-done), kind=kOutput, calls=%fused_computation.27 | convolution fusion | flops 11813257216 | bytes 21495808 | tf_op jit(solution)/shard_map/dot_general | solution.py:438
  395.3 10.7 %add_convert_fusion = bf16[1024,2816]{1,0:T(8,128)(2,1)} fusion(bf16[1024,2816]{1,0:T(8,128)(2,1)} %collective-permute-done.16, bf16[1024,2816]{1,0:T(8,128)(2,1)S(1)} %pad_maximum_fusion, bf16[1024,256]{1,0:T(8,128)(2,1)S(1)} %copy-done.46, bf16[1024,256]{1,0:T(8,128)(2,1)S(1)} %copy-done.47, bf16[1024,256]{1,0:T(8,128)(2,1)S(1)} %copy-done.48, ...), kind=kOutput, calls=%fused_computation | convolution fusion | flops 5922619392 | bytes 19398656 | tf_op jit(solution)/shard_map/dot_general | solution.py:438
  405.9 11.9 %collective-permute-done.17 = bf16[512,1024]{1,0:T(8,128)(2,1)S(1)} collective-permute-done((bf16[512,1024]{1,0:T(8,128)(2,1)}, bf16[512,1024]{1,0:T(8,128)(2,1)S(1)}, u32[]{:S(2)}, u32[]{:S(2)}) %collective-permute-start.17) | collective-permute-done | bytes 1048608 | tf_op jit(solution)/shard_map/ppermute | solution.py:442
  427.1 11.1 %collective-permute-done.19 = bf16[256,1024]{1,0:T(8,128)(2,1)} collective-permute-done((bf16[256,1024]{1,0:T(8,128)(2,1)}, bf16[256,1024]{1,0:T(8,128)(2,1)}, u32[]{:S(2)}, u32[]{:S(2)}) %collective-permute-start.19) | collective-permute-done | bytes 524320 | tf_op jit(solution)/shard_map/ppermute | solution.py:442
  446.2 8.5 %convolution_convert_fusion.3 = bf16[1024,2048]{1,0:T(8,128)(2,1)} fusion(bf16[1024,1408]{1,0:T(8,128)(2,1)S(1)} %copy-done.39, bf16[1408,2048]{1,0:T(8,128)(2,1)S(1)} %bitcast.94), kind=kOutput, calls=%fused_computation.28 | convolution fusion | flops 5907677184 | bytes 12845056 | tf_op jit(solution)/shard_map/dot_general | solution.py:438
  454.7 13.3 %collective-permute-done.21 = bf16[256,2048]{1,0:T(8,128)(2,1)S(1)} collective-permute-done((bf16[256,2048]{1,0:T(8,128)(2,1)S(1)}, bf16[256,2048]{1,0:T(8,128)(2,1)S(1)}, u32[]{:S(2)}, u32[]{:S(2)}) %collective-permute-start.21) | collective-permute-done | bytes 1048608 | tf_op jit(solution)/shard_map/ppermute | solution.py:442
  470.9 8.4 %collective-permute-done.26 = bf16[128,2048]{1,0:T(8,128)(2,1)S(1)} collective-permute-done((bf16[128,2048]{1,0:T(8,128)(2,1)S(1)}, bf16[128,2048]{1,0:T(8,128)(2,1)S(1)}, u32[]{:S(2)}, u32[]{:S(2)}) %collective-permute-start.26) | collective-permute-done | bytes 524320 | tf_op jit(solution)/shard_map/ppermute | solution.py:442
  518.1 63.2 %core_backward.1 = (bf16[1024,2048]{1,0:T(8,128)(2,1)S(1)}, f32[1024,8]{1,0:T(8,128)S(1)}, f32[4,2048]{1,0:T(4,128)S(1)}, f32[1,8]{1,0:T(1,128)S(1)}, f32[1,256]{1,0:T(1,128)S(1)}) custom-call(f32[1024,1024]{1,0:T(8,128)} %get-tuple-element.112.dn_in, f32[1024,2048]{1,0:T(8,128)} %fusion.84.pqkv, f32[1024,8]{1,0:T(8,128)S(1)} %copy-done.5, ...), custom_call_target="tpu_custom_call" | custom-call | flops 20000000000 | bytes 50331648 | tf_op jit(solution)/shard_map/core_backward/pallas_call | solution.py:333
  619.4 18.0 %projections_back.1 = (bf16[1024,2048]{1,0:T(8,128)(2,1)S(1)}, f32[1,2048]{1,0:T(1,128)S(1)}) custom-call(bf16[1024,2048]{1,0:T(8,128)(2,1)S(1)} %copy-done.8, bf16[1024,1024]{1,0:T(8,128)(2,1)S(1)} %get-tuple-element.206.dpo, bf16[1024,8]{1,0:T(8,128)(2,1)S(1)} %convert_element_type.267.dab, bf16[2048,2048]{1,0:T(8,128)(2,1)} %all-gather.5.cloned.1.call-done.w_qkv, ...), custom_call_target="tpu_custom_call" | custom-call | flops 12884901888 | bytes 33554432 | tf_op jit(solution)/shard_map/projections_back/pallas_call | solution.py:367
  676.1 8.5 %collective-permute-done.39 = f32[4384]{0:T(1024)S(1)} collective-permute-done((f32[4384]{0:T(1024)S(1)}, f32[4384]{0:T(1024)S(1)}, u32[]{:S(2)}, u32[]{:S(2)}) %collective-permute-start.39) | collective-permute-done | bytes 17568 | tf_op jit(solution)/shard_map/ppermute | solution.py:495
  (395 shorter events, 270.5 us)
Async XLA Ops:
  7.2 97.3 %all-gather.5.cloned.1.call-start = ((), (), s32[]{:S(2)}) async-start(), calls=%async_computation.5 | async-start | bytes 9437184 | tf_op jit(solution)/shard_map/all_gather | solution.py:519
  10.9 168.2 %all-gather.7.cloned.1.call-start = ((), (), s32[]{:S(2)}) async-start(), calls=%async_computation.6 | async-start | bytes 9437184 | tf_op jit(solution)/shard_map/all_gather | solution.py:519
  14.9 273.1 %all-gather.9.cloned.1.call-start = ((), (), s32[]{:S(2)}) async-start(), calls=%async_computation.7 | async-start | bytes 12976128 | tf_op jit(solution)/shard_map/all_gather | solution.py:519
  17.8 331.3 %all-gather.11.cloned.1.call-start = ((), (), s32[]{:S(2)}) async-start(), calls=%async_computation.8 | async-start | bytes 6488064 | tf_op jit(solution)/shard_map/all_gather | solution.py:519
  19.5 26.1 %collective-permute-start.1 = (bf16[256,2048]{1,0:T(8,128)(2,1)S(1)}, bf16[256,2048]{1,0:T(8,128)(2,1)S(1)}, u32[]{:S(2)}, u32[]{:S(2)}) collective-permute-start(bf16[256,2048]{1,0:T(8,128)(2,1)S(1)} %get-tuple-element.203), channel_id=1, source_target_pairs={{0,2},{1,3},{2,0},{3,1},{4,6},{5,7},{6,4},{7,5},{8,10},{9,11},{10,... | collective-permute-start | bytes 3145736 | tf_op jit(solution)/shard_map/ppermute | solution.py:442
  22.5 25.8 %collective-permute-start = (bf16[256,2048]{1,0:T(8,128)(2,1)S(1)}, bf16[256,2048]{1,0:T(8,128)(2,1)S(1)}, u32[]{:S(2)}, u32[]{:S(2)}) collective-permute-start(bf16[256,2048]{1,0:T(8,128)(2,1)S(1)} %get-tuple-element.203), channel_id=1, source_target_pairs={{0,1},{1,0},{2,3},{3,2},{4,5},{5,4},{6,7},{7,6},{8,9},{9,8},{10,11... | collective-permute-start | bytes 3145736 | tf_op jit(solution)/shard_map/ppermute | solution.py:442
  66.8 23.5 %collective-permute-start.5 = (bf16[256,2048]{1,0:T(8,128)(2,1)S(1)}, bf16[256,2048]{1,0:T(8,128)(2,1)S(1)}, u32[]{:S(2)}, u32[]{:S(2)}) collective-permute-start(bf16[256,2048]{1,0:T(8,128)(2,1)S(1)} %copy-done.36), channel_id=1, source_target_pairs={{0,2},{1,3},{2,0},{3,1},{4,6},{5,7},{6,4},{7,5},{8,10},{9,11},{10,... | collective-permute-start | bytes 3145736 | tf_op jit(solution)/shard_map/ppermute | solution.py:442
  68.3 24.3 %collective-permute-start.4 = (bf16[256,2048]{1,0:T(8,128)(2,1)S(1)}, bf16[256,2048]{1,0:T(8,128)(2,1)S(1)}, u32[]{:S(2)}, u32[]{:S(2)}) collective-permute-start(bf16[256,2048]{1,0:T(8,128)(2,1)S(1)} %copy-done.36), channel_id=1, source_target_pairs={{0,1},{1,0},{2,3},{3,2},{4,5},{5,4},{6,7},{7,6},{8,9},{9,8},{10,11... | collective-permute-start | bytes 3145736 | tf_op jit(solution)/shard_map/ppermute | solution.py:442
  195.3 25.4 %collective-permute-start.9 = (bf16[512,1024]{1,0:T(8,128)(2,1)S(1)}, bf16[512,1024]{1,0:T(8,128)(2,1)S(1)}, u32[]{:S(2)}, u32[]{:S(2)}) collective-permute-start(bf16[512,1024]{1,0:T(8,128)(2,1)S(1)} %pad_maximum_fusion.10), channel_id=1, source_target_pairs={{0,2},{1,3},{2,0},{3,1},{4,6},{5,7},{6,4},{7,5},{8,10},{9,11},{10,... | collective-permute-start | bytes 3145736 | tf_op jit(solution)/shard_map/ppermute | solution.py:442
  197.0 25.1 %collective-permute-start.8 = (bf16[512,1024]{1,0:T(8,128)(2,1)S(1)}, bf16[512,1024]{1,0:T(8,128)(2,1)S(1)}, u32[]{:S(2)}, u32[]{:S(2)}) collective-permute-start(bf16[512,1024]{1,0:T(8,128)(2,1)S(1)} %pad_maximum_fusion.9), channel_id=1, source_target_pairs={{0,1},{1,0},{2,3},{3,2},{4,5},{5,4},{6,7},{7,6},{8,9},{9,8},{10,11... | collective-permute-start | bytes 3145736 | tf_op jit(solution)/shard_map/ppermute | solution.py:442
  226.9 283.7 %reduce-scatter.5.cloned.1.call-start = ((), (), s32[]{:S(2)}) async-start(), calls=%async_computation.9 | async-start | bytes 6488064 | tf_op jit(solution)/shard_map/reduce_scatter | solution.py:615
  241.2 23.4 %collective-permute-start.13 = (bf16[256,2048]{1,0:T(8,128)(2,1)S(1)}, bf16[256,2048]{1,0:T(8,128)(2,1)S(1)}, u32[]{:S(2)}, u32[]{:S(2)}) collective-permute-start(bf16[256,2048]{1,0:T(8,128)(2,1)S(1)} %get-tuple-element.199), channel_id=1, source_target_pairs={{0,2},{1,3},{2,0},{3,1},{4,6},{5,7},{6,4},{7,5},{8,10},{9,11},{10,... | collective-permute-start | bytes 3145736 | tf_op jit(solution)/shard_map/ppermute | solution.py:442
  242.5 23.7 %collective-permute-start.12 = (bf16[256,2048]{1,0:T(8,128)(2,1)S(1)}, bf16[256,2048]{1,0:T(8,128)(2,1)S(1)}, u32[]{:S(2)}, u32[]{:S(2)}) collective-permute-start(bf16[256,2048]{1,0:T(8,128)(2,1)S(1)} %get-tuple-element.199), channel_id=1, source_target_pairs={{0,1},{1,0},{2,3},{3,2},{4,5},{5,4},{6,7},{7,6},{8,9},{9,8},{10,11... | collective-permute-start | bytes 3145736 | tf_op jit(solution)/shard_map/ppermute | solution.py:442
  321.7 261.6 %reduce-scatter.7.cloned.1.call-start = ((), (), s32[]{:S(2)}) async-start(), calls=%async_computation.10 | async-start | bytes 7208960 | tf_op jit(solution)/shard_map/reduce_scatter | solution.py:542
  392.3 25.5 %collective-permute-start.17 = (bf16[512,1024]{1,0:T(8,128)(2,1)}, bf16[512,1024]{1,0:T(8,128)(2,1)S(1)}, u32[]{:S(2)}, u32[]{:S(2)}) collective-permute-start(bf16[512,1024]{1,0:T(8,128)(2,1)} %pad_maximum_fusion.11), channel_id=1, source_target_pairs={{0,1},{1,0},{2,3},{3,2},{4,5},{5,4},{6,7},{7,6},{8,9},{9,8},{10,11... | collective-permute-start | bytes 3145736 | tf_op jit(solution)/shard_map/ppermute | solution.py:442
  393.8 25.3 %collective-permute-start.18 = (bf16[512,1024]{1,0:T(8,128)(2,1)}, bf16[512,1024]{1,0:T(8,128)(2,1)}, u32[]{:S(2)}, u32[]{:S(2)}) collective-permute-start(bf16[512,1024]{1,0:T(8,128)(2,1)} %concatenate.132), channel_id=1, source_target_pairs={{0,2},{1,3},{2,0},{3,1},{4,6},{5,7},{6,4},{7,5},{8,10},{9,11},{10,... | collective-permute-start | bytes 3145736 | tf_op jit(solution)/shard_map/ppermute | solution.py:442
  427.0 212.5 %reduce-scatter.9.cloned.1.call-start = ((), (), s32[]{:S(2)}) async-start(), calls=%async_computation.11 | async-start | bytes 5242880 | tf_op jit(solution)/shard_map/reduce_scatter | solution.py:542
  510.7 178.9 %reduce-scatter.11.cloned.1.call-start = ((), (), s32[]{:S(2)}) async-start(), calls=%async_computation.12 | async-start | bytes 5242880 | tf_op jit(solution)/shard_map/reduce_scatter | solution.py:542
  514.6 68.7 %collective-permute-start.23 = (bf16[256,2048]{1,0:T(8,128)(2,1)}, bf16[256,2048]{1,0:T(8,128)(2,1)}, u32[]{:S(2)}, u32[]{:S(2)}) collective-permute-start(bf16[256,2048]{1,0:T(8,128)(2,1)} %get-tuple-element.230), channel_id=1, source_target_pairs={{0,1},{1,0},{2,3},{3,2},{4,5},{5,4},{6,7},{7,6},{8,9},{9,8},{10,11... | collective-permute-start | bytes 3145736 | tf_op jit(solution)/shard_map/ppermute | solution.py:442
  515.4 67.9 %collective-permute-start.24 = (bf16[256,2048]{1,0:T(8,128)(2,1)}, bf16[256,2048]{1,0:T(8,128)(2,1)}, u32[]{:S(2)}, u32[]{:S(2)}) collective-permute-start(bf16[256,2048]{1,0:T(8,128)(2,1)} %get-tuple-element.229), channel_id=1, source_target_pairs={{0,2},{1,3},{2,0},{3,1},{4,6},{5,7},{6,4},{7,5},{8,10},{9,11},{10,... | collective-permute-start | bytes 3145736 | tf_op jit(solution)/shard_map/ppermute | solution.py:442
  515.7 67.6 %collective-permute-start.25 = (bf16[256,2048]{1,0:T(8,128)(2,1)}, bf16[256,2048]{1,0:T(8,128)(2,1)}, u32[]{:S(2)}, u32[]{:S(2)}) collective-permute-start(bf16[256,2048]{1,0:T(8,128)(2,1)} %get-tuple-element.228), channel_id=1, source_target_pairs={{0,3},{1,2},{2,1},{3,0},{4,7},{5,6},{6,5},{7,4},{8,11},{9,10},{10,... | collective-permute-start | bytes 3145736 | tf_op jit(solution)/shard_map/ppermute | solution.py:442
  613.6 46.3 %all-to-all-start = ((f32[8,12,256]{2,1,0:T(8,128)}), f32[8,12,256]{2,1,0:T(8,128)S(1)}, u32[]{:S(2)}, u32[]{:S(2)}) async-start(f32[8,12,256]{2,1,0:T(8,128)} %pad_maximum_fusion.14), calls=%async_computation.4 | async-start | bytes 262144 | tf_op jit(solution)/shard_map/all_to_all | solution.py:664
  642.8 25.4 %collective-permute-start.32 = (bf16[512,1024]{1,0:T(8,128)(2,1)}, bf16[512,1024]{1,0:T(8,128)(2,1)S(1)}, u32[]{:S(2)}, u32[]{:S(2)}) collective-permute-start(bf16[512,1024]{1,0:T(8,128)(2,1)} %pad_maximum_fusion.13), channel_id=1, source_target_pairs={{0,2},{1,3},{2,0},{3,1},{4,6},{5,7},{6,4},{7,5},{8,10},{9,11},{10,... | collective-permute-start | bytes 3145736 | tf_op jit(solution)/shard_map/ppermute | solution.py:442
  644.4 25.2 %collective-permute-start.31 = (bf16[512,1024]{1,0:T(8,128)(2,1)}, bf16[512,1024]{1,0:T(8,128)(2,1)S(1)}, u32[]{:S(2)}, u32[]{:S(2)}) collective-permute-start(bf16[512,1024]{1,0:T(8,128)(2,1)} %pad_maximum_fusion.12), channel_id=1, source_target_pairs={{0,1},{1,0},{2,3},{3,2},{4,5},{5,4},{6,7},{7,6},{8,9},{9,8},{10,11... | collective-permute-start | bytes 3145736 | tf_op jit(solution)/shard_map/ppermute | solution.py:442
  (101 other events, 1160.8 us)
Sparse Core Ops, SparseCore 0:
  11.0 85.1 all-gather.4
  98.4 80.6 all-gather.6
  181.3 106.5 all-gather.8
  290.0 59.1 all-gather.10
  351.3 63.0 reduce-scatter.4
  427.1 99.5 reduce-scatter.6
  529.0 77.2 reduce-scatter.8
  608.7 80.2 reduce-scatter.10

commit v6 on v5

--- a/solution.py
+++ b/solution.py
@@ -396,12 +396,12 @@
 
 def side_by_side(*parts):
     rows = parts[0].shape[0]
-    step = rows // 4
+    step = rows // 2
     width = sum(a.shape[1] for a in parts)
     band = lambda columns: pl.BlockSpec((step, columns), lambda n: (n, 0))
     return pl.pallas_call(
         side_by_side_kernel,
-        grid=(4,),
+        grid=(2,),
         in_specs=[band(a.shape[1]) for a in parts],
         out_specs=band(width),
         out_shape=jax.ShapeDtypeStruct((rows, width), BF16),
@@ -418,11 +418,11 @@
 
 def apart(whole, *widths):
     rows = whole.shape[0]
-    step = rows // 4
+    step = rows // 2
     band = lambda columns: pl.BlockSpec((step, columns), lambda n: (n, 0))
     return pl.pallas_call(
         apart_kernel,
-        grid=(4,),
+        grid=(2,),
         in_specs=[band(whole.shape[1])],
         out_specs=[band(width) for width in widths],
         out_shape=[jax.ShapeDtypeStruct((rows, width), F32) for width in widths],

time: 704 us -> 702 us (level)
  no operation moved by 1% of the time
where the time goes in v6:
time: 702 us; the launch traced here: 698 us
  waiting for transfers between devices  224 us (32%)
  matrix products  152 us (22%)
  Pallas kernels  134 us (19%)
  local copies, waits for them, and re-layouts  59.7 us (9%)
  starting transfers between devices  49.7 us (7%)
  other arithmetic  48.4 us (7%)
  between operations  15.7 us (2%)
  blocking collectives  14.3 us (2%)
    ppermute x31, waiting for transfers between devices, swap(): return lax.ppermute(piece, 'tensor', [(i, i ^ mask) for i in range(4)])  159 us
    dot_general x19, matrix products, dot(): return lax.dot_general(a, b, (dims, ((), ())), preferred_element_type=F32)  152 us
    pallas_call x1, Pallas kernels, core_backward(): pl.pallas_call(backward_kernel, grid=(blocks,), in_specs=[tokens(a.shape[...  63.2 us
    pallas_call x1, Pallas kernels, core_forward(): pl.pallas_call(forward_kernel, grid=(blocks,), in_specs=[tokens(a.shape[1...  47.7 us
    all_gather x4, waiting for transfers between devices, gather_dp(): return lax.all_gather(shard.astype(BF16), 'dp', axis=axis, tiled=True)  40.7 us
    ppermute x31, starting transfers between devices, swap(): return lax.ppermute(piece, 'tensor', [(i, i ^ mask) for i in range(4)])  39.7 us
    unnamed x172, local copies, waits for them, and re-layouts  36.2 us
    pallas_call x1, Pallas kernels, projections_back(): pl.pallas_call(projections_kernel, grid=(model // tile,), in_specs=[whole...  18 us
  transfers between devices with their start and end apart: 49, of which 31 were waited for; matrix products, arithmetic and copies ran while one was open for 34% of the time, Pallas kernels for 18%

profile of v6, /device:TPU:0, one launch (start us, length us, event | category | flops | bytes accessed | tf_op | source)
XLA Modules:
  0.0 698.2 jit_solution(585931880349356967)
XLA Ops:
  22.9 14.3 %all_gather.17 = bf16[8,12,256]{2,1,0:T(8,128)(2,1)S(1)} all-gather(bf16[1,12,256]{2,1,0:T(8,128)(2,1)S(1)} %pad_maximum_fusion.16), channel_id=1, replica_groups=mesh['dp'=8,'tensor'=4] {'dp'}, dimensions={0}, use_global_device_ids=true | all-gather | bytes 55296 | tf_op jit(solution)/shard_map/all_gather | solution.py:580
  72.7 16.4 %collective-permute-done.5 = bf16[256,2048]{1,0:T(8,128)(2,1)S(1)} collective-permute-done((bf16[256,2048]{1,0:T(8,128)(2,1)S(1)}, bf16[256,2048]{1,0:T(8,128)(2,1)S(1)}, u32[]{:S(2)}, u32[]{:S(2)}) %collective-permute-start.5) | collective-permute-done | bytes 1048608 | tf_op jit(solution)/shard_map/ppermute | solution.py:442
  103.2 15.5 %fusion.84.pqkv = f32[1024,2048]{1,0:T(8,128)} fusion(bf16[1024,2048]{1,0:T(8,128)(2,1)} %copy-done.21, bf16[2048,2048]{1,0:T(8,128)(2,1)} %all-gather.5.cloned.1.call-done.w_qkv), kind=kOutput, calls=%fused_computation.214 | convolution fusion | flops 8589934592 | bytes 20971520 | tf_op jit(solution)/shard_map/dot_general | solution.py:438
  118.8 47.7 %core_forward.1 = (bf16[1024,1024]{1,0:T(8,128)(2,1)S(1)}, f32[1024,4]{1,0:T(8,128)S(1)}, f32[1024,2048]{1,0:T(8,128)}, bf16[1024,1024]{1,0:T(8,128)(2,1)S(1)}, ...) custom-call(f32[1024,2048]{1,0:T(8,128)} %fusion.84.pqkv, f32[1024,8]{1,0:T(8,128)S(1)} %fusion.85.pab, ...), custom_call_target="tpu_custom_call" | custom-call | flops 8000000000 | bytes 33554432 | tf_op jit(solution)/shard_map/core_forward/pallas_call | solution.py:162
  178.2 10.7 %fusion.2 = (bf16[1024,1024]{1,0:T(8,128)(2,1)S(1)}, f32[1024,1024]{1,0:T(8,128)}) fusion(bf16[1024,1024]{1,0:T(8,128)(2,1)S(1)} %get-tuple-element.89.n_in, f32[1024]{0:T(1024)S(1)} %bitcast.89, bf16[1024,2048]{1,0:T(8,128)(2,1)} %copy-done.21, bf16[2048,2048]{1,0:T(8,128)(2,1)} %all-gather.7.cloned.1.call-done.w_out), kind=kOutput, calls=%fused_computation.13 | convolution fusion | flops 4303355904 | bytes 16781312 | tf_op jit(solution)/shard_map/dot_general | solution.py:438
  197.6 22.2 %collective-permute-done.9 = bf16[512,1024]{1,0:T(8,128)(2,1)S(1)} collective-permute-done((bf16[512,1024]{1,0:T(8,128)(2,1)S(1)}, bf16[512,1024]{1,0:T(8,128)(2,1)S(1)}, u32[]{:S(2)}, u32[]{:S(2)}) %collective-permute-start.9) | collective-permute-done | bytes 1048608 | tf_op jit(solution)/shard_map/ppermute | solution.py:442
  226.1 10.4 %collective-permute-done.10 = bf16[256,1024]{1,0:T(8,128)(2,1)} collective-permute-done((bf16[256,1024]{1,0:T(8,128)(2,1)}, bf16[256,1024]{1,0:T(8,128)(2,1)}, u32[]{:S(2)}, u32[]{:S(2)}) %collective-permute-start.10) | collective-permute-done | bytes 524320 | tf_op jit(solution)/shard_map/ppermute | solution.py:442
  243.1 20.8 %collective-permute-done.13 = bf16[256,2048]{1,0:T(8,128)(2,1)S(1)} collective-permute-done((bf16[256,2048]{1,0:T(8,128)(2,1)S(1)}, bf16[256,2048]{1,0:T(8,128)(2,1)S(1)}, u32[]{:S(2)}, u32[]{:S(2)}) %collective-permute-start.13) | collective-permute-done | bytes 1048608 | tf_op jit(solution)/shard_map/ppermute | solution.py:442
  266.7 9.0 %collective-permute-done.14 = bf16[128,2048]{1,0:T(8,128)(2,1)S(1)} collective-permute-done((bf16[128,2048]{1,0:T(8,128)(2,1)S(1)}, bf16[128,2048]{1,0:T(8,128)(2,1)S(1)}, u32[]{:S(2)}, u32[]{:S(2)}) %collective-permute-start.14) | collective-permute-done | bytes 524320 | tf_op jit(solution)/shard_map/ppermute | solution.py:442
  287.1 17.2 %fusion.86 = f32[1024,2816]{1,0:T(8,128)S(1)} fusion(bf16[1024,2048]{1,0:T(8,128)(2,1)} %copy-done.31, bf16[2048,2816]{1,0:T(8,128)(2,1)} %all-gather.9.cloned.1.call-done), kind=kOutput, calls=%fused_computation.216 | convolution fusion | flops 11811160064 | bytes 27262976 | tf_op jit(solution)/shard_map/dot_general | solution.py:438
  310.1 10.7 %convolution_convert_fusion = bf16[1408,2048]{1,0:T(8,128)(2,1)} fusion(bf16[1024,1408]{1,0:T(8,128)(2,1)S(1)} %multiply_convert_fusion.2, bf16[1024,2048]{1,0:T(8,128)(2,1)} %constant_dynamic-update-slice_fusion.5), kind=kOutput, calls=%fused_computation.2 | convolution fusion | flops 5908463616 | bytes 12845056 | tf_op jit(solution)/shard_map/dot_general | solution.py:438
  320.9 27.4 %all-gather.11.cloned.1.call-done = bf16[1408,2048]{1,0:T(8,128)(2,1)} async-done(((bf16[1408,256]{1,0:T(8,128)(2,1)}), bf16[1408,2048]{1,0:T(8,128)(2,1)}) %all-gather.11.cloned.1.call-update) | async-done | bytes 5767184 | tf_op jit(solution)/shard_map/all_gather | solution.py:519
  348.3 14.2 %multiply_convert_fusion.1 = (bf16[1024,1408]{1,0:T(8,128)(2,1)S(1)}, bf16[1024,1408]{1,0:T(8,128)(2,1)S(1)}) fusion(f32[1024,2816]{1,0:T(8,128)} %copy-done.25, bf16[1024,2048]{1,0:T(8,128)(2,1)} %constant_dynamic-update-slice_fusion.5, bf16[1408,2048]{1,0:T(8,128)(2,1)} %all-gather.11.cloned.1.call-done), kind=kOutput, calls=%fused_computation.5 | convolution fusion | flops 5924323328 | bytes 27262976 | tf_op jit(solution)/shard_map/dot_general | solution.py:438
  363.8 8.8 %convolution_convert_fusion.1 = bf16[1024,2816]{1,0:T(8,128)(2,1)} fusion(bf16[1024,256]{1,0:T(8,128)(2,1)S(1)} %get-tuple-element.239, bf16[1024,256]{1,0:T(8,128)(2,1)S(1)} %get-tuple-element.240, bf16[1024,256]{1,0:T(8,128)(2,1)S(1)} %copy-done.49, bf16[1024,256]{1,0:T(8,128)(2,1)S(1)} %copy-done.50, bf16[1024,1408]{1,0:T(8,128)(2,1)S(1)} %get-tuple-element.205, ...), kind=kOutput, calls=%fused_computation.9 | convolution fusion | flops 5928386560 | bytes 13631488 | tf_op jit(solution)/shard_map/dot_general | solution.py:438
  372.8 15.0 %convolution_convert_fusion.2 = bf16[1024,2048]{1,0:T(8,128)(2,1)S(1)} fusion(bf16[1024,2816]{1,0:T(8,128)(2,1)S(1)} %pad_maximum_fusion, bf16[2048,2816]{1,0:T(8,128)(2,1)} %all-gather.9.cloned.1.call-done), kind=kOutput, calls=%fused_computation.27 | convolution fusion | flops 11813257216 | bytes 21495808 | tf_op jit(solution)/shard_map/dot_general | solution.py:438
  394.4 10.7 %add_convert_fusion = bf16[1024,2816]{1,0:T(8,128)(2,1)} fusion(bf16[1024,2816]{1,0:T(8,128)(2,1)} %collective-permute-done.16, bf16[1024,2816]{1,0:T(8,128)(2,1)S(1)} %pad_maximum_fusion, bf16[1024,256]{1,0:T(8,128)(2,1)S(1)} %copy-done.46, bf16[1024,256]{1,0:T(8,128)(2,1)S(1)} %copy-done.47, bf16[1024,256]{1,0:T(8,128)(2,1)S(1)} %copy-done.48, ...), kind=kOutput, calls=%fused_computation | convolution fusion | flops 5922619392 | bytes 19398656 | tf_op jit(solution)/shard_map/dot_general | solution.py:438
  405.1 11.9 %collective-permute-done.17 = bf16[512,1024]{1,0:T(8,128)(2,1)S(1)} collective-permute-done((bf16[512,1024]{1,0:T(8,128)(2,1)}, bf16[512,1024]{1,0:T(8,128)(2,1)S(1)}, u32[]{:S(2)}, u32[]{:S(2)}) %collective-permute-start.17) | collective-permute-done | bytes 1048608 | tf_op jit(solution)/shard_map/ppermute | solution.py:442
  426.2 11.1 %collective-permute-done.19 = bf16[256,1024]{1,0:T(8,128)(2,1)} collective-permute-done((bf16[256,1024]{1,0:T(8,128)(2,1)}, bf16[256,1024]{1,0:T(8,128)(2,1)}, u32[]{:S(2)}, u32[]{:S(2)}) %collective-permute-start.19) | collective-permute-done | bytes 524320 | tf_op jit(solution)/shard_map/ppermute | solution.py:442
  445.4 8.5 %convolution_convert_fusion.3 = bf16[1024,2048]{1,0:T(8,128)(2,1)} fusion(bf16[1024,1408]{1,0:T(8,128)(2,1)S(1)} %copy-done.39, bf16[1408,2048]{1,0:T(8,128)(2,1)S(1)} %bitcast.94), kind=kOutput, calls=%fused_computation.28 | convolution fusion | flops 5907677184 | bytes 12845056 | tf_op jit(solution)/shard_map/dot_general | solution.py:438
  453.9 13.2 %collective-permute-done.21 = bf16[256,2048]{1,0:T(8,128)(2,1)S(1)} collective-permute-done((bf16[256,2048]{1,0:T(8,128)(2,1)S(1)}, bf16[256,2048]{1,0:T(8,128)(2,1)S(1)}, u32[]{:S(2)}, u32[]{:S(2)}) %collective-permute-start.21) | collective-permute-done | bytes 1048608 | tf_op jit(solution)/shard_map/ppermute | solution.py:442
  470.0 8.3 %collective-permute-done.26 = bf16[128,2048]{1,0:T(8,128)(2,1)S(1)} collective-permute-done((bf16[128,2048]{1,0:T(8,128)(2,1)S(1)}, bf16[128,2048]{1,0:T(8,128)(2,1)S(1)}, u32[]{:S(2)}, u32[]{:S(2)}) %collective-permute-start.26) | collective-permute-done | bytes 524320 | tf_op jit(solution)/shard_map/ppermute | solution.py:442
  517.1 63.2 %core_backward.1 = (bf16[1024,2048]{1,0:T(8,128)(2,1)S(1)}, f32[1024,8]{1,0:T(8,128)S(1)}, f32[4,2048]{1,0:T(4,128)S(1)}, f32[1,8]{1,0:T(1,128)S(1)}, f32[1,256]{1,0:T(1,128)S(1)}) custom-call(f32[1024,1024]{1,0:T(8,128)} %get-tuple-element.112.dn_in, f32[1024,2048]{1,0:T(8,128)} %fusion.84.pqkv, f32[1024,8]{1,0:T(8,128)S(1)} %copy-done.5, ...), custom_call_target="tpu_custom_call" | custom-call | flops 20000000000 | bytes 50331648 | tf_op jit(solution)/shard_map/core_backward/pallas_call | solution.py:333
  618.4 18.0 %projections_back.1 = (bf16[1024,2048]{1,0:T(8,128)(2,1)S(1)}, f32[1,2048]{1,0:T(1,128)S(1)}) custom-call(bf16[1024,2048]{1,0:T(8,128)(2,1)S(1)} %copy-done.8, bf16[1024,1024]{1,0:T(8,128)(2,1)S(1)} %get-tuple-element.206.dpo, bf16[1024,8]{1,0:T(8,128)(2,1)S(1)} %convert_element_type.267.dab, bf16[2048,2048]{1,0:T(8,128)(2,1)} %all-gather.5.cloned.1.call-done.w_qkv, ...), custom_call_target="tpu_custom_call" | custom-call | flops 12884901888 | bytes 33554432 | tf_op jit(solution)/shard_map/projections_back/pallas_call | solution.py:367
  675.0 8.8 %collective-permute-done.39 = f32[4384]{0:T(1024)S(1)} collective-permute-done((f32[4384]{0:T(1024)S(1)}, f32[4384]{0:T(1024)S(1)}, u32[]{:S(2)}, u32[]{:S(2)}) %collective-permute-start.39) | collective-permute-done | bytes 17568 | tf_op jit(solution)/shard_map/ppermute | solution.py:495
  (395 shorter events, 268.6 us)
Async XLA Ops:
  7.2 96.0 %all-gather.5.cloned.1.call-start = ((), (), s32[]{:S(2)}) async-start(), calls=%async_computation.5 | async-start | bytes 9437184 | tf_op jit(solution)/shard_map/all_gather | solution.py:519
  9.6 168.6 %all-gather.7.cloned.1.call-start = ((), (), s32[]{:S(2)}) async-start(), calls=%async_computation.6 | async-start | bytes 9437184 | tf_op jit(solution)/shard_map/all_gather | solution.py:519
  13.6 273.5 %all-gather.9.cloned.1.call-start = ((), (), s32[]{:S(2)}) async-start(), calls=%async_computation.7 | async-start | bytes 12976128 | tf_op jit(solution)/shard_map/all_gather | solution.py:519
  16.6 331.7 %all-gather.11.cloned.1.call-start = ((), (), s32[]{:S(2)}) async-start(), calls=%async_computation.8 | async-start | bytes 6488064 | tf_op jit(solution)/shard_map/all_gather | solution.py:519
  18.3 26.1 %collective-permute-start.1 = (bf16[256,2048]{1,0:T(8,128)(2,1)S(1)}, bf16[256,2048]{1,0:T(8,128)(2,1)S(1)}, u32[]{:S(2)}, u32[]{:S(2)}) collective-permute-start(bf16[256,2048]{1,0:T(8,128)(2,1)S(1)} %get-tuple-element.203), channel_id=1, source_target_pairs={{0,2},{1,3},{2,0},{3,1},{4,6},{5,7},{6,4},{7,5},{8,10},{9,11},{10,... | collective-permute-start | bytes 3145736 | tf_op jit(solution)/shard_map/ppermute | solution.py:442
  21.2 25.8 %collective-permute-start = (bf16[256,2048]{1,0:T(8,128)(2,1)S(1)}, bf16[256,2048]{1,0:T(8,128)(2,1)S(1)}, u32[]{:S(2)}, u32[]{:S(2)}) collective-permute-start(bf16[256,2048]{1,0:T(8,128)(2,1)S(1)} %get-tuple-element.203), channel_id=1, source_target_pairs={{0,1},{1,0},{2,3},{3,2},{4,5},{5,4},{6,7},{7,6},{8,9},{9,8},{10,11... | collective-permute-start | bytes 3145736 | tf_op jit(solution)/shard_map/ppermute | solution.py:442
  65.6 23.5 %collective-permute-start.5 = (bf16[256,2048]{1,0:T(8,128)(2,1)S(1)}, bf16[256,2048]{1,0:T(8,128)(2,1)S(1)}, u32[]{:S(2)}, u32[]{:S(2)}) collective-permute-start(bf16[256,2048]{1,0:T(8,128)(2,1)S(1)} %copy-done.36), channel_id=1, source_target_pairs={{0,2},{1,3},{2,0},{3,1},{4,6},{5,7},{6,4},{7,5},{8,10},{9,11},{10,... | collective-permute-start | bytes 3145736 | tf_op jit(solution)/shard_map/ppermute | solution.py:442
  67.1 24.3 %collective-permute-start.4 = (bf16[256,2048]{1,0:T(8,128)(2,1)S(1)}, bf16[256,2048]{1,0:T(8,128)(2,1)S(1)}, u32[]{:S(2)}, u32[]{:S(2)}) collective-permute-start(bf16[256,2048]{1,0:T(8,128)(2,1)S(1)} %copy-done.36), channel_id=1, source_target_pairs={{0,1},{1,0},{2,3},{3,2},{4,5},{5,4},{6,7},{7,6},{8,9},{9,8},{10,11... | collective-permute-start | bytes 3145736 | tf_op jit(solution)/shard_map/ppermute | solution.py:442
  194.5 25.4 %collective-permute-start.9 = (bf16[512,1024]{1,0:T(8,128)(2,1)S(1)}, bf16[512,1024]{1,0:T(8,128)(2,1)S(1)}, u32[]{:S(2)}, u32[]{:S(2)}) collective-permute-start(bf16[512,1024]{1,0:T(8,128)(2,1)S(1)} %pad_maximum_fusion.10), channel_id=1, source_target_pairs={{0,2},{1,3},{2,0},{3,1},{4,6},{5,7},{6,4},{7,5},{8,10},{9,11},{10,... | collective-permute-start | bytes 3145736 | tf_op jit(solution)/shard_map/ppermute | solution.py:442
  196.1 25.1 %collective-permute-start.8 = (bf16[512,1024]{1,0:T(8,128)(2,1)S(1)}, bf16[512,1024]{1,0:T(8,128)(2,1)S(1)}, u32[]{:S(2)}, u32[]{:S(2)}) collective-permute-start(bf16[512,1024]{1,0:T(8,128)(2,1)S(1)} %pad_maximum_fusion.9), channel_id=1, source_target_pairs={{0,1},{1,0},{2,3},{3,2},{4,5},{5,4},{6,7},{7,6},{8,9},{9,8},{10,11... | collective-permute-start | bytes 3145736 | tf_op jit(solution)/shard_map/ppermute | solution.py:442
  226.1 283.5 %reduce-scatter.5.cloned.1.call-start = ((), (), s32[]{:S(2)}) async-start(), calls=%async_computation.9 | async-start | bytes 6488064 | tf_op jit(solution)/shard_map/reduce_scatter | solution.py:615
  240.4 23.5 %collective-permute-start.13 = (bf16[256,2048]{1,0:T(8,128)(2,1)S(1)}, bf16[256,2048]{1,0:T(8,128)(2,1)S(1)}, u32[]{:S(2)}, u32[]{:S(2)}) collective-permute-start(bf16[256,2048]{1,0:T(8,128)(2,1)S(1)} %get-tuple-element.199), channel_id=1, source_target_pairs={{0,2},{1,3},{2,0},{3,1},{4,6},{5,7},{6,4},{7,5},{8,10},{9,11},{10,... | collective-permute-start | bytes 3145736 | tf_op jit(solution)/shard_map/ppermute | solution.py:442
  241.7 23.7 %collective-permute-start.12 = (bf16[256,2048]{1,0:T(8,128)(2,1)S(1)}, bf16[256,2048]{1,0:T(8,128)(2,1)S(1)}, u32[]{:S(2)}, u32[]{:S(2)}) collective-permute-start(bf16[256,2048]{1,0:T(8,128)(2,1)S(1)} %get-tuple-element.199), channel_id=1, source_target_pairs={{0,1},{1,0},{2,3},{3,2},{4,5},{5,4},{6,7},{7,6},{8,9},{9,8},{10,11... | collective-permute-start | bytes 3145736 | tf_op jit(solution)/shard_map/ppermute | solution.py:442
  320.8 261.4 %reduce-scatter.7.cloned.1.call-start = ((), (), s32[]{:S(2)}) async-start(), calls=%async_computation.10 | async-start | bytes 7208960 | tf_op jit(solution)/shard_map/reduce_scatter | solution.py:542
  391.5 25.5 %collective-permute-start.17 = (bf16[512,1024]{1,0:T(8,128)(2,1)}, bf16[512,1024]{1,0:T(8,128)(2,1)S(1)}, u32[]{:S(2)}, u32[]{:S(2)}) collective-permute-start(bf16[512,1024]{1,0:T(8,128)(2,1)} %pad_maximum_fusion.11), channel_id=1, source_target_pairs={{0,1},{1,0},{2,3},{3,2},{4,5},{5,4},{6,7},{7,6},{8,9},{9,8},{10,11... | collective-permute-start | bytes 3145736 | tf_op jit(solution)/shard_map/ppermute | solution.py:442
  392.9 25.3 %collective-permute-start.18 = (bf16[512,1024]{1,0:T(8,128)(2,1)}, bf16[512,1024]{1,0:T(8,128)(2,1)}, u32[]{:S(2)}, u32[]{:S(2)}) collective-permute-start(bf16[512,1024]{1,0:T(8,128)(2,1)} %concatenate.132), channel_id=1, source_target_pairs={{0,2},{1,3},{2,0},{3,1},{4,6},{5,7},{6,4},{7,5},{8,10},{9,11},{10,... | collective-permute-start | bytes 3145736 | tf_op jit(solution)/shard_map/ppermute | solution.py:442
  426.2 212.3 %reduce-scatter.9.cloned.1.call-start = ((), (), s32[]{:S(2)}) async-start(), calls=%async_computation.11 | async-start | bytes 5242880 | tf_op jit(solution)/shard_map/reduce_scatter | solution.py:542
  509.6 179.1 %reduce-scatter.11.cloned.1.call-start = ((), (), s32[]{:S(2)}) async-start(), calls=%async_computation.12 | async-start | bytes 5242880 | tf_op jit(solution)/shard_map/reduce_scatter | solution.py:542
  513.5 68.7 %collective-permute-start.23 = (bf16[256,2048]{1,0:T(8,128)(2,1)}, bf16[256,2048]{1,0:T(8,128)(2,1)}, u32[]{:S(2)}, u32[]{:S(2)}) collective-permute-start(bf16[256,2048]{1,0:T(8,128)(2,1)} %get-tuple-element.230), channel_id=1, source_target_pairs={{0,1},{1,0},{2,3},{3,2},{4,5},{5,4},{6,7},{7,6},{8,9},{9,8},{10,11... | collective-permute-start | bytes 3145736 | tf_op jit(solution)/shard_map/ppermute | solution.py:442
  514.3 67.9 %collective-permute-start.24 = (bf16[256,2048]{1,0:T(8,128)(2,1)}, bf16[256,2048]{1,0:T(8,128)(2,1)}, u32[]{:S(2)}, u32[]{:S(2)}) collective-permute-start(bf16[256,2048]{1,0:T(8,128)(2,1)} %get-tuple-element.229), channel_id=1, source_target_pairs={{0,2},{1,3},{2,0},{3,1},{4,6},{5,7},{6,4},{7,5},{8,10},{9,11},{10,... | collective-permute-start | bytes 3145736 | tf_op jit(solution)/shard_map/ppermute | solution.py:442
  514.8 67.5 %collective-permute-start.25 = (bf16[256,2048]{1,0:T(8,128)(2,1)}, bf16[256,2048]{1,0:T(8,128)(2,1)}, u32[]{:S(2)}, u32[]{:S(2)}) collective-permute-start(bf16[256,2048]{1,0:T(8,128)(2,1)} %get-tuple-element.228), channel_id=1, source_target_pairs={{0,3},{1,2},{2,1},{3,0},{4,7},{5,6},{6,5},{7,4},{8,11},{9,10},{10,... | collective-permute-start | bytes 3145736 | tf_op jit(solution)/shard_map/ppermute | solution.py:442
  612.6 46.7 %all-to-all-start = ((f32[8,12,256]{2,1,0:T(8,128)}), f32[8,12,256]{2,1,0:T(8,128)S(1)}, u32[]{:S(2)}, u32[]{:S(2)}) async-start(f32[8,12,256]{2,1,0:T(8,128)} %pad_maximum_fusion.14), calls=%async_computation.4 | async-start | bytes 262144 | tf_op jit(solution)/shard_map/all_to_all | solution.py:664
  641.7 25.4 %collective-permute-start.32 = (bf16[512,1024]{1,0:T(8,128)(2,1)}, bf16[512,1024]{1,0:T(8,128)(2,1)S(1)}, u32[]{:S(2)}, u32[]{:S(2)}) collective-permute-start(bf16[512,1024]{1,0:T(8,128)(2,1)} %pad_maximum_fusion.13), channel_id=1, source_target_pairs={{0,2},{1,3},{2,0},{3,1},{4,6},{5,7},{6,4},{7,5},{8,10},{9,11},{10,... | collective-permute-start | bytes 3145736 | tf_op jit(solution)/shard_map/ppermute | solution.py:442
  643.4 25.2 %collective-permute-start.31 = (bf16[512,1024]{1,0:T(8,128)(2,1)}, bf16[512,1024]{1,0:T(8,128)(2,1)S(1)}, u32[]{:S(2)}, u32[]{:S(2)}) collective-permute-start(bf16[512,1024]{1,0:T(8,128)(2,1)} %pad_maximum_fusion.12), channel_id=1, source_target_pairs={{0,1},{1,0},{2,3},{3,2},{4,5},{5,4},{6,7},{7,6},{8,9},{9,8},{10,11... | collective-permute-start | bytes 3145736 | tf_op jit(solution)/shard_map/ppermute | solution.py:442
  (101 other events, 1162.6 us)
Sparse Core Ops, SparseCore 0:
  10.2 85.1 all-gather.4
  97.6 80.5 all-gather.6
  180.4 106.5 all-gather.8
  289.1 59.1 all-gather.10
  350.4 63.0 reduce-scatter.4
  426.3 99.5 reduce-scatter.6
  528.1 77.2 reduce-scatter.8
  607.9 80.3 reduce-scatter.10

commit v7 on v6

--- a/solution.py
+++ b/solution.py
@@ -362,7 +362,7 @@
 
 def projections_back(dqkv, dpo, dab, w_qkv, w_out, w_ab, normed):
     rows, model = normed.shape
-    tile = 256
+    tile = 512
     whole = lambda a: pl.BlockSpec(a.shape, lambda n: (0, 0), pipeline_mode=pl.Buffered(1))
     return pl.pallas_call(
         projections_kernel,

time: 702 us -> 702 us (level)
  transfers between devices with their start and end apart: 49 -> 49, of which waited for: 31 -> 32; matrix products, arithmetic and copies ran while one was open for 34% -> 34% of each run, Pallas kernels for 18% -> 18%
where the time goes in v7:
time: 702 us; the launch traced here: 698 us
  waiting for transfers between devices  224 us (32%)
  matrix products  152 us (22%)
  Pallas kernels  133 us (19%)
  local copies, waits for them, and re-layouts  59.7 us (9%)
  starting transfers between devices  49.5 us (7%)
  other arithmetic  48.4 us (7%)
  between operations  15.7 us (2%)
  blocking collectives  14.3 us (2%)
    ppermute x31, waiting for transfers between devices, swap(): return lax.ppermute(piece, 'tensor', [(i, i ^ mask) for i in range(4)])  159 us
    dot_general x19, matrix products, dot(): return lax.dot_general(a, b, (dims, ((), ())), preferred_element_type=F32)  152 us
    pallas_call x1, Pallas kernels, core_backward(): pl.pallas_call(backward_kernel, grid=(blocks,), in_specs=[tokens(a.shape[...  63.2 us
    pallas_call x1, Pallas kernels, core_forward(): pl.pallas_call(forward_kernel, grid=(blocks,), in_specs=[tokens(a.shape[1...  47.7 us
    all_gather x4, waiting for transfers between devices, gather_dp(): return lax.all_gather(shard.astype(BF16), 'dp', axis=axis, tiled=True)  40.7 us
    ppermute x31, starting transfers between devices, swap(): return lax.ppermute(piece, 'tensor', [(i, i ^ mask) for i in range(4)])  39.8 us
    unnamed x172, local copies, waits for them, and re-layouts  36.2 us
    pallas_call x1, Pallas kernels, projections_back(): pl.pallas_call(projections_kernel, grid=(model // tile,), in_specs=[whole...  17.4 us
  transfers between devices with their start and end apart: 49, of which 32 were waited for; matrix products, arithmetic and copies ran while one was open for 34% of the time, Pallas kernels for 18%

profile of v7, /device:TPU:0, one launch (start us, length us, event | category | flops | bytes accessed | tf_op | source)
XLA Modules:
  0.0 697.7 jit_solution(2339607828697524560)
XLA Ops:
  22.9 14.3 %all_gather.17 = bf16[8,12,256]{2,1,0:T(8,128)(2,1)S(1)} all-gather(bf16[1,12,256]{2,1,0:T(8,128)(2,1)S(1)} %pad_maximum_fusion.16), channel_id=1, replica_groups=mesh['dp'=8,'tensor'=4] {'dp'}, dimensions={0}, use_global_device_ids=true | all-gather | bytes 55296 | tf_op jit(solution)/shard_map/all_gather | solution.py:580
  72.7 16.4 %collective-permute-done.5 = bf16[256,2048]{1,0:T(8,128)(2,1)S(1)} collective-permute-done((bf16[256,2048]{1,0:T(8,128)(2,1)S(1)}, bf16[256,2048]{1,0:T(8,128)(2,1)S(1)}, u32[]{:S(2)}, u32[]{:S(2)}) %collective-permute-start.5) | collective-permute-done | bytes 1048608 | tf_op jit(solution)/shard_map/ppermute | solution.py:442
  103.2 15.5 %fusion.84.pqkv = f32[1024,2048]{1,0:T(8,128)} fusion(bf16[1024,2048]{1,0:T(8,128)(2,1)} %copy-done.21, bf16[2048,2048]{1,0:T(8,128)(2,1)} %all-gather.5.cloned.1.call-done.w_qkv), kind=kOutput, calls=%fused_computation.214 | convolution fusion | flops 8589934592 | bytes 20971520 | tf_op jit(solution)/shard_map/dot_general | solution.py:438
  118.8 47.7 %core_forward.1 = (bf16[1024,1024]{1,0:T(8,128)(2,1)S(1)}, f32[1024,4]{1,0:T(8,128)S(1)}, f32[1024,2048]{1,0:T(8,128)}, bf16[1024,1024]{1,0:T(8,128)(2,1)S(1)}, ...) custom-call(f32[1024,2048]{1,0:T(8,128)} %fusion.84.pqkv, f32[1024,8]{1,0:T(8,128)S(1)} %fusion.85.pab, ...), custom_call_target="tpu_custom_call" | custom-call | flops 8000000000 | bytes 33554432 | tf_op jit(solution)/shard_map/core_forward/pallas_call | solution.py:162
  178.2 10.7 %fusion.2 = (bf16[1024,1024]{1,0:T(8,128)(2,1)S(1)}, f32[1024,1024]{1,0:T(8,128)}) fusion(bf16[1024,1024]{1,0:T(8,128)(2,1)S(1)} %get-tuple-element.89.n_in, f32[1024]{0:T(1024)S(1)} %bitcast.89, bf16[1024,2048]{1,0:T(8,128)(2,1)} %copy-done.21, bf16[2048,2048]{1,0:T(8,128)(2,1)} %all-gather.7.cloned.1.call-done.w_out), kind=kOutput, calls=%fused_computation.13 | convolution fusion | flops 4303355904 | bytes 16781312 | tf_op jit(solution)/shard_map/dot_general | solution.py:438
  197.6 22.2 %collective-permute-done.9 = bf16[512,1024]{1,0:T(8,128)(2,1)S(1)} collective-permute-done((bf16[512,1024]{1,0:T(8,128)(2,1)S(1)}, bf16[512,1024]{1,0:T(8,128)(2,1)S(1)}, u32[]{:S(2)}, u32[]{:S(2)}) %collective-permute-start.9) | collective-permute-done | bytes 1048608 | tf_op jit(solution)/shard_map/ppermute | solution.py:442
  226.1 10.4 %collective-permute-done.10 = bf16[256,1024]{1,0:T(8,128)(2,1)} collective-permute-done((bf16[256,1024]{1,0:T(8,128)(2,1)}, bf16[256,1024]{1,0:T(8,128)(2,1)}, u32[]{:S(2)}, u32[]{:S(2)}) %collective-permute-start.10) | collective-permute-done | bytes 524320 | tf_op jit(solution)/shard_map/ppermute | solution.py:442
  243.1 20.8 %collective-permute-done.13 = bf16[256,2048]{1,0:T(8,128)(2,1)S(1)} collective-permute-done((bf16[256,2048]{1,0:T(8,128)(2,1)S(1)}, bf16[256,2048]{1,0:T(8,128)(2,1)S(1)}, u32[]{:S(2)}, u32[]{:S(2)}) %collective-permute-start.13) | collective-permute-done | bytes 1048608 | tf_op jit(solution)/shard_map/ppermute | solution.py:442
  266.7 9.0 %collective-permute-done.14 = bf16[128,2048]{1,0:T(8,128)(2,1)S(1)} collective-permute-done((bf16[128,2048]{1,0:T(8,128)(2,1)S(1)}, bf16[128,2048]{1,0:T(8,128)(2,1)S(1)}, u32[]{:S(2)}, u32[]{:S(2)}) %collective-permute-start.14) | collective-permute-done | bytes 524320 | tf_op jit(solution)/shard_map/ppermute | solution.py:442
  287.1 17.2 %fusion.86 = f32[1024,2816]{1,0:T(8,128)S(1)} fusion(bf16[1024,2048]{1,0:T(8,128)(2,1)} %copy-done.31, bf16[2048,2816]{1,0:T(8,128)(2,1)} %all-gather.9.cloned.1.call-done), kind=kOutput, calls=%fused_computation.216 | convolution fusion | flops 11811160064 | bytes 27262976 | tf_op jit(solution)/shard_map/dot_general | solution.py:438
  310.1 10.7 %convolution_convert_fusion = bf16[1408,2048]{1,0:T(8,128)(2,1)} fusion(bf16[1024,1408]{1,0:T(8,128)(2,1)S(1)} %multiply_convert_fusion.2, bf16[1024,2048]{1,0:T(8,128)(2,1)} %constant_dynamic-update-slice_fusion.5), kind=kOutput, calls=%fused_computation.2 | convolution fusion | flops 5908463616 | bytes 12845056 | tf_op jit(solution)/shard_map/dot_general | solution.py:438
  320.9 27.4 %all-gather.11.cloned.1.call-done = bf16[1408,2048]{1,0:T(8,128)(2,1)} async-done(((bf16[1408,256]{1,0:T(8,128)(2,1)}), bf16[1408,2048]{1,0:T(8,128)(2,1)}) %all-gather.11.cloned.1.call-update) | async-done | bytes 5767184 | tf_op jit(solution)/shard_map/all_gather | solution.py:519
  348.3 14.2 %multiply_convert_fusion.1 = (bf16[1024,1408]{1,0:T(8,128)(2,1)S(1)}, bf16[1024,1408]{1,0:T(8,128)(2,1)S(1)}) fusion(f32[1024,2816]{1,0:T(8,128)} %copy-done.25, bf16[1024,2048]{1,0:T(8,128)(2,1)} %constant_dynamic-update-slice_fusion.5, bf16[1408,2048]{1,0:T(8,128)(2,1)} %all-gather.11.cloned.1.call-done), kind=kOutput, calls=%fused_computation.5 | convolution fusion | flops 5924323328 | bytes 27262976 | tf_op jit(solution)/shard_map/dot_general | solution.py:438
  363.8 8.8 %convolution_convert_fusion.1 = bf16[1024,2816]{1,0:T(8,128)(2,1)} fusion(bf16[1024,256]{1,0:T(8,128)(2,1)S(1)} %get-tuple-element.239, bf16[1024,256]{1,0:T(8,128)(2,1)S(1)} %get-tuple-element.240, bf16[1024,256]{1,0:T(8,128)(2,1)S(1)} %copy-done.49, bf16[1024,256]{1,0:T(8,128)(2,1)S(1)} %copy-done.50, bf16[1024,1408]{1,0:T(8,128)(2,1)S(1)} %get-tuple-element.205, ...), kind=kOutput, calls=%fused_computation.9 | convolution fusion | flops 5928386560 | bytes 13631488 | tf_op jit(solution)/shard_map/dot_general | solution.py:438
  372.8 15.0 %convolution_convert_fusion.2 = bf16[1024,2048]{1,0:T(8,128)(2,1)S(1)} fusion(bf16[1024,2816]{1,0:T(8,128)(2,1)S(1)} %pad_maximum_fusion, bf16[2048,2816]{1,0:T(8,128)(2,1)} %all-gather.9.cloned.1.call-done), kind=kOutput, calls=%fused_computation.27 | convolution fusion | flops 11813257216 | bytes 21495808 | tf_op jit(solution)/shard_map/dot_general | solution.py:438
  394.4 10.7 %add_convert_fusion = bf16[1024,2816]{1,0:T(8,128)(2,1)} fusion(bf16[1024,2816]{1,0:T(8,128)(2,1)} %collective-permute-done.16, bf16[1024,2816]{1,0:T(8,128)(2,1)S(1)} %pad_maximum_fusion, bf16[1024,256]{1,0:T(8,128)(2,1)S(1)} %copy-done.46, bf16[1024,256]{1,0:T(8,128)(2,1)S(1)} %copy-done.47, bf16[1024,256]{1,0:T(8,128)(2,1)S(1)} %copy-done.48, ...), kind=kOutput, calls=%fused_computation | convolution fusion | flops 5922619392 | bytes 19398656 | tf_op jit(solution)/shard_map/dot_general | solution.py:438
  405.1 11.9 %collective-permute-done.17 = bf16[512,1024]{1,0:T(8,128)(2,1)S(1)} collective-permute-done((bf16[512,1024]{1,0:T(8,128)(2,1)}, bf16[512,1024]{1,0:T(8,128)(2,1)S(1)}, u32[]{:S(2)}, u32[]{:S(2)}) %collective-permute-start.17) | collective-permute-done | bytes 1048608 | tf_op jit(solution)/shard_map/ppermute | solution.py:442
  426.2 11.1 %collective-permute-done.19 = bf16[256,1024]{1,0:T(8,128)(2,1)} collective-permute-done((bf16[256,1024]{1,0:T(8,128)(2,1)}, bf16[256,1024]{1,0:T(8,128)(2,1)}, u32[]{:S(2)}, u32[]{:S(2)}) %collective-permute-start.19) | collective-permute-done | bytes 524320 | tf_op jit(solution)/shard_map/ppermute | solution.py:442
  445.4 8.5 %convolution_convert_fusion.3 = bf16[1024,2048]{1,0:T(8,128)(2,1)} fusion(bf16[1024,1408]{1,0:T(8,128)(2,1)S(1)} %copy-done.39, bf16[1408,2048]{1,0:T(8,128)(2,1)S(1)} %bitcast.94), kind=kOutput, calls=%fused_computation.28 | convolution fusion | flops 5907677184 | bytes 12845056 | tf_op jit(solution)/shard_map/dot_general | solution.py:438
  453.9 13.2 %collective-permute-done.21 = bf16[256,2048]{1,0:T(8,128)(2,1)S(1)} collective-permute-done((bf16[256,2048]{1,0:T(8,128)(2,1)S(1)}, bf16[256,2048]{1,0:T(8,128)(2,1)S(1)}, u32[]{:S(2)}, u32[]{:S(2)}) %collective-permute-start.21) | collective-permute-done | bytes 1048608 | tf_op jit(solution)/shard_map/ppermute | solution.py:442
  470.0 8.3 %collective-permute-done.26 = bf16[128,2048]{1,0:T(8,128)(2,1)S(1)} collective-permute-done((bf16[128,2048]{1,0:T(8,128)(2,1)S(1)}, bf16[128,2048]{1,0:T(8,128)(2,1)S(1)}, u32[]{:S(2)}, u32[]{:S(2)}) %collective-permute-start.26) | collective-permute-done | bytes 524320 | tf_op jit(solution)/shard_map/ppermute | solution.py:442
  517.1 63.2 %core_backward.1 = (bf16[1024,2048]{1,0:T(8,128)(2,1)S(1)}, f32[1024,8]{1,0:T(8,128)S(1)}, f32[4,2048]{1,0:T(4,128)S(1)}, f32[1,8]{1,0:T(1,128)S(1)}, f32[1,256]{1,0:T(1,128)S(1)}) custom-call(f32[1024,1024]{1,0:T(8,128)} %get-tuple-element.112.dn_in, f32[1024,2048]{1,0:T(8,128)} %fusion.84.pqkv, f32[1024,8]{1,0:T(8,128)S(1)} %copy-done.5, ...), custom_call_target="tpu_custom_call" | custom-call | flops 20000000000 | bytes 50331648 | tf_op jit(solution)/shard_map/core_backward/pallas_call | solution.py:333
  618.4 17.4 %projections_back.1 = (bf16[1024,2048]{1,0:T(8,128)(2,1)S(1)}, f32[1,2048]{1,0:T(1,128)S(1)}) custom-call(bf16[1024,2048]{1,0:T(8,128)(2,1)S(1)} %copy-done.8, bf16[1024,1024]{1,0:T(8,128)(2,1)S(1)} %get-tuple-element.206.dpo, bf16[1024,8]{1,0:T(8,128)(2,1)S(1)} %convert_element_type.267.dab, bf16[2048,2048]{1,0:T(8,128)(2,1)} %all-gather.5.cloned.1.call-done.w_qkv, ...), custom_call_target="tpu_custom_call" | custom-call | flops 12884901888 | bytes 33554432 | tf_op jit(solution)/shard_map/projections_back/pallas_call | solution.py:367
  674.5 8.7 %collective-permute-done.39 = f32[4384]{0:T(1024)S(1)} collective-permute-done((f32[4384]{0:T(1024)S(1)}, f32[4384]{0:T(1024)S(1)}, u32[]{:S(2)}, u32[]{:S(2)}) %collective-permute-start.39) | collective-permute-done | bytes 17568 | tf_op jit(solution)/shard_map/ppermute | solution.py:495
  (395 shorter events, 268.8 us)
Async XLA Ops:
  7.2 96.0 %all-gather.5.cloned.1.call-start = ((), (), s32[]{:S(2)}) async-start(), calls=%async_computation.5 | async-start | bytes 9437184 | tf_op jit(solution)/shard_map/all_gather | solution.py:519
  9.6 168.6 %all-gather.7.cloned.1.call-start = ((), (), s32[]{:S(2)}) async-start(), calls=%async_computation.6 | async-start | bytes 9437184 | tf_op jit(solution)/shard_map/all_gather | solution.py:519
  13.6 273.5 %all-gather.9.cloned.1.call-start = ((), (), s32[]{:S(2)}) async-start(), calls=%async_computation.7 | async-start | bytes 12976128 | tf_op jit(solution)/shard_map/all_gather | solution.py:519
  16.6 331.7 %all-gather.11.cloned.1.call-start = ((), (), s32[]{:S(2)}) async-start(), calls=%async_computation.8 | async-start | bytes 6488064 | tf_op jit(solution)/shard_map/all_gather | solution.py:519
  18.3 26.1 %collective-permute-start.1 = (bf16[256,2048]{1,0:T(8,128)(2,1)S(1)}, bf16[256,2048]{1,0:T(8,128)(2,1)S(1)}, u32[]{:S(2)}, u32[]{:S(2)}) collective-permute-start(bf16[256,2048]{1,0:T(8,128)(2,1)S(1)} %get-tuple-element.203), channel_id=1, source_target_pairs={{0,2},{1,3},{2,0},{3,1},{4,6},{5,7},{6,4},{7,5},{8,10},{9,11},{10,... | collective-permute-start | bytes 3145736 | tf_op jit(solution)/shard_map/ppermute | solution.py:442
  21.2 25.8 %collective-permute-start = (bf16[256,2048]{1,0:T(8,128)(2,1)S(1)}, bf16[256,2048]{1,0:T(8,128)(2,1)S(1)}, u32[]{:S(2)}, u32[]{:S(2)}) collective-permute-start(bf16[256,2048]{1,0:T(8,128)(2,1)S(1)} %get-tuple-element.203), channel_id=1, source_target_pairs={{0,1},{1,0},{2,3},{3,2},{4,5},{5,4},{6,7},{7,6},{8,9},{9,8},{10,11... | collective-permute-start | bytes 3145736 | tf_op jit(solution)/shard_map/ppermute | solution.py:442
  65.6 23.5 %collective-permute-start.5 = (bf16[256,2048]{1,0:T(8,128)(2,1)S(1)}, bf16[256,2048]{1,0:T(8,128)(2,1)S(1)}, u32[]{:S(2)}, u32[]{:S(2)}) collective-permute-start(bf16[256,2048]{1,0:T(8,128)(2,1)S(1)} %copy-done.36), channel_id=1, source_target_pairs={{0,2},{1,3},{2,0},{3,1},{4,6},{5,7},{6,4},{7,5},{8,10},{9,11},{10,... | collective-permute-start | bytes 3145736 | tf_op jit(solution)/shard_map/ppermute | solution.py:442
  67.1 24.3 %collective-permute-start.4 = (bf16[256,2048]{1,0:T(8,128)(2,1)S(1)}, bf16[256,2048]{1,0:T(8,128)(2,1)S(1)}, u32[]{:S(2)}, u32[]{:S(2)}) collective-permute-start(bf16[256,2048]{1,0:T(8,128)(2,1)S(1)} %copy-done.36), channel_id=1, source_target_pairs={{0,1},{1,0},{2,3},{3,2},{4,5},{5,4},{6,7},{7,6},{8,9},{9,8},{10,11... | collective-permute-start | bytes 3145736 | tf_op jit(solution)/shard_map/ppermute | solution.py:442
  194.5 25.4 %collective-permute-start.9 = (bf16[512,1024]{1,0:T(8,128)(2,1)S(1)}, bf16[512,1024]{1,0:T(8,128)(2,1)S(1)}, u32[]{:S(2)}, u32[]{:S(2)}) collective-permute-start(bf16[512,1024]{1,0:T(8,128)(2,1)S(1)} %pad_maximum_fusion.10), channel_id=1, source_target_pairs={{0,2},{1,3},{2,0},{3,1},{4,6},{5,7},{6,4},{7,5},{8,10},{9,11},{10,... | collective-permute-start | bytes 3145736 | tf_op jit(solution)/shard_map/ppermute | solution.py:442
  196.1 25.1 %collective-permute-start.8 = (bf16[512,1024]{1,0:T(8,128)(2,1)S(1)}, bf16[512,1024]{1,0:T(8,128)(2,1)S(1)}, u32[]{:S(2)}, u32[]{:S(2)}) collective-permute-start(bf16[512,1024]{1,0:T(8,128)(2,1)S(1)} %pad_maximum_fusion.9), channel_id=1, source_target_pairs={{0,1},{1,0},{2,3},{3,2},{4,5},{5,4},{6,7},{7,6},{8,9},{9,8},{10,11... | collective-permute-start | bytes 3145736 | tf_op jit(solution)/shard_map/ppermute | solution.py:442
  226.1 283.5 %reduce-scatter.5.cloned.1.call-start = ((), (), s32[]{:S(2)}) async-start(), calls=%async_computation.9 | async-start | bytes 6488064 | tf_op jit(solution)/shard_map/reduce_scatter | solution.py:615
  240.4 23.5 %collective-permute-start.13 = (bf16[256,2048]{1,0:T(8,128)(2,1)S(1)}, bf16[256,2048]{1,0:T(8,128)(2,1)S(1)}, u32[]{:S(2)}, u32[]{:S(2)}) collective-permute-start(bf16[256,2048]{1,0:T(8,128)(2,1)S(1)} %get-tuple-element.199), channel_id=1, source_target_pairs={{0,2},{1,3},{2,0},{3,1},{4,6},{5,7},{6,4},{7,5},{8,10},{9,11},{10,... | collective-permute-start | bytes 3145736 | tf_op jit(solution)/shard_map/ppermute | solution.py:442
  241.7 23.7 %collective-permute-start.12 = (bf16[256,2048]{1,0:T(8,128)(2,1)S(1)}, bf16[256,2048]{1,0:T(8,128)(2,1)S(1)}, u32[]{:S(2)}, u32[]{:S(2)}) collective-permute-start(bf16[256,2048]{1,0:T(8,128)(2,1)S(1)} %get-tuple-element.199), channel_id=1, source_target_pairs={{0,1},{1,0},{2,3},{3,2},{4,5},{5,4},{6,7},{7,6},{8,9},{9,8},{10,11... | collective-permute-start | bytes 3145736 | tf_op jit(solution)/shard_map/ppermute | solution.py:442
  320.8 261.4 %reduce-scatter.7.cloned.1.call-start = ((), (), s32[]{:S(2)}) async-start(), calls=%async_computation.10 | async-start | bytes 7208960 | tf_op jit(solution)/shard_map/reduce_scatter | solution.py:542
  391.5 25.5 %collective-permute-start.17 = (bf16[512,1024]{1,0:T(8,128)(2,1)}, bf16[512,1024]{1,0:T(8,128)(2,1)S(1)}, u32[]{:S(2)}, u32[]{:S(2)}) collective-permute-start(bf16[512,1024]{1,0:T(8,128)(2,1)} %pad_maximum_fusion.11), channel_id=1, source_target_pairs={{0,1},{1,0},{2,3},{3,2},{4,5},{5,4},{6,7},{7,6},{8,9},{9,8},{10,11... | collective-permute-start | bytes 3145736 | tf_op jit(solution)/shard_map/ppermute | solution.py:442
  392.9 25.3 %collective-permute-start.18 = (bf16[512,1024]{1,0:T(8,128)(2,1)}, bf16[512,1024]{1,0:T(8,128)(2,1)}, u32[]{:S(2)}, u32[]{:S(2)}) collective-permute-start(bf16[512,1024]{1,0:T(8,128)(2,1)} %concatenate.132), channel_id=1, source_target_pairs={{0,2},{1,3},{2,0},{3,1},{4,6},{5,7},{6,4},{7,5},{8,10},{9,11},{10,... | collective-permute-start | bytes 3145736 | tf_op jit(solution)/shard_map/ppermute | solution.py:442
  426.2 211.8 %reduce-scatter.9.cloned.1.call-start = ((), (), s32[]{:S(2)}) async-start(), calls=%async_computation.11 | async-start | bytes 5242880 | tf_op jit(solution)/shard_map/reduce_scatter | solution.py:542
  509.6 178.6 %reduce-scatter.11.cloned.1.call-start = ((), (), s32[]{:S(2)}) async-start(), calls=%async_computation.12 | async-start | bytes 5242880 | tf_op jit(solution)/shard_map/reduce_scatter | solution.py:542
  513.5 68.7 %collective-permute-start.23 = (bf16[256,2048]{1,0:T(8,128)(2,1)}, bf16[256,2048]{1,0:T(8,128)(2,1)}, u32[]{:S(2)}, u32[]{:S(2)}) collective-permute-start(bf16[256,2048]{1,0:T(8,128)(2,1)} %get-tuple-element.230), channel_id=1, source_target_pairs={{0,1},{1,0},{2,3},{3,2},{4,5},{5,4},{6,7},{7,6},{8,9},{9,8},{10,11... | collective-permute-start | bytes 3145736 | tf_op jit(solution)/shard_map/ppermute | solution.py:442
  514.3 67.9 %collective-permute-start.24 = (bf16[256,2048]{1,0:T(8,128)(2,1)}, bf16[256,2048]{1,0:T(8,128)(2,1)}, u32[]{:S(2)}, u32[]{:S(2)}) collective-permute-start(bf16[256,2048]{1,0:T(8,128)(2,1)} %get-tuple-element.229), channel_id=1, source_target_pairs={{0,2},{1,3},{2,0},{3,1},{4,6},{5,7},{6,4},{7,5},{8,10},{9,11},{10,... | collective-permute-start | bytes 3145736 | tf_op jit(solution)/shard_map/ppermute | solution.py:442
  514.8 67.5 %collective-permute-start.25 = (bf16[256,2048]{1,0:T(8,128)(2,1)}, bf16[256,2048]{1,0:T(8,128)(2,1)}, u32[]{:S(2)}, u32[]{:S(2)}) collective-permute-start(bf16[256,2048]{1,0:T(8,128)(2,1)} %get-tuple-element.228), channel_id=1, source_target_pairs={{0,3},{1,2},{2,1},{3,0},{4,7},{5,6},{6,5},{7,4},{8,11},{9,10},{10,... | collective-permute-start | bytes 3145736 | tf_op jit(solution)/shard_map/ppermute | solution.py:442
  612.6 46.4 %all-to-all-start = ((f32[8,12,256]{2,1,0:T(8,128)}), f32[8,12,256]{2,1,0:T(8,128)S(1)}, u32[]{:S(2)}, u32[]{:S(2)}) async-start(f32[8,12,256]{2,1,0:T(8,128)} %pad_maximum_fusion.14), calls=%async_computation.4 | async-start | bytes 262144 | tf_op jit(solution)/shard_map/all_to_all | solution.py:664
  641.2 25.4 %collective-permute-start.32 = (bf16[512,1024]{1,0:T(8,128)(2,1)}, bf16[512,1024]{1,0:T(8,128)(2,1)S(1)}, u32[]{:S(2)}, u32[]{:S(2)}) collective-permute-start(bf16[512,1024]{1,0:T(8,128)(2,1)} %pad_maximum_fusion.13), channel_id=1, source_target_pairs={{0,2},{1,3},{2,0},{3,1},{4,6},{5,7},{6,4},{7,5},{8,10},{9,11},{10,... | collective-permute-start | bytes 3145736 | tf_op jit(solution)/shard_map/ppermute | solution.py:442
  642.9 25.2 %collective-permute-start.31 = (bf16[512,1024]{1,0:T(8,128)(2,1)}, bf16[512,1024]{1,0:T(8,128)(2,1)S(1)}, u32[]{:S(2)}, u32[]{:S(2)}) collective-permute-start(bf16[512,1024]{1,0:T(8,128)(2,1)} %pad_maximum_fusion.12), channel_id=1, source_target_pairs={{0,1},{1,0},{2,3},{3,2},{4,5},{5,4},{6,7},{7,6},{8,9},{9,8},{10,11... | collective-permute-start | bytes 3145736 | tf_op jit(solution)/shard_map/ppermute | solution.py:442
  (101 other events, 1161.9 us)
Sparse Core Ops, SparseCore 0:
  10.2 85.1 all-gather.4
  97.6 80.5 all-gather.6
  180.4 106.5 all-gather.8
  289.1 59.1 all-gather.10
  350.4 63.0 reduce-scatter.4
  426.3 99.5 reduce-scatter.6
  528.1 77.2 reduce-scatter.8
  607.9 80.3 reduce-scatter.10
